TPU v7x, 32 devices: a whole 2x2x4 slice. The times are simulated.
32 devices in a mesh: face: 4 (over z), dom: 8 (over y, x, core).
Axes of the slice: x: 2, y: 2, z: 4, core: 2. Of those that a mesh axis runs over, the one named last changes fastest.
Arguments:
- prognostic: float32 [2, 64, 384, 1024], P(None, None, 'face', 'dom'), may hold values from -6 to 6
- velocity: bfloat16 [2, 64, 384, 1024], P(None, None, 'face', 'dom'), may hold values from -4 to 4
- jacobian: float32 [96, 256], P('face', 'dom'), may hold values from 0.5 to 2
- element_span: int32 [96, 256], P('face', 'dom'), may hold values from 0 to 31, as said below
- sunlit: int32 [96, 256], P('face', 'dom'), may hold values from 0 to 1, as said below
- first_weight: bfloat16 [128, 512], replicated, may hold values from -0.5 to 0.5
- first_bias: float32 [512], replicated, may hold values from -3 to 3
- second_weight: bfloat16 [512, 512], replicated, may hold values from -0.25 to 0.25
- second_bias: float32 [512], replicated, may hold values from -3 to 3
- third_weight: bfloat16 [512, 512], replicated, may hold values from -0.25 to 0.25
- third_bias: float32 [512], replicated, may hold values from -3 to 3
- output_weight: bfloat16 [512, 128], replicated, may hold values from -0.25 to 0.25
- output_bias: float32 [128], replicated, may hold values from -3 to 3
- solar_inner: bfloat16 [128, 512], replicated, may hold values from -0.5 to 0.5
- solar_inner_bias: float32 [512], replicated, may hold values from -3 to 3
- solar_middle: bfloat16 [512, 512], replicated, may hold values from -0.25 to 0.25
- solar_middle_bias: float32 [512], replicated, may hold values from -3 to 3
- solar_outer: bfloat16 [512, 128], replicated, may hold values from -0.25 to 0.25
- solar_outer_bias: float32 [128], replicated, may hold values from -3 to 3
Outputs:
- new_state: float32 [2, 64, 384, 1024], P(None, None, 'face', 'dom')
- span_state: bfloat16 [98304, 128], P(('face', 'dom'))
Inputs may be any that keep to these rules, and one draw needn't show every extreme that they name: `element_span`: span c lives on device c (face index slowest). Every span receives exactly 768 elements, half of them sunlit; one device sends at most 48 elements to one span, and 48 is reached. sunlit is the same for all elements of one device, and is 1 on half of the devices.
All inputs are finite; a program needn't handle non-finite values.
Results may differ from a plain program's by a relative error of at most 0.0025.
Values may be sent and summed in bfloat16 or wider, within the bound.
No kernel may reach another device: no remote copies, remote signals or barrier semaphores. Data moves between devices by JAX's collectives and lax.ppermute only.
A program may use at most 128 MiB of HBM per device.

v0:
```python
import jax
import jax.numpy as jnp
import numpy as np
from jax import lax
from jax.experimental import pallas as pl
from jax.experimental.pallas import tpu as pltpu
from jax.sharding import PartitionSpec as P

TIME_STEP = 0.1
LEAK_SLOPE = 0.15
F32 = jnp.float32
BF16 = jnp.bfloat16
HIGHEST = lax.Precision.HIGHEST
CELL_WEIGHTS = (1.0 / 6.0, 5.0 / 6.0, 5.0 / 6.0, 1.0 / 6.0)
MIB = 1024 * 1024
EMPTY = 1e30


def derivative_matrix():
    points = np.array([-1.0, -1.0 / np.sqrt(5.0), 1.0 / np.sqrt(5.0), 1.0])
    legendre = (5.0 * points**3 - 3.0 * points) / 2.0
    derivative = np.zeros((4, 4))
    for i in range(4):
        for k in range(4):
            if i != k:
                derivative[i, k] = legendre[i] / (legendre[k] * (points[i] - points[k]))
    derivative[0, 0] = -3.0
    derivative[3, 3] = 3.0
    return derivative


D = derivative_matrix()


def y_derivative_operand(width):
    full = np.kron(np.eye(width // 4), D.T).astype(np.float32)
    high = full.astype(jnp.bfloat16)
    low = (full - high.astype(np.float32)).astype(jnp.bfloat16)
    return np.concatenate([high, high, low], axis=0)


def iota(shape, dim):
    return lax.broadcasted_iota(jnp.int32, shape, dim)


def split(values):
    high = values.astype(BF16)
    return high, (values - high.astype(F32)).astype(BF16)


def copies_along_y(values):
    width = values.shape[-1]
    lane = iota((1, width), 1)
    up = ((lane & 3) == 3) & (lane < width - 1)
    down = ((lane & 3) == 0) & (lane > 0)
    return jnp.where(
        up, pltpu.roll(values, width - 1, 1), jnp.where(down, pltpu.roll(values, 1, 1), 0.0)
    )


def along_lanes(jac, width):
    expand = (iota((jac.shape[1], width), 1) >> 2) == iota((jac.shape[1], width), 0)
    return jnp.dot(jac, expand.astype(F32), precision=HIGHEST, preferred_element_type=F32)


def inner_reciprocals(mass):
    width = mass.shape[1]
    lane = iota(mass.shape, 1)
    row = iota(mass.shape, 0)
    inner = (lane > 0) & (lane < width - 1)
    inside = jnp.where(inner, 1.0 / mass, 0.0)
    shared = jnp.where(inner & (row > 0), 1.0 / (mass + pltpu.roll(mass, 1, 0)), 0.0)
    return inside, shared


def dynamics_kernel(
    prog_ref, vel_ref, jac_ref, dcat_ref, adv_ref, xlo_ref, xhi_ref, ylo_ref, yhi_ref,
    sy3_ref, vf3_ref, pf3_ref, scale_ref, inside_ref, shared_ref, zlo_ref, zhi_ref,
):
    step = pl.program_id(0)
    _, tile, width_x, width = prog_ref.shape
    elements_x, elements_y = jac_ref.shape
    features = zlo_ref.shape[0]
    levels = features // 2
    planes = 2 * tile
    pitch = sy3_ref.shape[1]
    sy_ref = sy3_ref.reshape(planes * pitch, width)
    vf_ref = vf3_ref.reshape(planes * pitch, width)
    pf_ref = pf3_ref.reshape(planes * pitch, width)

    @pl.when(step == 0)
    def _():
        mass = along_lanes(jac_ref[...], width)
        scale_ref[...] = -TIME_STEP * jnp.sqrt(mass)
        inside, shared = inner_reciprocals(mass + copies_along_y(mass))
        inside_ref[...] = inside
        shared_ref[...] = shared

    vf3_ref[:, 0:width_x, :] = vel_ref[...].astype(F32).reshape(planes, width_x, width)
    piece = planes // 4
    for at in range(4):
        first = at * piece
        values = prog_ref[first // tile, first % tile : first % tile + piece]
        pf3_ref[first : first + piece, 0:width_x, :] = values
        high, low = split(values.reshape(piece * width_x, width))
        sy3_ref[first : first + piece, 0:width_x, :] = jnp.dot(
            jnp.concatenate([high, low, high], axis=1), dcat_ref[...], preferred_element_type=F32
        ).reshape(piece, width_x, width)

    lane = iota((tile, width), 1)
    p0, p1 = (D[0, 0] - D[0, 3]) / 2, (D[0, 1] - D[0, 2]) / 2
    q0 = (D[0, 1] + D[0, 2]) / 2
    r0, r1 = (D[1, 0] - D[1, 3]) / 2, -D[1, 2] / 2
    t0 = D[1, 2] / 2

    def rims(lines):
        first, second, third = lines
        a = pltpu.roll(first, 1, 1)
        b = pltpu.roll(second, 2, 1)
        c = pltpu.roll(third, 3, 1)

        def pick(base):
            return jnp.where(
                lane == base, first,
                jnp.where(
                    lane == (base + 1) % width, a,
                    jnp.where(
                        lane == (base + 2) % width, b, jnp.where(lane == (base + 3) % width, c, 0.0)
                    ),
                ),
            )

        return pick(0), pick(width - 1)

    def element(p, carry):
        scale = scale_ref[p : p + 1, :]
        inside = inside_ref[p : p + 1, :]
        shared = shared_ref[p : p + 1, :]
        shift = (4 * p + width - 1) % width
        vx = [vf_ref[pl.ds(4 * p + k, tile, stride=pitch), :] for k in range(4)]
        vy = [
            vf_ref[pl.ds(tile * pitch + 4 * p + k, tile, stride=pitch), :] for k in range(4)
        ]
        out = []
        for v in range(2):
            last_e, last_f, z_low, z_high = carry[4 * v : 4 * v + 4]
            base = v * tile * pitch + 4 * p
            f = [pf_ref[pl.ds(base + k, tile, stride=pitch), :] for k in range(4)]
            sy = [sy_ref[pl.ds(base + k, tile, stride=pitch), :] for k in range(4)]
            outer_gap, inner_gap = f[0] - f[3], f[1] - f[2]
            bend = (f[1] + f[2]) - (f[0] + f[3])
            odd = p0 * outer_gap + p1 * inner_gap
            even = q0 * bend
            odd_in = r0 * outer_gap + r1 * inner_gap
            even_in = t0 * bend
            sx = [odd + even, odd_in + even_in, odd_in - even_in, odd - even]
            e = []
            for k in range(4):
                moved = (vx[k] * sx[k] + vy[k] * sy[k]) * scale
                e.append(moved + copies_along_y(moved))
            joined = last_e + e[0]
            gain = joined * shared
            adv_ref[4 * p, v] = f[0] + gain
            adv_ref[4 * p + 1, v] = f[1] + e[1] * inside
            adv_ref[4 * p + 2, v] = f[2] + e[2] * inside

            if p == 0:
                xlo_ref[pl.ds(pl.multiple_of(v * levels + tile * step, tile), tile), :] = joined
            else:
                adv_ref[4 * p - 1, v] = last_f + gain

            low, high = rims((joined, e[1], e[2]))
            out += [
                e[3], f[3],
                z_low + pltpu.roll(low, shift, 1), z_high + pltpu.roll(high, shift, 1),
            ]
        return tuple(out)

    zero = jnp.zeros((tile, width), F32)
    final = (zero,) * 8
    for p in range(elements_x):
        final = element(p, final)
    for v in range(2):
        last_e, last_f, z_low, z_high = final[4 * v : 4 * v + 4]
        at = pl.ds(pl.multiple_of(v * levels + tile * step, tile), tile)
        adv_ref[width_x - 1, v] = last_f
        xhi_ref[at, :] = last_e
        zlo_ref[at, :] = jnp.where(
            lane == width_x - 1, pltpu.roll(last_e, width_x - 1, 1), z_low
        )
        zhi_ref[at, :] = pltpu.roll(
            jnp.where(lane == width_x - 2, pltpu.roll(last_e, width_x - 1, 1), z_high), 1, 1
        )

    @pl.when(step == pl.num_programs(0) - 1)
    def _():
        jac = jac_ref[...]
        mass = along_lanes(jac, width)
        mass = mass + copies_along_y(mass)
        ylo_ref[...] = zlo_ref[...].T
        yhi_ref[...] = zhi_ref[...].T
        for ref, q in ((ylo_ref, 0), (yhi_ref, elements_y - 1)):
            ref[width_x : width_x + elements_x, :] = jnp.broadcast_to(
                jac[:, q : q + 1], (elements_x, features)
            )
        for ref, x, p in ((xlo_ref, 0, 0), (xhi_ref, width_x - 1, elements_x - 1)):
            ref[features : features + 8, :] = jnp.concatenate(
                [
                    ylo_ref[x : x + 1, :],
                    yhi_ref[x : x + 1, :],
                    mass[p : p + 1, :],
                    ylo_ref[width_x + p : width_x + p + 1, :],
                    yhi_ref[width_x + p : width_x + p + 1, :],
                    jnp.zeros((3, width), F32),
                ],
                axis=0,
            )


def cells_kernel(capacity, devices, adv_ref, span_ref, col_ref, slot_ref):
    group = adv_ref.shape[0] // 4
    width = adv_ref.shape[3]
    features = adv_ref.shape[1] * adv_ref.shape[2]
    elements_x, elements_y = span_ref.shape
    elements = elements_x * elements_y

    @pl.when(pl.program_id(0) == 0)
    def _():
        lane = iota((elements_y, elements), 1)
        tiled = lax.rem(lane, elements_y) == iota((elements_y, elements), 0)
        spread = jnp.dot(
            span_ref[...].astype(F32).astype(BF16), tiled.astype(BF16), preferred_element_type=F32
        )
        start = iota((elements_x, elements), 0) * elements_y
        at = iota((elements_x, elements), 1)
        own = (at >= start) & (at < start + elements_y)
        target = jnp.sum(jnp.where(own, spread, 0.0), axis=0, keepdims=True)
        chosen = jnp.where(
            target == iota((devices, elements), 0).astype(F32), 1.0, 0.0
        )
        before = iota((elements, elements), 0) < iota((elements, elements), 1)
        earlier = jnp.dot(
            chosen.astype(BF16), before.astype(BF16), preferred_element_type=F32
        )
        rank = jnp.sum(chosen * earlier, axis=0, keepdims=True)
        slot_ref[...] = (target * capacity + rank).astype(jnp.int32)

    select = select_cells(elements_y, width)
    for p in range(group):
        for a in range(2):
            line = adv_ref[4 * p + 2 * a] * CELL_WEIGHTS[2 * a]
            line += adv_ref[4 * p + 2 * a + 1] * CELL_WEIGHTS[2 * a + 1]
            low, high = cells_of_line(line.reshape(features, width), select)
            at = slice(p * elements_y, (p + 1) * elements_y)
            col_ref[2 * a, at, :] = low
            col_ref[2 * a + 1, at, :] = high


def select_cells(elements_y, width):
    shape = (2 * elements_y, width)
    row, lane = iota(shape, 0), iota(shape, 1)
    wanted = jnp.where(row < elements_y, 4 * row, 4 * (row - elements_y) + 2)
    return (lane == wanted).astype(BF16)


def cells_of_line(line, select):
    features, width = line.shape
    inner = (iota((1, width), 1) & 3)
    line = line * jnp.where((inner == 0) | (inner == 3), 1.0 / 6.0, 5.0 / 6.0)
    line = line + pltpu.roll(line, width - 1, 1)
    high, low = split(line)
    both = lax.dot_general(
        select, jnp.concatenate([high, low], axis=0), (((1,), (1,)), ((), ())),
        preferred_element_type=F32,
    )
    cells = both[:, :features] + both[:, features:]
    half = select.shape[0] // 2
    return cells[:half], cells[half:]


def corners_kernel(width_x, elements_x, ylo_ref, yhi_ref, prev_ref, next_ref, ylo_out, yhi_out):
    features = prev_ref.shape[0] - 8
    spare = width_x + elements_x
    for side, (ref, out) in enumerate(((ylo_ref, ylo_out), (yhi_ref, yhi_out))):
        row = iota(ref.shape, 0)
        values = ref[...]
        prev = prev_ref[features + side : features + side + 1, :]
        later = next_ref[features + side : features + side + 1, :]
        prev_mass = prev_ref[features + 3 + side : features + 4 + side, :]
        later_mass = next_ref[features + 3 + side : features + 4 + side, :]
        values = values + jnp.where(row == 0, prev, 0.0)
        values = values + jnp.where(row == width_x - 1, later, 0.0)
        values = jnp.where(row == spare, prev_mass, values)
        out[...] = jnp.where(row == spare + 1, later_mass, values)


def send_kernel(
    width_x, elements_x,
    col_ref, slot_ref, xlo_ref, xhi_ref, prev_ref, next_ref, ylo_ref, yhi_ref, yprev_ref,
    ynext_ref, colbf_ref, out_ref, fy_ref, ry_ref, fx_ref, rx_ref, work_ref,
):
    _, elements, features = col_ref.shape
    elements_y = elements // elements_x
    width = xlo_ref.shape[1]
    work_ref[...] = col_ref[...]
    select = select_cells(elements_y, width)
    lane = iota((1, width), 1)
    inner = (lane > 0) & (lane < width - 1)
    for side, (own, other) in enumerate(((ylo_ref, yprev_ref), (yhi_ref, ynext_ref))):
        total = own[...] + other[...]
        mass = total[width_x : width_x + elements_x]
        row = iota(mass.shape, 0)
        spare = width_x + elements_x
        before = jnp.where(row == 0, total[spare : spare + 1], pltpu.roll(mass, 1, 0))
        after = jnp.where(
            row == elements_x - 1, total[spare + 1 : spare + 2], pltpu.roll(mass, elements_x - 1, 0)
        )
        inside = 1.0 / mass
        ry_ref[side, pl.ds(0, elements_x, stride=4), :] = 1.0 / (mass + before)
        ry_ref[side, pl.ds(1, elements_x, stride=4), :] = inside
        ry_ref[side, pl.ds(2, elements_x, stride=4), :] = inside
        ry_ref[side, pl.ds(3, elements_x, stride=4), :] = 1.0 / (mass + after)
        fy_ref[side] = total[:width_x] * ry_ref[side]
        fixes = [fy_ref[side, pl.ds(k, elements_x, stride=4), :] for k in range(4)]
        at = pl.ds(side * (elements_y - 1), elements_x, stride=elements_y)
        for a in range(2):
            added = CELL_WEIGHTS[2 * a] * fixes[2 * a] + CELL_WEIGHTS[2 * a + 1] * fixes[2 * a + 1]
            k = 2 * a + side
            work_ref[k, at, :] = work_ref[k, at, :] + CELL_WEIGHTS[0] * added
    for side, (own, other) in enumerate(((xlo_ref, prev_ref), (xhi_ref, next_ref))):
        mass = own[features + 2 : features + 3, :] + other[features + 2 : features + 3, :]
        reciprocal = jnp.where(inner, 1.0 / mass, 0.0)
        rx_ref[side] = jnp.broadcast_to(reciprocal, (8, width))
        fix = (own[:features] + other[:features]) * reciprocal
        fx_ref[side] = fix
        low, high = cells_of_line(CELL_WEIGHTS[0] * fix, select)
        at = slice(side * (elements_x - 1) * elements_y, (side * (elements_x - 1) + 1) * elements_y)
        work_ref[2 * side, at, :] = work_ref[2 * side, at, :] + low
        work_ref[2 * side + 1, at, :] = work_ref[2 * side + 1, at, :] + high
    for k in range(4):
        colbf_ref[:, k * features : (k + 1) * features] = work_ref[k].astype(BF16)
    slots = out_ref.shape[0]
    piece = slots // 4
    for part in range(4):
        chosen = (iota((piece, elements), 0) + part * piece) == slot_ref[...]
        chosen = jnp.where(chosen, 1.0, 0.0)
        filled = jnp.max(chosen, axis=1, keepdims=True)
        moved = jnp.dot(chosen.astype(BF16), colbf_ref[...], preferred_element_type=F32)
        out_ref[pl.ds(part * piece, piece), :] = jnp.where(filled > 0.0, moved, EMPTY).astype(BF16)


def dense(inputs, weight_ref, bias_ref):
    return jnp.dot(inputs, weight_ref[...], preferred_element_type=F32) + bias_ref[...]


def leaky(values):
    return jnp.maximum(values, LEAK_SLOPE * values).astype(BF16)


def network_kernel(
    lit_ref, col_ref, w1, b1, w2, b2, w3, b3, w4, b4, s1, c1, s2, c2, s3, c3, inc_ref, total_ref
):
    rows = col_ref.shape[0]
    features = col_ref.shape[1] // 4
    inputs = jnp.concatenate(
        [col_ref[:, k * features : (k + 1) * features] for k in range(4)], axis=0
    )
    hidden = leaky(dense(inputs, w1, b1))
    hidden = leaky(dense(hidden, w2, b2))
    hidden = leaky(dense(hidden, w3, b3))
    total_ref[...] = dense(hidden, w4, b4)

    @pl.when(lit_ref[0, 0] != 0)
    def _():
        solar = leaky(dense(inputs, s1, c1))
        solar = leaky(dense(solar, s2, c2))
        total_ref[...] += lit_ref[0, 0].astype(F32) * dense(solar, s3, c3)

    for k in range(4):
        inc_ref[:, k * features : (k + 1) * features] = total_ref[
            k * rows : (k + 1) * rows, :
        ].astype(BF16)


def spread_operand(mass_line, elements_y):
    width = mass_line.shape[1]
    shape = (2 * elements_y, width)
    row, lane = iota(shape, 0), iota(shape, 1)
    upper = row >= elements_y
    q = jnp.where(upper, row - elements_y, row)
    b = jnp.where(upper, 1, 0)
    own = (lane >> 1) == 2 * q + b
    copy = lane == jnp.where(upper, 4 * q + 4, 4 * q - 1)
    weights = jnp.where(
        own, mass_line, jnp.where(copy, copies_along_y(mass_line), 0.0)
    )
    high, low = split(weights)
    return jnp.concatenate([high, low], axis=0)


def spread_line(inc_ref, p, a, operand, elements_y):
    features = inc_ref.shape[1] // 4
    at = pl.ds(pl.multiple_of(p * elements_y, elements_y), elements_y)
    cells = [
        inc_ref[at, (2 * a + b) * features : (2 * a + b + 1) * features] for b in range(2)
    ]
    return lax.dot_general(
        jnp.concatenate(cells + cells, axis=0), operand, (((0,), (0,)), ((), ())),
        preferred_element_type=F32,
    )


def rims_kernel(inc_ref, jac_ref, xlo_ref, xhi_ref, ylo_ref, yhi_ref, wide_ref):
    elements_x, elements_y = jac_ref.shape
    features = inc_ref.shape[1] // 4
    width = xlo_ref.shape[1]
    width_x = 4 * elements_x
    for k in range(4):
        wide_ref[k] = inc_ref[:, k * features : (k + 1) * features].astype(F32)
    mass = along_lanes(jac_ref[...], width)
    for side, ref in enumerate((ylo_ref, yhi_ref)):
        q = side * (elements_y - 1)
        column = jac_ref[:, q : q + 1]
        at = pl.ds(q, elements_x, stride=elements_y)
        first = column * wide_ref[side, at, :]
        second = column * wide_ref[2 + side, at, :]
        row = iota(first.shape, 0)
        ref[pl.ds(0, elements_x, stride=4), :] = first + jnp.where(
            row == 0, 0.0, pltpu.roll(second, 1, 0)
        )
        ref[pl.ds(1, elements_x, stride=4), :] = first
        ref[pl.ds(2, elements_x, stride=4), :] = second
        ref[pl.ds(3, elements_x, stride=4), :] = second + jnp.where(
            row == elements_x - 1, 0.0, pltpu.roll(first, elements_x - 1, 0)
        )
        ref[width_x:, :] = jnp.zeros((ref.shape[0] - width_x, features), F32)
    for side, ref in enumerate((xlo_ref, xhi_ref)):
        p = side * (elements_x - 1)
        x = side * (width_x - 1)
        operand = spread_operand(mass[p : p + 1], elements_y)
        ref[0:features, :] = spread_line(inc_ref, p, side, operand, elements_y)
        ref[features : features + 8, :] = jnp.concatenate(
            [ylo_ref[x : x + 1, :], yhi_ref[x : x + 1, :], jnp.zeros((6, width), F32)], axis=0
        )


def final_kernel(
    adv_ref, inc_ref, jac_ref, xlo_ref, xhi_ref, prev_ref, next_ref, ylo_ref, yhi_ref, yprev_ref,
    ynext_ref, fy_ref, ry_ref, fx_ref, rx_ref, out_ref, mass_ref, inside_ref, shared_ref,
    rim_ref, edge_ref,
):
    step = pl.program_id(0)
    elements_x, elements_y = jac_ref.shape
    width_x = 4 * elements_x
    lines = adv_ref.shape[0]
    group = lines // 4
    width = adv_ref.shape[3]
    features = adv_ref.shape[1] * adv_ref.shape[2]

    @pl.when(step == 0)
    def _():
        mass = along_lanes(jac_ref[...], width)
        mass_ref[...] = mass
        inside, shared = inner_reciprocals(mass + copies_along_y(mass))
        inside_ref[...] = inside
        shared_ref[0:elements_x, :] = shared
        shared_ref[elements_x:, :] = jnp.zeros((8, width), F32)
        for side, (own, other) in enumerate(((ylo_ref, yprev_ref), (yhi_ref, ynext_ref))):
            rim_ref[side] = fy_ref[side] + (own[0:width_x, :] + other[0:width_x, :]) * ry_ref[side]
        for side, (own, other) in enumerate(((xlo_ref, prev_ref), (xhi_ref, next_ref))):
            edge_ref[side] = (
                fx_ref[side] + (own[0:features, :] + other[0:features, :]) * rx_ref[side, 0:1, :]
            )

    out = out_ref.reshape(features * lines, width)
    row = iota((16, width), 0)
    lane = iota((16, width), 1)
    place = (((row < 2) & (lane == 0)) | ((row >= 2) & (row < 4) & (lane == width - 1))).astype(BF16)

    def rim_of(x):
        low = rim_ref[0, pl.ds(x, 1), :]
        high = rim_ref[1, pl.ds(x, 1), :]
        parts = jnp.where(row < 2, low, high)
        rough = parts.astype(BF16).astype(F32)
        rest = parts - rough
        stacked = jnp.where((row == 0) | (row == 2), rough, jnp.where(row < 4, rest, 0.0))
        return lax.dot_general(
            stacked.astype(BF16), place, (((0,), (0,)), ((), ())), preferred_element_type=F32
        )

    def line_of(p, a):
        operand = spread_operand(mass_ref[pl.ds(p, 1), :], elements_y)
        return spread_line(inc_ref, p, a, operand, elements_y)

    def store(at, values):
        out[pl.ds(at, features, stride=lines), :] = adv_ref[at].reshape(features, width) + values

    first = step * group
    before = line_of(jnp.maximum(first - 1, 0), 1)
    here = line_of(first, 0)
    joint = (before + here) * shared_ref[pl.ds(first, 1), :] + rim_of(4 * first)
    for k in range(group):
        p = first + k
        inside = inside_ref[pl.ds(p, 1), :]
        store(4 * k, joint)
        store(4 * k + 1, here * inside + rim_of(4 * p + 1))
        there = line_of(p, 1)
        store(4 * k + 2, there * inside + rim_of(4 * p + 2))
        here = line_of(jnp.minimum(p + 1, elements_x - 1), 0)
        joint = (there + here) * shared_ref[pl.ds(p + 1, 1), :] + rim_of(4 * p + 3)
        store(4 * k + 3, joint)

    @pl.when(step == 0)
    def _():
        at = pl.ds(0, features, stride=lines)
        out[at, :] = out[at, :] + edge_ref[0]

    @pl.when(step == pl.num_programs(0) - 1)
    def _():
        at = pl.ds(lines - 1, features, stride=lines)
        out[at, :] = out[at, :] + edge_ref[1]


def arrange_kernel(capacity, data_ref, out_ref, wide_ref, rows_ref, vector_ref, start_ref, sem):
    devices = vector_ref.shape[0]
    slots = data_ref.shape[0]
    features = data_ref.shape[1] // 4
    elements = out_ref.shape[0] // 4
    filled = jnp.where(data_ref[:, 0:features].astype(F32) < 0.5 * EMPTY, 1.0, 0.0).astype(BF16)
    before = iota((devices, slots), 1) < iota((devices, slots), 0) * capacity
    starts = jnp.dot(
        jnp.where(before, 1.0, 0.0).astype(BF16), filled, preferred_element_type=F32
    )
    vector_ref[...] = jnp.clip(starts, 0.0, float(elements)).astype(jnp.int32)
    copy = pltpu.make_async_copy(vector_ref, start_ref, sem)
    copy.start()
    for k in range(4):
        wide_ref[k] = data_ref[:, k * features : (k + 1) * features].astype(F32)
    copy.wait()

    def one(s, carry):
        start = start_ref[s, 0]
        for k in range(4):
            rows_ref[pl.ds(4 * start + k, capacity, stride=4), :] = wide_ref[
                k, pl.ds(s * capacity, capacity), :
            ]
        return carry

    lax.fori_loop(0, devices, one, 0)
    out_ref[...] = rows_ref[0 : out_ref.shape[0], :].astype(BF16)


def params(mib):
    return pltpu.CompilerParams(vmem_limit_bytes=mib * MIB)


def whole(shape):
    return pl.BlockSpec(shape, lambda *_: (0,) * len(shape))


def cost(flops, bytes_accessed):
    return pl.CostEstimate(flops=flops, bytes_accessed=bytes_accessed, transcendentals=0)


def shape_of(shape, dtype=F32):
    return jax.ShapeDtypeStruct(shape, dtype)


def shifted(axis, by):
    count = lax.axis_size(axis)
    return [(i, (i + by) % count) for i in range(count)]


def dynamics_call(prognostic, velocity, jacobian):
    fields, levels, width_x, width = prognostic.shape
    elements_x, elements_y = jacobian.shape
    features = fields * levels
    tile = 8
    packet = features + 8
    dcat = jnp.asarray(y_derivative_operand(width))
    return pl.pallas_call(
        dynamics_kernel,
        grid=(levels // tile,),
        in_specs=[
            pl.BlockSpec((2, tile, width_x, width), lambda t: (0, t, 0, 0)),
            pl.BlockSpec((2, tile, width_x, width), lambda t: (0, t, 0, 0)),
            whole((elements_x, elements_y)),
            whole((3 * width, width)),
        ],
        out_specs=[
            pl.BlockSpec((width_x, 2, tile, width), lambda t: (0, 0, t, 0)),
            whole((packet, width)),
            whole((packet, width)),
            whole((width, features)),
            whole((width, features)),
        ],
        out_shape=[
            shape_of((width_x, fields, levels, width)),
            shape_of((packet, width)),
            shape_of((packet, width)),
            shape_of((width, features)),
            shape_of((width, features)),
        ],
        scratch_shapes=[
            pltpu.VMEM((2 * tile, width_x + 8, width), F32),
            pltpu.VMEM((2 * tile, width_x + 8, width), F32),
            pltpu.VMEM((2 * tile, width_x + 8, width), F32),
            pltpu.VMEM((elements_x, width), F32),
            pltpu.VMEM((elements_x, width), F32),
            pltpu.VMEM((elements_x, width), F32),
            pltpu.VMEM((features, width), F32),
            pltpu.VMEM((features, width), F32),
        ],
        compiler_params=params(58),
        cost_estimate=cost(2_000_000_000, 16_000_000),
        name="dynamics",
    )(prognostic, velocity, jacobian, dcat)


def on_device(
    prognostic,
    velocity,
    jacobian,
    element_span,
    sunlit,
    *weights,
):
    fields, levels, width_x, width = prognostic.shape
    elements_x, elements_y = jacobian.shape
    features = fields * levels
    elements = elements_x * elements_y
    devices = lax.axis_size("face") * lax.axis_size("dom")
    capacity = max(2, 2 * elements // devices)
    slots = devices * capacity
    packet = features + 8
    vmem = pl.BlockSpec(memory_space=pltpu.VMEM)
    smem = pl.BlockSpec(memory_space=pltpu.SMEM)

    adv, xlo, xhi, ylo, yhi = dynamics_call(prognostic, velocity, jacobian)

    group = 4
    col, slot_ids = pl.pallas_call(
        lambda *refs: cells_kernel(capacity, devices, *refs),
        grid=(elements_x // group,),
        in_specs=[
            pl.BlockSpec((4 * group, fields, levels, width), lambda g: (g, 0, 0, 0)),
            whole((elements_x, elements_y)),
        ],
        out_specs=[
            pl.BlockSpec((4, group * elements_y, features), lambda g: (0, g, 0)),
            whole((1, elements)),
        ],
        out_shape=[
            shape_of((4, elements, features)),
            shape_of((1, elements), jnp.int32),
        ],
        compiler_params=params(58),
        cost_estimate=cost(1_000_000_000, 8_000_000),
        name="cells",
    )(adv, element_span)

    def exchange(xlo, xhi, ylo, yhi):
        prev = lax.ppermute(xhi, "face", shifted("face", 1))
        later = lax.ppermute(xlo, "face", shifted("face", -1))
        ylo, yhi = pl.pallas_call(
            lambda *refs: corners_kernel(width_x, elements_x, *refs),
            in_specs=[vmem] * 4,
            out_specs=[vmem] * 2,
            out_shape=[shape_of((width, features))] * 2,
            compiler_params=params(16),
            name="corners",
        )(ylo, yhi, prev, later)
        yprev = lax.ppermute(yhi, "dom", shifted("dom", 1))
        ynext = lax.ppermute(ylo, "dom", shifted("dom", -1))
        return prev, later, ylo, yhi, yprev, ynext

    prev, later, ylo, yhi, yprev, ynext = exchange(xlo, xhi, ylo, yhi)

    colbf, outgoing, fy, ry, fx, rx = pl.pallas_call(
        lambda *refs: send_kernel(width_x, elements_x, *refs),
        in_specs=[vmem] * 10,
        out_specs=[vmem] * 6,
        out_shape=[
            shape_of((elements, 4 * features), BF16),
            shape_of((slots, 4 * features), BF16),
            shape_of((2, width_x, features)),
            shape_of((2, width_x, features)),
            shape_of((2, features, width)),
            shape_of((2, 8, width)),
        ],
        scratch_shapes=[pltpu.VMEM((4, elements, features), F32)],
        compiler_params=params(24),
        cost_estimate=cost(2_000_000_000, 5_000_000),
        name="send",
    )(col, slot_ids, xlo, xhi, prev, later, ylo, yhi, yprev, ynext)

    arrived = lax.all_to_all(
        outgoing.reshape(devices, capacity, 4 * features), ("face", "dom"),
        split_axis=0, concat_axis=0, tiled=True,
    ).reshape(slots, 4 * features)

    chunk = elements // 3
    hidden = weights[0].shape[1]
    operands, operand_specs = [], []
    for item in weights:
        item = item if item.ndim == 2 else item.reshape(1, -1)
        operands.append(item)
        operand_specs.append(whole(item.shape))
    inc = pl.pallas_call(
        network_kernel,
        grid=(3,),
        in_specs=[smem, pl.BlockSpec((chunk, 4 * features), lambda g: (g, 0))] + operand_specs,
        out_specs=pl.BlockSpec((chunk, 4 * features), lambda g: (g, 0)),
        out_shape=shape_of((elements, 4 * features), BF16),
        scratch_shapes=[pltpu.VMEM((4 * chunk, features), F32)],
        compiler_params=params(58),
        cost_estimate=cost(8 * elements * (4 * features * hidden + 3 * hidden * hidden), 4_000_000),
        name="network",
    )(sunlit, colbf, *operands)

    xlo2, xhi2, ylo2, yhi2 = pl.pallas_call(
        rims_kernel,
        in_specs=[vmem] * 2,
        out_specs=[vmem] * 4,
        out_shape=[
            shape_of((packet, width)),
            shape_of((packet, width)),
            shape_of((width, features)),
            shape_of((width, features)),
        ],
        scratch_shapes=[pltpu.VMEM((4, elements, features), F32)],
        compiler_params=params(16),
        cost_estimate=cost(10_000_000, 2_000_000),
        name="rims",
    )(inc, jacobian)

    prev2, later2, ylo2, yhi2, yprev2, ynext2 = exchange(xlo2, xhi2, ylo2, yhi2)

    new_state = pl.pallas_call(
        final_kernel,
        grid=(elements_x // group,),
        in_specs=[
            pl.BlockSpec((4 * group, fields, levels, width), lambda g: (g, 0, 0, 0)),
            whole((elements, 4 * features)),
            whole((elements_x, elements_y)),
            whole((packet, width)),
            whole((packet, width)),
            whole((packet, width)),
            whole((packet, width)),
            whole((width, features)),
            whole((width, features)),
            whole((width, features)),
            whole((width, features)),
            whole((2, width_x, features)),
            whole((2, width_x, features)),
            whole((2, features, width)),
            whole((2, 8, width)),
        ],
        out_specs=pl.BlockSpec((fields, levels, 4 * group, width), lambda g: (0, 0, g, 0)),
        out_shape=shape_of((fields, levels, width_x, width)),
        scratch_shapes=[
            pltpu.VMEM((elements_x, width), F32),
            pltpu.VMEM((elements_x, width), F32),
            pltpu.VMEM((elements_x + 8, width), F32),
            pltpu.VMEM((2, width_x, features), F32),
            pltpu.VMEM((2, features, width), F32),
        ],
        compiler_params=params(58),
        cost_estimate=cost(1_000_000_000, 14_000_000),
        name="final",
    )(
        adv, inc, jacobian, xlo2, xhi2, prev2, later2, ylo2, yhi2, yprev2, ynext2, fy, ry, fx, rx
    )

    span_state = pl.pallas_call(
        lambda *refs: arrange_kernel(capacity, *refs),
        in_specs=[vmem],
        out_specs=vmem,
        out_shape=shape_of((4 * elements, features), BF16),
        scratch_shapes=[
            pltpu.VMEM((4, slots, features), F32),
            pltpu.VMEM((4 * (elements + capacity), features), F32),
            pltpu.VMEM((devices, features), jnp.int32),
            pltpu.SMEM((devices, features), jnp.int32),
            pltpu.SemaphoreType.DMA,
        ],
        compiler_params=params(24),
        cost_estimate=cost(1_000_000, 3_000_000),
        name="arrange",
    )(arrived)
    return (new_state, span_state)


def solution(mesh):
    return jax.shard_map(
        on_device,
        mesh=mesh,
        in_specs=(
            P(None, None, "face", "dom"),
            P(None, None, "face", "dom"),
            P("face", "dom"),
            P("face", "dom"),
            P("face", "dom"),
        )
        + (P(),) * 14,
        out_specs=(P(None, None, "face", "dom"), P(("face", "dom"), None)),
        check_vma=False,
    )
```

profile of v0, /device:TPU:8, one launch (start us, length us, event | category | flops | bytes accessed | tf_op | source)
XLA Modules:
  0.0 103.9 jit_solution(12113433218622604804)
XLA Ops:
  0.6 14.2 %dynamics.1 = (f32[96,2,64,128]{3,2,1,0:T(8,128)}, f32[136,128]{1,0:T(8,128)}, f32[136,128]{1,0:T(8,128)}, f32[128,128]{1,0:T(8,128)}, f32[128,128]{1,0:T(8,128)}) custom-call(f32[2,64,96,128]{3,2,1,0:T(8,128)} %prog_ref.1, bf16[2,64,96,128]{3,2,1,0:T(8,128)(2,1)} %vel_ref.1, f32[24,32]{1,0:T(8,128)} %jac_ref.5, bf16[384,128]{1,0:T(8,128)(2,1)} %constant.2.clone.dcat_ref), custom_call_target="tpu_custom_call" | custom-call | flops 2000000000 | bytes 16000000 | tf_op jit(solution)/shard_map/dynamics/pallas_call | solution.py:581
  14.9 0.0 collective-permute-start.1
  14.9 2.0 %collective-permute-start = (f32[136,128]{1,0:T(8,128)}, f32[136,128]{1,0:T(8,128)S(1)}, u32[]{:S(2)}, u32[]{:S(2)}) collective-permute-start(f32[136,128]{1,0:T(8,128)} %get-tuple-element.27.refs_3_), channel_id=1, source_target_pairs={{0,8},{8,16},{16,24},{24,0},{1,9},{9,17},{17,25},{25,1},{2,10},{10... | collective-permute-start | bytes 208904 | tf_op jit(solution)/shard_map/ppermute | solution.py:663
  16.9 2.5 %collective-permute-done.1.refs_3_.refs_5_ = f32[136,128]{1,0:T(8,128)S(1)} collective-permute-done((f32[136,128]{1,0:T(8,128)}, f32[136,128]{1,0:T(8,128)S(1)}, u32[]{:S(2)}, u32[]{:S(2)}) %collective-permute-start.1) | collective-permute-done | bytes 69664 | tf_op jit(solution)/shard_map/ppermute | solution.py:664
  19.4 3.1 %collective-permute-done.refs_2_.refs_4_ = f32[136,128]{1,0:T(8,128)S(1)} collective-permute-done((f32[136,128]{1,0:T(8,128)}, f32[136,128]{1,0:T(8,128)S(1)}, u32[]{:S(2)}, u32[]{:S(2)}) %collective-permute-start) | collective-permute-done | bytes 69664 | tf_op jit(solution)/shard_map/ppermute | solution.py:663
  22.5 0.8 copy-done.11
  23.4 0.8 copy-done.12
  24.2 0.8 collective-permute-start.3
  25.0 7.0 %cells.1 = (f32[4,768,128]{2,1,0:T(8,128)}, s32[1,768]{1,0:T(1,128)}) custom-call(f32[96,2,64,128]{3,2,1,0:T(8,128)} %get-tuple-element.23.refs_0_.adv_ref, s32[24,32]{1,0:T(8,128)} %refs_1_.1), custom_call_target="tpu_custom_call" | custom-call | flops 1000000000 | bytes 8000000 | tf_op jit(solution)/shard_map/cells/pallas_call | solution.py:642
  32.0 0.0 copy-start.14
  32.0 1.4 %copy-done.14 = f32[4,768,128]{2,1,0:T(8,128)S(1)} copy-done((f32[4,768,128]{2,1,0:T(8,128)S(1)}, f32[4,768,128]{2,1,0:T(8,128)}, u32[]{:S(2)}) %copy-start.14) | copy-done | bytes 1572888
  33.4 0.7 copy-done.17
  34.1 3.1 %send.1 = (bf16[768,512]{1,0:T(8,128)(2,1)S(1)}, bf16[1536,512]{1,0:T(8,128)(2,1)}, f32[2,96,128]{2,1,0:T(8,128)S(1)}, f32[2,96,128]{2,1,0:T(8,128)S(1)}, f32[2,...) custom-call(f32[4,768,128]{2,1,0:T(8,128)S(1)} %copy-done.14, s32[1,768]{1,0:T(1,128)S(1)} %copy-done.17, ...), custom_call_target="tpu_custom_call" | custom-call | flops 2000000000 | bytes 5000000 | tf_op jit(solution)/shard_map/send/pallas_call | solution.py:679
  37.2 0.7 copy-done.3
  37.9 0.6 copy-done.5
  38.5 0.6 copy-done.6
  39.2 0.6 copy-done.13
  39.8 0.9 copy-done.18
  40.6 5.2 %all-to-all-start = ((bf16[32,48,512]{2,1,0:T(8,128)(2,1)}), bf16[32,48,512]{2,1,0:T(8,128)(2,1)S(1)}, u32[]{:S(2)}, u32[]{:S(2)}) async-start(bf16[32,48,512]{2,1,0:T(8,128)(2,1)} %bitcast.7), calls=%async_computation | async-start | bytes 3145728 | tf_op jit(solution)/shard_map/all_to_all | solution.py:697
  45.8 0.0 copy-start.4
  45.8 12.6 %network.1.inc_ref = bf16[768,512]{1,0:T(8,128)(2,1)} custom-call(s32[24,32]{1,0:T(8,128)} %lit_ref.1, bf16[768,512]{1,0:T(8,128)(2,1)} %copy-done.18, bf16[128,512]{1,0:T(8,128)(2,1)} %w1.1, f32[1,512]{1,0:T(1,128)} %bitcast.10, bf16[512,512]{1,0:T(8,128)(2,1)} %w2.1, f32[1,512]{1,0:T(1,128)} %bitcast.11, bf16[512,512]{1,0:T(8,128)(2,1)} %w3.1, ...), custom_call_target="tpu_custom_call" | custom-call | flops 6442450944 | bytes 4000000 | tf_op jit(solution)/shard_map/network/pallas_call | solution.py:709
  58.5 1.1 %copy-done = bf16[768,512]{1,0:T(8,128)(2,1)S(1)} copy-done((bf16[768,512]{1,0:T(8,128)(2,1)S(1)}, bf16[768,512]{1,0:T(8,128)(2,1)}, u32[]{:S(2)}) %copy-start) | copy-done | bytes 786456
  59.6 0.4 rims.1
  60.0 0.1 collective-permute-start.5
  60.1 2.0 %collective-permute-start.4 = (f32[136,128]{1,0:T(8,128)S(1)}, f32[136,128]{1,0:T(8,128)S(1)}, u32[]{:S(2)}, u32[]{:S(2)}) collective-permute-start(f32[136,128]{1,0:T(8,128)S(1)} %get-tuple-element.34.xhi_ref), channel_id=1, source_target_pairs={{0,8},{8,16},{16,24},{24,0},{1,9},{9,17},{17,25},{25,1},{2,10},{10... | collective-permute-start | bytes 208904 | tf_op jit(solution)/shard_map/ppermute | solution.py:663
  62.1 23.0 %collective-permute-done.5.refs_3_.next_ref = f32[136,128]{1,0:T(8,128)S(1)} collective-permute-done((f32[136,128]{1,0:T(8,128)S(1)}, f32[136,128]{1,0:T(8,128)S(1)}, u32[]{:S(2)}, u32[]{:S(2)}) %collective-permute-start.5) | collective-permute-done | bytes 69664 | tf_op jit(solution)/shard_map/ppermute | solution.py:664
  85.2 1.7 %collective-permute-start.7 = (f32[128,128]{1,0:T(8,128)S(1)}, f32[128,128]{1,0:T(8,128)S(1)}, u32[]{:S(2)}, u32[]{:S(2)}) collective-permute-start(f32[128,128]{1,0:T(8,128)S(1)} %get-tuple-element.37.ylo_ref), channel_id=1, source_target_pairs={{0,7},{1,0},{2,1},{3,2},{4,3},{5,4},{6,5},{7,6},{8,15},{9,8},{10,9... | collective-permute-start | bytes 196616 | tf_op jit(solution)/shard_map/ppermute | solution.py:674
  86.9 1.9 %collective-permute-done.7.ynext_ref = f32[128,128]{1,0:T(8,128)S(1)} collective-permute-done((f32[128,128]{1,0:T(8,128)S(1)}, f32[128,128]{1,0:T(8,128)S(1)}, u32[]{:S(2)}, u32[]{:S(2)}) %collective-permute-start.7) | collective-permute-done | bytes 65568 | tf_op jit(solution)/shard_map/ppermute | solution.py:674
  88.8 2.7 %collective-permute-done.6.yprev_ref = f32[128,128]{1,0:T(8,128)S(1)} collective-permute-done((f32[128,128]{1,0:T(8,128)S(1)}, f32[128,128]{1,0:T(8,128)S(1)}, u32[]{:S(2)}, u32[]{:S(2)}) %collective-permute-start.6) | collective-permute-done | bytes 65568 | tf_op jit(solution)/shard_map/ppermute | solution.py:673
  91.5 0.6 copy-done.20
  92.1 9.5 %final.1 = f32[2,64,96,128]{3,2,1,0:T(8,128)} custom-call(f32[96,2,64,128]{3,2,1,0:T(8,128)} %get-tuple-element.23.refs_0_.adv_ref, bf16[768,512]{1,0:T(8,128)(2,1)} %network.1.inc_ref, f32[24,32]{1,0:T(8,128)} %jac_ref.5, f32[136,128]{1,0:T(8,128)} %copy-done.7, f32[136,128]{1,0:T(8,128)} %copy-done.8, f32[136,128]{1,0:T(8,128)} %copy-done.2, ...), custom_call_target="tpu_custom_call" | custom-call | flops 1000000000 | bytes 14000000 | tf_op jit(solution)/shard_map/final/pallas_call | solution.py:739
  101.6 2.4 %arrange.1 = bf16[3072,128]{1,0:T(8,128)(2,1)} custom-call(bf16[1536,512]{1,0:T(8,128)(2,1)S(1)} %bitcast.9), custom_call_target="tpu_custom_call" | custom-call | flops 1000000 | bytes 3000000 | tf_op jit(solution)/shard_map/arrange/pallas_call | solution.py:775
  (37 shorter events, 0.1 us)
Async XLA Ops:
  14.9 4.5 %collective-permute-start.1 = (f32[136,128]{1,0:T(8,128)}, f32[136,128]{1,0:T(8,128)S(1)}, u32[]{:S(2)}, u32[]{:S(2)}) collective-permute-start(f32[136,128]{1,0:T(8,128)} %get-tuple-element.26.refs_2_), channel_id=1, source_target_pairs={{0,24},{8,0},{16,8},{24,16},{1,25},{9,1},{17,9},{25,17},{2,26},{10... | collective-permute-start | bytes 208904 | tf_op jit(solution)/shard_map/ppermute | solution.py:664
  14.9 7.6 %collective-permute-start = (f32[136,128]{1,0:T(8,128)}, f32[136,128]{1,0:T(8,128)S(1)}, u32[]{:S(2)}, u32[]{:S(2)}) collective-permute-start(f32[136,128]{1,0:T(8,128)} %get-tuple-element.27.refs_3_), channel_id=1, source_target_pairs={{0,8},{8,16},{16,24},{24,0},{1,9},{9,17},{17,25},{25,1},{2,10},{10... | collective-permute-start | bytes 208904 | tf_op jit(solution)/shard_map/ppermute | solution.py:663
  22.5 0.8 copy-start.11
  23.4 0.8 copy-start.12
  24.2 7.7 %collective-permute-start.3 = (f32[128,128]{1,0:T(8,128)S(1)}, f32[128,128]{1,0:T(8,128)S(1)}, u32[]{:S(2)}, u32[]{:S(2)}) collective-permute-start(f32[128,128]{1,0:T(8,128)S(1)} %get-tuple-element.30.refs_6_), channel_id=1, source_target_pairs={{0,7},{1,0},{2,1},{3,2},{4,3},{5,4},{6,5},{7,6},{8,15},{9,8},{10,9... | collective-permute-start | bytes 196616 | tf_op jit(solution)/shard_map/ppermute | solution.py:674
  25.0 7.0 %collective-permute-start.2 = (f32[128,128]{1,0:T(8,128)S(1)}, f32[128,128]{1,0:T(8,128)S(1)}, u32[]{:S(2)}, u32[]{:S(2)}) collective-permute-start(f32[128,128]{1,0:T(8,128)S(1)} %get-tuple-element.31.refs_7_), channel_id=1, source_target_pairs={{0,1},{1,2},{2,3},{3,4},{4,5},{5,6},{6,7},{7,0},{8,9},{9,10},{10,1... | collective-permute-start | bytes 196616 | tf_op jit(solution)/shard_map/ppermute | solution.py:673
  25.0 7.0 %copy-start.15 = (f32[136,128]{1,0:T(8,128)S(1)}, f32[136,128]{1,0:T(8,128)}, u32[]{:S(2)}) copy-start(f32[136,128]{1,0:T(8,128)} %get-tuple-element.26.refs_2_) | copy-start | bytes 208900
  25.0 7.0 %copy-start.16 = (f32[136,128]{1,0:T(8,128)S(1)}, f32[136,128]{1,0:T(8,128)}, u32[]{:S(2)}) copy-start(f32[136,128]{1,0:T(8,128)} %get-tuple-element.27.refs_3_) | copy-start | bytes 208900
  32.0 1.4 %copy-start.14 = (f32[4,768,128]{2,1,0:T(8,128)S(1)}, f32[4,768,128]{2,1,0:T(8,128)}, u32[]{:S(2)}) copy-start(f32[4,768,128]{2,1,0:T(8,128)} %get-tuple-element.24.refs_0_) | copy-start | bytes 4718596
  33.4 0.7 copy-start.17
  37.2 0.7 copy-start.3
  37.9 0.6 copy-start.5
  38.5 0.6 copy-start.6
  39.2 0.6 copy-start.13
  39.7 0.9 copy-start.18
  40.6 61.0 %all-to-all-start = ((bf16[32,48,512]{2,1,0:T(8,128)(2,1)}), bf16[32,48,512]{2,1,0:T(8,128)(2,1)S(1)}, u32[]{:S(2)}, u32[]{:S(2)}) async-start(bf16[32,48,512]{2,1,0:T(8,128)(2,1)} %bitcast.7), calls=%async_computation | async-start | bytes 3145728 | tf_op jit(solution)/shard_map/all_to_all | solution.py:697
  45.8 12.6 %copy-start.4 = (f32[24,32]{1,0:T(8,128)S(1)}, f32[24,32]{1,0:T(8,128)}, u32[]{:S(2)}) copy-start(f32[24,32]{1,0:T(8,128)} %jac_ref.5) | copy-start | bytes 9220
  58.5 1.1 %copy-start = (bf16[768,512]{1,0:T(8,128)(2,1)S(1)}, bf16[768,512]{1,0:T(8,128)(2,1)}, u32[]{:S(2)}) copy-start(bf16[768,512]{1,0:T(8,128)(2,1)} %network.1.inc_ref) | copy-start | bytes 2359300
  60.0 31.4 %copy-start.7 = (f32[136,128]{1,0:T(8,128)}, f32[136,128]{1,0:T(8,128)S(1)}, u32[]{:S(2)}) copy-start(f32[136,128]{1,0:T(8,128)S(1)} %get-tuple-element.33.xlo_ref) | copy-start | bytes 208900
  60.0 31.4 %copy-start.8 = (f32[136,128]{1,0:T(8,128)}, f32[136,128]{1,0:T(8,128)S(1)}, u32[]{:S(2)}) copy-start(f32[136,128]{1,0:T(8,128)S(1)} %get-tuple-element.34.xhi_ref) | copy-start | bytes 208900
  60.0 25.1 %collective-permute-start.5 = (f32[136,128]{1,0:T(8,128)S(1)}, f32[136,128]{1,0:T(8,128)S(1)}, u32[]{:S(2)}, u32[]{:S(2)}) collective-permute-start(f32[136,128]{1,0:T(8,128)S(1)} %get-tuple-element.33.xlo_ref), channel_id=1, source_target_pairs={{0,24},{8,0},{16,8},{24,16},{1,25},{9,1},{17,9},{25,17},{2,26},{10... | collective-permute-start | bytes 208904 | tf_op jit(solution)/shard_map/ppermute | solution.py:664
  60.1 25.0 %collective-permute-start.4 = (f32[136,128]{1,0:T(8,128)S(1)}, f32[136,128]{1,0:T(8,128)S(1)}, u32[]{:S(2)}, u32[]{:S(2)}) collective-permute-start(f32[136,128]{1,0:T(8,128)S(1)} %get-tuple-element.34.xhi_ref), channel_id=1, source_target_pairs={{0,8},{8,16},{16,24},{24,0},{1,9},{9,17},{17,25},{25,1},{2,10},{10... | collective-permute-start | bytes 208904 | tf_op jit(solution)/shard_map/ppermute | solution.py:663
  85.1 6.3 %copy-start.1 = (f32[136,128]{1,0:T(8,128)}, f32[136,128]{1,0:T(8,128)S(1)}, u32[]{:S(2)}) copy-start(f32[136,128]{1,0:T(8,128)S(1)} %collective-permute-done.5.refs_3_.next_ref) | copy-start | bytes 208900
  85.1 6.3 %copy-start.2 = (f32[136,128]{1,0:T(8,128)}, f32[136,128]{1,0:T(8,128)S(1)}, u32[]{:S(2)}) copy-start(f32[136,128]{1,0:T(8,128)S(1)} %collective-permute-done.4.refs_2_.prev_ref) | copy-start | bytes 208900
  85.1 6.3 %copy-start.9 = (f32[128,128]{1,0:T(8,128)}, f32[128,128]{1,0:T(8,128)S(1)}, u32[]{:S(2)}) copy-start(f32[128,128]{1,0:T(8,128)S(1)} %get-tuple-element.37.ylo_ref) | copy-start | bytes 196612
  85.2 6.3 %copy-start.10 = (f32[128,128]{1,0:T(8,128)}, f32[128,128]{1,0:T(8,128)S(1)}, u32[]{:S(2)}) copy-start(f32[128,128]{1,0:T(8,128)S(1)} %get-tuple-element.38.yhi_ref) | copy-start | bytes 196612
  85.2 3.6 %collective-permute-start.7 = (f32[128,128]{1,0:T(8,128)S(1)}, f32[128,128]{1,0:T(8,128)S(1)}, u32[]{:S(2)}, u32[]{:S(2)}) collective-permute-start(f32[128,128]{1,0:T(8,128)S(1)} %get-tuple-element.37.ylo_ref), channel_id=1, source_target_pairs={{0,7},{1,0},{2,1},{3,2},{4,3},{5,4},{6,5},{7,6},{8,15},{9,8},{10,9... | collective-permute-start | bytes 196616 | tf_op jit(solution)/shard_map/ppermute | solution.py:674
  86.9 4.6 %collective-permute-start.6 = (f32[128,128]{1,0:T(8,128)S(1)}, f32[128,128]{1,0:T(8,128)S(1)}, u32[]{:S(2)}, u32[]{:S(2)}) collective-permute-start(f32[128,128]{1,0:T(8,128)S(1)} %get-tuple-element.38.yhi_ref), channel_id=1, source_target_pairs={{0,1},{1,2},{2,3},{3,4},{4,5},{5,6},{6,7},{7,0},{8,9},{9,10},{10,1... | collective-permute-start | bytes 196616 | tf_op jit(solution)/shard_map/ppermute | solution.py:673
  88.8 2.7 %copy-start.19 = (f32[128,128]{1,0:T(8,128)}, f32[128,128]{1,0:T(8,128)S(1)}, u32[]{:S(2)}) copy-start(f32[128,128]{1,0:T(8,128)S(1)} %collective-permute-done.7.ynext_ref) | copy-start | bytes 196612
  91.4 0.6 copy-start.20
where the time goes:
time: 105 us; the launch traced here: 104 us
  Pallas kernels  49.3 us (47%)
  waiting for transfers between devices  33.2 us (32%)
  starting transfers between devices  11.7 us (11%)
  local copies, waits for them, and re-layouts  8.89 us (8%)
    ppermute x2, waiting for transfers between devices, exchange(): later = lax.ppermute(xlo, 'face', shifted('face', -1))  25.5 us
    pallas_call x1, Pallas kernels, dynamics_call(): pl.pallas_call(dynamics_kernel, grid=(levels // tile,), in_specs=[pl.Bloc...  14.2 us
    pallas_call x1, Pallas kernels, on_device(): pl.pallas_call(network_kernel, grid=(3,), in_specs=[smem, pl.BlockSpec((c...  12.6 us
    pallas_call x1, Pallas kernels, on_device(): pl.pallas_call(final_kernel, grid=(elements_x // group,), in_specs=[pl.Bl...  9.53 us
    unnamed x42, local copies, waits for them, and re-layouts  8.89 us
    pallas_call x1, Pallas kernels, on_device(): pl.pallas_call(lambda *refs: cells_kernel(capacity, devices, *refs), grid...  6.96 us
    all_to_all x1, starting transfers between devices, on_device(): lax.all_to_all(outgoing.reshape(devices, capacity, 4 * features), ('face'...  5.19 us
    ppermute x2, starting transfers between devices, exchange(): prev = lax.ppermute(xhi, 'face', shifted('face', 1))  4.03 us
  transfers between devices with their start and end apart: 9, of which 5 were waited for; matrix products, arithmetic and copies ran while one was open for 0% of the time, Pallas kernels for 28%

commit v1 on v0

--- a/solution.py
+++ b/solution.py
@@ -73,8 +73,77 @@
     return inside, shared
 
 
+def element_slopes(f):
+    outer_gap, inner_gap = f[0] - f[3], f[1] - f[2]
+    bend = (f[1] + f[2]) - (f[0] + f[3])
+    odd = (D[0, 0] - D[0, 3]) / 2 * outer_gap + (D[0, 1] - D[0, 2]) / 2 * inner_gap
+    even = (D[0, 1] + D[0, 2]) / 2 * bend
+    odd_in = (D[1, 0] - D[1, 3]) / 2 * outer_gap - D[1, 2] / 2 * inner_gap
+    even_in = D[1, 2] / 2 * bend
+    return [odd + even, odd_in + even_in, odd_in - even_in, odd - even]
+
+
+def edges_kernel(
+    lit_ref, proglo_ref, proghi_ref, vello_ref, velhi_ref, jac_ref, dcat_ref, xlo_ref, xhi_ref,
+    vf_ref,
+):
+    elements_x, elements_y = jac_ref.shape
+    fields, levels, _, width = proglo_ref.shape
+    features = fields * levels
+    jac = jac_ref[...]
+    mass = along_lanes(jac, width)
+    joined = mass + copies_along_y(mass)
+    inside, _ = inner_reciprocals(joined)
+    lit = lit_ref[0, 0].astype(F32)
+    sides = ((proglo_ref, vello_ref, xlo_ref), (proghi_ref, velhi_ref, xhi_ref))
+    for side, (prog_ref, vel_ref, out_ref) in enumerate(sides):
+        p = side * (elements_x - 1)
+        lines = prog_ref.shape[2]
+        prog = prog_ref.reshape(features * lines, width)
+        first = side * (lines - 4)
+        f = [prog[pl.ds(first + k, features, stride=lines), :] for k in range(4)]
+        vlines = vel_ref.shape[2]
+        vf_ref[...] = vel_ref[...].astype(F32).reshape(2 * levels * vlines, width)
+        slopes = element_slopes(f)
+        turned, moved = [], []
+        for node in (3 * side, 1 + side):
+            row = node + side * (vlines - 4)
+            vx = vf_ref[pl.ds(row, levels, stride=vlines), :]
+            vy = vf_ref[pl.ds(levels * vlines + row, levels, stride=vlines), :]
+            high, low = split(f[node])
+            sy = jnp.dot(
+                jnp.concatenate([high, low, high], axis=1), dcat_ref[...],
+                preferred_element_type=F32,
+            )
+            vx = jnp.concatenate([vx] * fields, axis=0)
+            vy = jnp.concatenate([vy] * fields, axis=0)
+            line = (vx * slopes[node] + vy * sy) * (-TIME_STEP * jnp.sqrt(mass[p : p + 1]))
+            line = line + copies_along_y(line)
+            moved.append(line)
+            turned.append(line.T)
+        out_ref[0:features, :] = moved[0]
+        out_ref[features : 2 * features, :] = CELL_WEIGHTS[0] * f[3 * side] + CELL_WEIGHTS[1] * (
+            f[1 + side] + moved[1] * inside[p : p + 1]
+        )
+        out_ref[2 * features : 2 * features + 16, :] = jnp.concatenate(
+            [
+                turned[0][0:1],
+                turned[0][width - 1 : width],
+                joined[p : p + 1],
+                jnp.broadcast_to(jac[p : p + 1, 0:1], (1, width)),
+                jnp.broadcast_to(jac[p : p + 1, elements_y - 1 : elements_y], (1, width)),
+                turned[1][0:1],
+                turned[1][width - 1 : width],
+                jnp.broadcast_to(lit, (1, width)),
+                mass[p : p + 1],
+                jnp.zeros((7, width), F32),
+            ],
+            axis=0,
+        )
+
+
 def dynamics_kernel(
-    prog_ref, vel_ref, jac_ref, dcat_ref, adv_ref, xlo_ref, xhi_ref, ylo_ref, yhi_ref,
+    prog_ref, vel_ref, jac_ref, dcat_ref, adv_ref, ylo_ref, yhi_ref,
     sy3_ref, vf3_ref, pf3_ref, scale_ref, inside_ref, shared_ref, zlo_ref, zhi_ref,
 ):
     step = pl.program_id(0)
@@ -108,10 +177,6 @@
         ).reshape(piece, width_x, width)
 
     lane = iota((tile, width), 1)
-    p0, p1 = (D[0, 0] - D[0, 3]) / 2, (D[0, 1] - D[0, 2]) / 2
-    q0 = (D[0, 1] + D[0, 2]) / 2
-    r0, r1 = (D[1, 0] - D[1, 3]) / 2, -D[1, 2] / 2
-    t0 = D[1, 2] / 2
 
     def rims(lines):
         first, second, third = lines
@@ -147,13 +212,7 @@
             base = v * tile * pitch + 4 * p
             f = [pf_ref[pl.ds(base + k, tile, stride=pitch), :] for k in range(4)]
             sy = [sy_ref[pl.ds(base + k, tile, stride=pitch), :] for k in range(4)]
-            outer_gap, inner_gap = f[0] - f[3], f[1] - f[2]
-            bend = (f[1] + f[2]) - (f[0] + f[3])
-            odd = p0 * outer_gap + p1 * inner_gap
-            even = q0 * bend
-            odd_in = r0 * outer_gap + r1 * inner_gap
-            even_in = t0 * bend
-            sx = [odd + even, odd_in + even_in, odd_in - even_in, odd - even]
+            sx = element_slopes(f)
             e = []
             for k in range(4):
                 moved = (vx[k] * sx[k] + vy[k] * sy[k]) * scale
@@ -164,9 +223,7 @@
             adv_ref[4 * p + 1, v] = f[1] + e[1] * inside
             adv_ref[4 * p + 2, v] = f[2] + e[2] * inside
 
-            if p == 0:
-                xlo_ref[pl.ds(pl.multiple_of(v * levels + tile * step, tile), tile), :] = joined
-            else:
+            if p > 0:
                 adv_ref[4 * p - 1, v] = last_f + gain
 
             low, high = rims((joined, e[1], e[2]))
@@ -184,7 +241,6 @@
         last_e, last_f, z_low, z_high = final[4 * v : 4 * v + 4]
         at = pl.ds(pl.multiple_of(v * levels + tile * step, tile), tile)
         adv_ref[width_x - 1, v] = last_f
-        xhi_ref[at, :] = last_e
         zlo_ref[at, :] = jnp.where(
             lane == width_x - 1, pltpu.roll(last_e, width_x - 1, 1), z_low
         )
@@ -195,25 +251,11 @@
     @pl.when(step == pl.num_programs(0) - 1)
     def _():
         jac = jac_ref[...]
-        mass = along_lanes(jac, width)
-        mass = mass + copies_along_y(mass)
         ylo_ref[...] = zlo_ref[...].T
         yhi_ref[...] = zhi_ref[...].T
         for ref, q in ((ylo_ref, 0), (yhi_ref, elements_y - 1)):
             ref[width_x : width_x + elements_x, :] = jnp.broadcast_to(
                 jac[:, q : q + 1], (elements_x, features)
-            )
-        for ref, x, p in ((xlo_ref, 0, 0), (xhi_ref, width_x - 1, elements_x - 1)):
-            ref[features : features + 8, :] = jnp.concatenate(
-                [
-                    ylo_ref[x : x + 1, :],
-                    yhi_ref[x : x + 1, :],
-                    mass[p : p + 1, :],
-                    ylo_ref[width_x + p : width_x + p + 1, :],
-                    yhi_ref[width_x + p : width_x + p + 1, :],
-                    jnp.zeros((3, width), F32),
-                ],
-                axis=0,
             )
 
 
@@ -279,27 +321,29 @@
 
 
 def corners_kernel(width_x, elements_x, ylo_ref, yhi_ref, prev_ref, next_ref, ylo_out, yhi_out):
-    features = prev_ref.shape[0] - 8
+    tail = prev_ref.shape[0] - 16
     spare = width_x + elements_x
     for side, (ref, out) in enumerate(((ylo_ref, ylo_out), (yhi_ref, yhi_out))):
         row = iota(ref.shape, 0)
         values = ref[...]
-        prev = prev_ref[features + side : features + side + 1, :]
-        later = next_ref[features + side : features + side + 1, :]
-        prev_mass = prev_ref[features + 3 + side : features + 4 + side, :]
-        later_mass = next_ref[features + 3 + side : features + 4 + side, :]
-        values = values + jnp.where(row == 0, prev, 0.0)
-        values = values + jnp.where(row == width_x - 1, later, 0.0)
-        values = jnp.where(row == spare, prev_mass, values)
-        out[...] = jnp.where(row == spare + 1, later_mass, values)
-
-
-def send_kernel(
+        for k, (packet, x) in enumerate(((prev_ref, 0), (next_ref, width_x - 1))):
+            rim = packet[tail + side : tail + side + 1, :]
+            mass = packet[tail + 3 + side : tail + 4 + side, :]
+            inner = packet[tail + 5 + side : tail + 6 + side, :]
+            values = values + jnp.where(row == x, rim, 0.0)
+            values = jnp.where(row == spare + k, mass, values)
+            values = jnp.where(row == spare + 2 + k, inner, values)
+        out[...] = values
+
+
+def complete_kernel(
     width_x, elements_x,
-    col_ref, slot_ref, xlo_ref, xhi_ref, prev_ref, next_ref, ylo_ref, yhi_ref, yprev_ref,
-    ynext_ref, colbf_ref, out_ref, fy_ref, ry_ref, fx_ref, rx_ref, work_ref,
+    col_ref, xlo_ref, xhi_ref, prev_ref, next_ref, ylo_ref, yhi_ref, yprev_ref,
+    ynext_ref, colbf_ref, fy_ref, ry_ref, fx_ref, rx_ref, ghost_ref, work_ref, cell_ref,
 ):
     _, elements, features = col_ref.shape
+    tail = 2 * features
+    ghost_fixes = []
     elements_y = elements // elements_x
     width = xlo_ref.shape[1]
     work_ref[...] = col_ref[...]
@@ -321,6 +365,7 @@
         ry_ref[side, pl.ds(2, elements_x, stride=4), :] = inside
         ry_ref[side, pl.ds(3, elements_x, stride=4), :] = 1.0 / (mass + after)
         fy_ref[side] = total[:width_x] * ry_ref[side]
+        ghost_fixes.append(total[spare + 2 : spare + 4] / total[spare : spare + 2])
         fixes = [fy_ref[side, pl.ds(k, elements_x, stride=4), :] for k in range(4)]
         at = pl.ds(side * (elements_y - 1), elements_x, stride=elements_y)
         for a in range(2):
@@ -328,7 +373,7 @@
             k = 2 * a + side
             work_ref[k, at, :] = work_ref[k, at, :] + CELL_WEIGHTS[0] * added
     for side, (own, other) in enumerate(((xlo_ref, prev_ref), (xhi_ref, next_ref))):
-        mass = own[features + 2 : features + 3, :] + other[features + 2 : features + 3, :]
+        mass = own[tail + 2 : tail + 3, :] + other[tail + 2 : tail + 3, :]
         reciprocal = jnp.where(inner, 1.0 / mass, 0.0)
         rx_ref[side] = jnp.broadcast_to(reciprocal, (8, width))
         fix = (own[:features] + other[:features]) * reciprocal
@@ -337,8 +382,24 @@
         at = slice(side * (elements_x - 1) * elements_y, (side * (elements_x - 1) + 1) * elements_y)
         work_ref[2 * side, at, :] = work_ref[2 * side, at, :] + low
         work_ref[2 * side + 1, at, :] = work_ref[2 * side + 1, at, :] + high
+        line = other[features : 2 * features] + CELL_WEIGHTS[0] * fix
+        cell_ref[2 * side], cell_ref[2 * side + 1] = cells_of_line(line, select)
+        for end in range(2):
+            x = side * (width_x - 1)
+            added = CELL_WEIGHTS[0] * fy_ref[end, x : x + 1, :]
+            added = added + CELL_WEIGHTS[1] * ghost_fixes[end][side : side + 1]
+            q = end * (elements_y - 1)
+            cell_ref[2 * side + end, q : q + 1, :] = (
+                cell_ref[2 * side + end, q : q + 1, :] + CELL_WEIGHTS[0] * added
+            )
+    for k in range(4):
+        ghost_ref[k * elements_y : (k + 1) * elements_y, :] = cell_ref[k].astype(BF16)
     for k in range(4):
         colbf_ref[:, k * features : (k + 1) * features] = work_ref[k].astype(BF16)
+
+
+def send_kernel(colbf_ref, slot_ref, out_ref):
+    elements = colbf_ref.shape[0]
     slots = out_ref.shape[0]
     piece = slots // 4
     for part in range(4):
@@ -358,28 +419,49 @@
 
 
 def network_kernel(
-    lit_ref, col_ref, w1, b1, w2, b2, w3, b3, w4, b4, s1, c1, s2, c2, s3, c3, inc_ref, total_ref
+    lit_ref, col_ref, ghost_ref, prev_ref, next_ref, w1, b1, w2, b2, w3, b3, w4, b4, s1, c1, s2,
+    c2, s3, c3, inc_ref, ghost_inc_ref, total_ref,
 ):
     rows = col_ref.shape[0]
     features = col_ref.shape[1] // 4
     inputs = jnp.concatenate(
         [col_ref[:, k * features : (k + 1) * features] for k in range(4)], axis=0
     )
-    hidden = leaky(dense(inputs, w1, b1))
-    hidden = leaky(dense(hidden, w2, b2))
-    hidden = leaky(dense(hidden, w3, b3))
-    total_ref[...] = dense(hidden, w4, b4)
+    total_ref[...] = primary(inputs, w1, b1, w2, b2, w3, b3, w4, b4)
 
     @pl.when(lit_ref[0, 0] != 0)
     def _():
-        solar = leaky(dense(inputs, s1, c1))
-        solar = leaky(dense(solar, s2, c2))
-        total_ref[...] += lit_ref[0, 0].astype(F32) * dense(solar, s3, c3)
+        total_ref[...] += lit_ref[0, 0].astype(F32) * solar(inputs, s1, c1, s2, c2, s3, c3)
 
     for k in range(4):
         inc_ref[:, k * features : (k + 1) * features] = total_ref[
             k * rows : (k + 1) * rows, :
         ].astype(BF16)
+
+    @pl.when(pl.program_id(0) == 0)
+    def _():
+        near = ghost_ref[...]
+        tail = 2 * features + 7
+        row = iota(near.shape, 0)
+        lit = jnp.where(
+            row < near.shape[0] // 2, prev_ref[tail : tail + 1, :], next_ref[tail : tail + 1, :]
+        )
+        near_inc = primary(near, w1, b1, w2, b2, w3, b3, w4, b4)
+        near_inc = near_inc + lit * solar(near, s1, c1, s2, c2, s3, c3)
+        ghost_inc_ref[...] = near_inc.astype(BF16)
+
+
+def primary(inputs, w1, b1, w2, b2, w3, b3, w4, b4):
+    hidden = leaky(dense(inputs, w1, b1))
+    hidden = leaky(dense(hidden, w2, b2))
+    hidden = leaky(dense(hidden, w3, b3))
+    return dense(hidden, w4, b4)
+
+
+def solar(inputs, s1, c1, s2, c2, s3, c3):
+    hidden = leaky(dense(inputs, s1, c1))
+    hidden = leaky(dense(hidden, s2, c2))
+    return dense(hidden, s3, c3)
 
 
 def spread_operand(mass_line, elements_y):
@@ -400,52 +482,56 @@
 
 def spread_line(inc_ref, p, a, operand, elements_y):
     features = inc_ref.shape[1] // 4
-    at = pl.ds(pl.multiple_of(p * elements_y, elements_y), elements_y)
+    start = p * elements_y
+    if not isinstance(p, int):
+        start = pl.multiple_of(start, elements_y)
+    at = pl.ds(start, elements_y)
     cells = [
         inc_ref[at, (2 * a + b) * features : (2 * a + b + 1) * features] for b in range(2)
     ]
+    return spread_cells(cells, operand)
+
+
+def spread_cells(cells, operand):
     return lax.dot_general(
         jnp.concatenate(cells + cells, axis=0), operand, (((0,), (0,)), ((), ())),
         preferred_element_type=F32,
     )
 
 
-def rims_kernel(inc_ref, jac_ref, xlo_ref, xhi_ref, ylo_ref, yhi_ref, wide_ref):
+def rims_kernel(inc_ref, near_ref, jac_ref, prev_ref, next_ref, ylo_ref, yhi_ref, wide_ref):
     elements_x, elements_y = jac_ref.shape
-    features = inc_ref.shape[1] // 4
-    width = xlo_ref.shape[1]
+    features = near_ref.shape[1]
     width_x = 4 * elements_x
+    tail = 2 * features
     for k in range(4):
         wide_ref[k] = inc_ref[:, k * features : (k + 1) * features].astype(F32)
-    mass = along_lanes(jac_ref[...], width)
+    near = near_ref[...].astype(F32)
     for side, ref in enumerate((ylo_ref, yhi_ref)):
         q = side * (elements_y - 1)
         column = jac_ref[:, q : q + 1]
         at = pl.ds(q, elements_x, stride=elements_y)
         first = column * wide_ref[side, at, :]
         second = column * wide_ref[2 + side, at, :]
+        ghosts = []
+        for k, packet in enumerate((prev_ref, next_ref)):
+            cell = (2 * k + side) * elements_y + q
+            mass = packet[tail + 3 + side : tail + 4 + side, :]
+            ghosts.append(mass * near[cell : cell + 1])
         row = iota(first.shape, 0)
         ref[pl.ds(0, elements_x, stride=4), :] = first + jnp.where(
-            row == 0, 0.0, pltpu.roll(second, 1, 0)
+            row == 0, ghosts[0], pltpu.roll(second, 1, 0)
         )
         ref[pl.ds(1, elements_x, stride=4), :] = first
         ref[pl.ds(2, elements_x, stride=4), :] = second
         ref[pl.ds(3, elements_x, stride=4), :] = second + jnp.where(
-            row == elements_x - 1, 0.0, pltpu.roll(first, elements_x - 1, 0)
+            row == elements_x - 1, ghosts[1], pltpu.roll(first, elements_x - 1, 0)
         )
         ref[width_x:, :] = jnp.zeros((ref.shape[0] - width_x, features), F32)
-    for side, ref in enumerate((xlo_ref, xhi_ref)):
-        p = side * (elements_x - 1)
-        x = side * (width_x - 1)
-        operand = spread_operand(mass[p : p + 1], elements_y)
-        ref[0:features, :] = spread_line(inc_ref, p, side, operand, elements_y)
-        ref[features : features + 8, :] = jnp.concatenate(
-            [ylo_ref[x : x + 1, :], yhi_ref[x : x + 1, :], jnp.zeros((6, width), F32)], axis=0
-        )
 
 
 def final_kernel(
-    adv_ref, inc_ref, jac_ref, xlo_ref, xhi_ref, prev_ref, next_ref, ylo_ref, yhi_ref, yprev_ref,
+    adv_ref, inc_ref, near_ref, jac_ref, prev_ref, next_ref, ylo_ref, yhi_ref, yprev_ref,
     ynext_ref, fy_ref, ry_ref, fx_ref, rx_ref, out_ref, mass_ref, inside_ref, shared_ref,
     rim_ref, edge_ref,
 ):
@@ -467,10 +553,18 @@
         shared_ref[elements_x:, :] = jnp.zeros((8, width), F32)
         for side, (own, other) in enumerate(((ylo_ref, yprev_ref), (yhi_ref, ynext_ref))):
             rim_ref[side] = fy_ref[side] + (own[0:width_x, :] + other[0:width_x, :]) * ry_ref[side]
-        for side, (own, other) in enumerate(((xlo_ref, prev_ref), (xhi_ref, next_ref))):
-            edge_ref[side] = (
-                fx_ref[side] + (own[0:features, :] + other[0:features, :]) * rx_ref[side, 0:1, :]
+        for side, packet in enumerate((prev_ref, next_ref)):
+            p = side * (elements_x - 1)
+            own = spread_line(
+                inc_ref, p, side, spread_operand(mass[p : p + 1], elements_y), elements_y
             )
+            tail = 2 * features + 8
+            at = 2 * side * elements_y
+            other = spread_cells(
+                [near_ref[at : at + 2 * elements_y, :]],
+                spread_operand(packet[tail : tail + 1, :], elements_y),
+            )
+            edge_ref[side] = fx_ref[side] + (own + other) * rx_ref[side, 0:1, :]
 
     out = out_ref.reshape(features * lines, width)
     row = iota((16, width), 0)
@@ -571,12 +665,37 @@
     return [(i, (i + by) % count) for i in range(count)]
 
 
+def edges_call(sunlit, prognostic, velocity, jacobian):
+    fields, levels, width_x, width = prognostic.shape
+    features = fields * levels
+    last = width_x // 8 - 1, width_x // 16 - 1
+    dcat = jnp.asarray(y_derivative_operand(width))
+    return pl.pallas_call(
+        edges_kernel,
+        grid=(1,),
+        in_specs=[
+            pl.BlockSpec(memory_space=pltpu.SMEM),
+            pl.BlockSpec((fields, levels, 8, width), lambda g: (0, 0, 0, 0)),
+            pl.BlockSpec((fields, levels, 8, width), lambda g: (0, 0, last[0], 0)),
+            pl.BlockSpec((2, levels, 16, width), lambda g: (0, 0, 0, 0)),
+            pl.BlockSpec((2, levels, 16, width), lambda g: (0, 0, last[1], 0)),
+            whole(jacobian.shape),
+            whole((3 * width, width)),
+        ],
+        out_specs=[whole((2 * features + 16, width))] * 2,
+        out_shape=[shape_of((2 * features + 16, width))] * 2,
+        scratch_shapes=[pltpu.VMEM((2 * levels * 16, width), F32)],
+        compiler_params=params(58),
+        cost_estimate=cost(50_000_000, 2_000_000),
+        name="edges",
+    )(sunlit, prognostic, prognostic, velocity, velocity, jacobian, dcat)
+
+
 def dynamics_call(prognostic, velocity, jacobian):
     fields, levels, width_x, width = prognostic.shape
     elements_x, elements_y = jacobian.shape
     features = fields * levels
     tile = 8
-    packet = features + 8
     dcat = jnp.asarray(y_derivative_operand(width))
     return pl.pallas_call(
         dynamics_kernel,
@@ -589,15 +708,11 @@
         ],
         out_specs=[
             pl.BlockSpec((width_x, 2, tile, width), lambda t: (0, 0, t, 0)),
-            whole((packet, width)),
-            whole((packet, width)),
             whole((width, features)),
             whole((width, features)),
         ],
         out_shape=[
             shape_of((width_x, fields, levels, width)),
-            shape_of((packet, width)),
-            shape_of((packet, width)),
             shape_of((width, features)),
             shape_of((width, features)),
         ],
@@ -632,11 +747,12 @@
     devices = lax.axis_size("face") * lax.axis_size("dom")
     capacity = max(2, 2 * elements // devices)
     slots = devices * capacity
-    packet = features + 8
+    packet = 2 * features + 16
     vmem = pl.BlockSpec(memory_space=pltpu.VMEM)
     smem = pl.BlockSpec(memory_space=pltpu.SMEM)
 
-    adv, xlo, xhi, ylo, yhi = dynamics_call(prognostic, velocity, jacobian)
+    xlo, xhi = edges_call(sunlit, prognostic, velocity, jacobian)
+    adv, ylo, yhi = dynamics_call(prognostic, velocity, jacobian)
 
     group = 4
     col, slot_ids = pl.pallas_call(
@@ -654,50 +770,44 @@
             shape_of((4, elements, features)),
             shape_of((1, elements), jnp.int32),
         ],
-        compiler_params=params(58),
+        compiler_params=params(20),
         cost_estimate=cost(1_000_000_000, 8_000_000),
         name="cells",
     )(adv, element_span)
 
-    def exchange(xlo, xhi, ylo, yhi):
-        prev = lax.ppermute(xhi, "face", shifted("face", 1))
-        later = lax.ppermute(xlo, "face", shifted("face", -1))
-        ylo, yhi = pl.pallas_call(
-            lambda *refs: corners_kernel(width_x, elements_x, *refs),
-            in_specs=[vmem] * 4,
-            out_specs=[vmem] * 2,
-            out_shape=[shape_of((width, features))] * 2,
-            compiler_params=params(16),
-            name="corners",
-        )(ylo, yhi, prev, later)
-        yprev = lax.ppermute(yhi, "dom", shifted("dom", 1))
-        ynext = lax.ppermute(ylo, "dom", shifted("dom", -1))
-        return prev, later, ylo, yhi, yprev, ynext
-
-    prev, later, ylo, yhi, yprev, ynext = exchange(xlo, xhi, ylo, yhi)
-
-    colbf, outgoing, fy, ry, fx, rx = pl.pallas_call(
-        lambda *refs: send_kernel(width_x, elements_x, *refs),
-        in_specs=[vmem] * 10,
+    prev = lax.ppermute(xhi, "face", shifted("face", 1))
+    later = lax.ppermute(xlo, "face", shifted("face", -1))
+    ylo, yhi = pl.pallas_call(
+        lambda *refs: corners_kernel(width_x, elements_x, *refs),
+        in_specs=[vmem] * 4,
+        out_specs=[vmem] * 2,
+        out_shape=[shape_of((width, features))] * 2,
+        compiler_params=params(12),
+        name="corners",
+    )(ylo, yhi, prev, later)
+    yprev = lax.ppermute(yhi, "dom", shifted("dom", 1))
+    ynext = lax.ppermute(ylo, "dom", shifted("dom", -1))
+
+    colbf, fy, ry, fx, rx, ghosts = pl.pallas_call(
+        lambda *refs: complete_kernel(width_x, elements_x, *refs),
+        in_specs=[vmem] * 9,
         out_specs=[vmem] * 6,
         out_shape=[
             shape_of((elements, 4 * features), BF16),
-            shape_of((slots, 4 * features), BF16),
             shape_of((2, width_x, features)),
             shape_of((2, width_x, features)),
             shape_of((2, features, width)),
             shape_of((2, 8, width)),
-        ],
-        scratch_shapes=[pltpu.VMEM((4, elements, features), F32)],
-        compiler_params=params(24),
-        cost_estimate=cost(2_000_000_000, 5_000_000),
-        name="send",
-    )(col, slot_ids, xlo, xhi, prev, later, ylo, yhi, yprev, ynext)
-
-    arrived = lax.all_to_all(
-        outgoing.reshape(devices, capacity, 4 * features), ("face", "dom"),
-        split_axis=0, concat_axis=0, tiled=True,
-    ).reshape(slots, 4 * features)
+            shape_of((4 * elements_y, features), BF16),
+        ],
+        scratch_shapes=[
+            pltpu.VMEM((4, elements, features), F32),
+            pltpu.VMEM((4, elements_y, features), F32),
+        ],
+        compiler_params=params(16),
+        cost_estimate=cost(10_000_000, 3_000_000),
+        name="complete",
+    )(col, xlo, xhi, prev, later, ylo, yhi, yprev, ynext)
 
     chunk = elements // 3
     hidden = weights[0].shape[1]
@@ -706,35 +816,58 @@
         item = item if item.ndim == 2 else item.reshape(1, -1)
         operands.append(item)
         operand_specs.append(whole(item.shape))
-    inc = pl.pallas_call(
+    outgoing = pl.pallas_call(
+        send_kernel,
+        in_specs=[vmem] * 2,
+        out_specs=vmem,
+        out_shape=shape_of((slots, 4 * features), BF16),
+        compiler_params=params(16),
+        cost_estimate=cost(2_000_000_000, 3_000_000),
+        name="send",
+    )(colbf, slot_ids)
+
+    arrived = lax.all_to_all(
+        outgoing.reshape(devices, capacity, 4 * features), ("face", "dom"),
+        split_axis=0, concat_axis=0, tiled=True,
+    ).reshape(slots, 4 * features)
+
+    inc, near = pl.pallas_call(
         network_kernel,
         grid=(3,),
-        in_specs=[smem, pl.BlockSpec((chunk, 4 * features), lambda g: (g, 0))] + operand_specs,
-        out_specs=pl.BlockSpec((chunk, 4 * features), lambda g: (g, 0)),
-        out_shape=shape_of((elements, 4 * features), BF16),
+        in_specs=[
+            smem,
+            pl.BlockSpec((chunk, 4 * features), lambda g: (g, 0)),
+            whole((4 * elements_y, features)),
+            whole((packet, width)),
+            whole((packet, width)),
+        ]
+        + operand_specs,
+        out_specs=[
+            pl.BlockSpec((chunk, 4 * features), lambda g: (g, 0)),
+            whole((4 * elements_y, features)),
+        ],
+        out_shape=[
+            shape_of((elements, 4 * features), BF16),
+            shape_of((4 * elements_y, features), BF16),
+        ],
         scratch_shapes=[pltpu.VMEM((4 * chunk, features), F32)],
-        compiler_params=params(58),
+        compiler_params=params(24),
         cost_estimate=cost(8 * elements * (4 * features * hidden + 3 * hidden * hidden), 4_000_000),
         name="network",
-    )(sunlit, colbf, *operands)
-
-    xlo2, xhi2, ylo2, yhi2 = pl.pallas_call(
+    )(sunlit, colbf, ghosts, prev, later, *operands)
+
+    ylo2, yhi2 = pl.pallas_call(
         rims_kernel,
-        in_specs=[vmem] * 2,
-        out_specs=[vmem] * 4,
-        out_shape=[
-            shape_of((packet, width)),
-            shape_of((packet, width)),
-            shape_of((width, features)),
-            shape_of((width, features)),
-        ],
+        in_specs=[vmem] * 5,
+        out_specs=[vmem] * 2,
+        out_shape=[shape_of((width, features))] * 2,
         scratch_shapes=[pltpu.VMEM((4, elements, features), F32)],
         compiler_params=params(16),
         cost_estimate=cost(10_000_000, 2_000_000),
         name="rims",
-    )(inc, jacobian)
-
-    prev2, later2, ylo2, yhi2, yprev2, ynext2 = exchange(xlo2, xhi2, ylo2, yhi2)
+    )(inc, near, jacobian, prev, later)
+    yprev2 = lax.ppermute(yhi2, "dom", shifted("dom", 1))
+    ynext2 = lax.ppermute(ylo2, "dom", shifted("dom", -1))
 
     new_state = pl.pallas_call(
         final_kernel,
@@ -742,9 +875,8 @@
         in_specs=[
             pl.BlockSpec((4 * group, fields, levels, width), lambda g: (g, 0, 0, 0)),
             whole((elements, 4 * features)),
+            whole((4 * elements_y, features)),
             whole((elements_x, elements_y)),
-            whole((packet, width)),
-            whole((packet, width)),
             whole((packet, width)),
             whole((packet, width)),
             whole((width, features)),
@@ -765,11 +897,11 @@
             pltpu.VMEM((2, width_x, features), F32),
             pltpu.VMEM((2, features, width), F32),
         ],
-        compiler_params=params(58),
+        compiler_params=params(20),
         cost_estimate=cost(1_000_000_000, 14_000_000),
         name="final",
     )(
-        adv, inc, jacobian, xlo2, xhi2, prev2, later2, ylo2, yhi2, yprev2, ynext2, fy, ry, fx, rx
+        adv, inc, near, jacobian, prev, later, ylo2, yhi2, yprev2, ynext2, fy, ry, fx, rx
     )
 
     span_state = pl.pallas_call(

time: 105 us -> 80.1 us (0.76)
  the two profiles are of different devices: /device:TPU:8 before, /device:TPU:0 now
where the time goes in v1:
time: 80.1 us; the launch traced here: 79.3 us
  Pallas kernels  39.6 us (49%)
  starting transfers between devices  13.8 us (17%)
  local copies, waits for them, and re-layouts  13.2 us (16%)
  waiting for transfers between devices  11.9 us (15%)
  between operations  0.84 us (1%)
    pallas_call x1, Pallas kernels, dynamics_call(): pl.pallas_call(dynamics_kernel, grid=(levels // tile,), in_specs=[pl.Bloc...  14 us
    unnamed x48, local copies, waits for them, and re-layouts  13.2 us
    all_to_all x1, waiting for transfers between devices, on_device(): lax.all_to_all(outgoing.reshape(devices, capacity, 4 * features), ('face'...  8.83 us
    pallas_call x1, Pallas kernels, on_device(): pl.pallas_call(network_kernel, grid=(3,), in_specs=[smem, pl.BlockSpec((c...  7.67 us
    pallas_call x1, Pallas kernels, on_device(): pl.pallas_call(final_kernel, grid=(elements_x // group,), in_specs=[pl.Bl...  6.64 us
    all_to_all x1, starting transfers between devices, on_device(): lax.all_to_all(outgoing.reshape(devices, capacity, 4 * features), ('face'...  3.32 us
    ppermute x1, starting transfers between devices, on_device(): prev = lax.ppermute(xhi, 'face', shifted('face', 1))  3.02 us
    ppermute x1, waiting for transfers between devices, on_device(): yprev2 = lax.ppermute(yhi2, 'dom', shifted('dom', 1))  3.02 us
  transfers between devices with their start and end apart: 7, of which 2 were waited for; matrix products, arithmetic and copies ran while one was open for 0% of the time, Pallas kernels for 39%

profile of v1, /device:TPU:0, one launch (start us, length us, event | category | flops | bytes accessed | tf_op | source)
XLA Modules:
  0.0 79.3 jit_solution(10107936349731738730)
XLA Ops:
  0.6 2.9 %edges.1 = (f32[272,128]{1,0:T(8,128)}, f32[272,128]{1,0:T(8,128)}) custom-call(s32[24,32]{1,0:T(8,128)} %lit_ref.3, f32[2,64,96,128]{3,2,1,0:T(8,128)} %proghi_ref.1, f32[2,64,96,128]{3,2,1,0:T(8,128)} %proghi_ref.1, bf16[2,64,96,128]{3,2,1,0:T(8,128)(2,1)} %velhi_ref.1, bf16[2,64,96,128]{3,2,1,0:T(8,128)(2,1)} %velhi_ref.1, f32[24,32]{1,0:T(8,128)} %jac_ref.7, ...), custom_call_target="tpu_custom_call" | custom-call | flops 50000000 | bytes 2000000 | tf_op jit(solution)/shard_map/edges/pallas_call | solution.py:673
  3.5 3.0 %collective-permute-start = (f32[272,128]{1,0:T(8,128)}, f32[272,128]{1,0:T(8,128)S(1)}, u32[]{:S(2)}, u32[]{:S(2)}) collective-permute-start(f32[272,128]{1,0:T(8,128)} %get-tuple-element.24.refs_2_), channel_id=1, source_target_pairs={{0,8},{8,16},{16,24},{24,0},{1,9},{9,17},{17,25},{25,1},{2,10},{10... | collective-permute-start | bytes 417800 | tf_op jit(solution)/shard_map/ppermute | solution.py:778
  6.5 2.1 %collective-permute-start.1 = (f32[272,128]{1,0:T(8,128)}, f32[272,128]{1,0:T(8,128)S(1)}, u32[]{:S(2)}, u32[]{:S(2)}) collective-permute-start(f32[272,128]{1,0:T(8,128)} %get-tuple-element.23.refs_1_), channel_id=1, source_target_pairs={{0,24},{8,0},{16,8},{24,16},{1,25},{9,1},{17,9},{25,17},{2,26},{10... | collective-permute-start | bytes 417800 | tf_op jit(solution)/shard_map/ppermute | solution.py:779
  8.6 14.0 %dynamics.1 = (f32[96,2,64,128]{3,2,1,0:T(8,128)}, f32[128,128]{1,0:T(8,128)}, f32[128,128]{1,0:T(8,128)}) custom-call(f32[2,64,96,128]{3,2,1,0:T(8,128)} %proghi_ref.1, bf16[2,64,96,128]{3,2,1,0:T(8,128)(2,1)} %velhi_ref.1, f32[24,32]{1,0:T(8,128)} %jac_ref.7, bf16[384,128]{1,0:T(8,128)(2,1)} %constant.2.clone.dcat_ref), custom_call_target="tpu_custom_call" | custom-call | flops 2000000000 | bytes 16000000 | tf_op jit(solution)/shard_map/dynamics/pallas_call | solution.py:700
  22.6 0.8 %copy-done.4 = f32[128,128]{1,0:T(8,128)S(1)} copy-done((f32[128,128]{1,0:T(8,128)S(1)}, f32[128,128]{1,0:T(8,128)}, u32[]{:S(2)}) %copy-start.4) | copy-done | bytes 65560
  23.5 0.8 %copy-done.5 = f32[128,128]{1,0:T(8,128)S(1)} copy-done((f32[128,128]{1,0:T(8,128)S(1)}, f32[128,128]{1,0:T(8,128)}, u32[]{:S(2)}) %copy-start.5) | copy-done | bytes 65560
  24.3 0.1 collective-permute-start.2
  24.4 2.6 %collective-permute-start.3 = (f32[128,128]{1,0:T(8,128)S(1)}, f32[128,128]{1,0:T(8,128)S(1)}, u32[]{:S(2)}, u32[]{:S(2)}) collective-permute-start(f32[128,128]{1,0:T(8,128)S(1)} %get-tuple-element.27.refs_5_), channel_id=1, source_target_pairs={{0,7},{1,0},{2,1},{3,2},{4,3},{5,4},{6,5},{7,6},{8,15},{9,8},{10,9... | collective-permute-start | bytes 196616 | tf_op jit(solution)/shard_map/ppermute | solution.py:789
  27.0 2.8 %copy-done = f32[96,2,64,128]{3,2,1,0:T(8,128)S(1)} copy-done((f32[96,2,64,128]{3,2,1,0:T(8,128)S(1)}, f32[96,2,64,128]{3,2,1,0:T(8,128)}, u32[]{:S(2)}) %copy-start) | copy-done | bytes 6291480
  29.8 2.8 %cells.1 = (f32[4,768,128]{2,1,0:T(8,128)S(1)}, s32[1,768]{1,0:T(1,128)S(1)}) custom-call(f32[96,2,64,128]{3,2,1,0:T(8,128)S(1)} %copy-done, s32[24,32]{1,0:T(8,128)S(1)} %copy-done.7), custom_call_target="tpu_custom_call" | custom-call | flops 1000000000 | bytes 8000000 | tf_op jit(solution)/shard_map/cells/pallas_call | solution.py:758
  32.7 0.5 complete.1
  33.2 2.7 %send.1 = bf16[1536,512]{1,0:T(8,128)(2,1)} custom-call(bf16[768,512]{1,0:T(8,128)(2,1)S(1)} %get-tuple-element.29.col_ref.colbf_ref, s32[1,768]{1,0:T(1,128)S(1)} %get-tuple-element.39.slot_ref), custom_call_target="tpu_custom_call" | custom-call | flops 2000000000 | bytes 3000000 | tf_op jit(solution)/shard_map/send/pallas_call | solution.py:819
  35.9 3.3 %all-to-all-start = ((bf16[32,48,512]{2,1,0:T(8,128)(2,1)}), bf16[32,48,512]{2,1,0:T(8,128)(2,1)S(1)}, u32[]{:S(2)}, u32[]{:S(2)}) async-start(bf16[32,48,512]{2,1,0:T(8,128)(2,1)} %bitcast.7), calls=%async_computation | async-start | bytes 3145728 | tf_op jit(solution)/shard_map/all_to_all | solution.py:829
  39.2 0.0 slice-start
  39.3 1.2 %copy-done.9 = bf16[512,512]{1,0:T(8,128)(2,1)S(1)} copy-done((bf16[512,512]{1,0:T(8,128)(2,1)S(1)}, bf16[512,512]{1,0:T(8,128)(2,1)}, u32[]{:S(2)}) %copy-start.9) | copy-done | bytes 524312
  40.5 1.2 %copy-done.10 = bf16[512,512]{1,0:T(8,128)(2,1)S(1)} copy-done((bf16[512,512]{1,0:T(8,128)(2,1)S(1)}, bf16[512,512]{1,0:T(8,128)(2,1)}, u32[]{:S(2)}) %copy-start.10) | copy-done | bytes 524312
  41.7 0.9 %copy-done.11 = bf16[128,512]{1,0:T(8,128)(2,1)S(1)} copy-done((bf16[128,512]{1,0:T(8,128)(2,1)S(1)}, bf16[128,512]{1,0:T(8,128)(2,1)}, u32[]{:S(2)}) %copy-start.11) | copy-done | bytes 131096
  42.6 0.9 %copy-done.12 = bf16[512,128]{1,0:T(8,128)(2,1)S(1)} copy-done((bf16[512,128]{1,0:T(8,128)(2,1)S(1)}, bf16[512,128]{1,0:T(8,128)(2,1)}, u32[]{:S(2)}) %copy-start.12) | copy-done | bytes 131096
  43.5 0.9 %copy-done.13 = bf16[128,512]{1,0:T(8,128)(2,1)S(1)} copy-done((bf16[128,512]{1,0:T(8,128)(2,1)S(1)}, bf16[128,512]{1,0:T(8,128)(2,1)}, u32[]{:S(2)}) %copy-start.13) | copy-done | bytes 131096
  44.4 0.9 %copy-done.14 = bf16[512,128]{1,0:T(8,128)(2,1)S(1)} copy-done((bf16[512,128]{1,0:T(8,128)(2,1)S(1)}, bf16[512,128]{1,0:T(8,128)(2,1)}, u32[]{:S(2)}) %copy-start.14) | copy-done | bytes 131096
  45.3 0.7 copy-done.18
  46.0 0.7 copy-done.19
  46.7 0.7 copy-done.20
  47.3 0.7 copy-done.21
  48.0 7.7 %network.1 = (bf16[768,512]{1,0:T(8,128)(2,1)S(1)}, bf16[128,128]{1,0:T(8,128)(2,1)S(1)}) custom-call(s32[24,32]{1,0:T(8,128)S(1)} %copy-done.6, bf16[768,512]{1,0:T(8,128)(2,1)S(1)} %get-tuple-element.29.col_ref.colbf_ref, bf16[128,128]{1,0:T(8,128)(2,1)S(1)} %get-tuple-element.30.ghost_ref, f32[272,128]{1,0:T(8,128)S(1)} %collective-permute-done.refs_2_.refs_3_.prev_ref, ...), custom_call_target="tpu_custom_call" | custom-call | flops 6442450944 | bytes 4000000 | tf_op jit(solution)/shard_map/network/pallas_call | solution.py:834
  55.7 0.1 rims.1
  55.8 0.3 collective-permute-start.4
  56.1 2.4 %collective-permute-start.5 = (f32[128,128]{1,0:T(8,128)S(1)}, f32[128,128]{1,0:T(8,128)S(1)}, u32[]{:S(2)}, u32[]{:S(2)}) collective-permute-start(f32[128,128]{1,0:T(8,128)S(1)} %get-tuple-element.33.ylo_ref), channel_id=1, source_target_pairs={{0,7},{1,0},{2,1},{3,2},{4,3},{5,4},{6,5},{7,6},{8,15},{9,8},{10,9... | collective-permute-start | bytes 196616 | tf_op jit(solution)/shard_map/ppermute | solution.py:870
  58.5 3.0 %collective-permute-done.4.yprev_ref = f32[128,128]{1,0:T(8,128)S(1)} collective-permute-done((f32[128,128]{1,0:T(8,128)S(1)}, f32[128,128]{1,0:T(8,128)S(1)}, u32[]{:S(2)}, u32[]{:S(2)}) %collective-permute-start.4) | collective-permute-done | bytes 65568 | tf_op jit(solution)/shard_map/ppermute | solution.py:869
  61.5 6.6 %final.1 = f32[2,64,96,128]{3,2,1,0:T(8,128)} custom-call(f32[96,2,64,128]{3,2,1,0:T(8,128)S(1)} %bitcast.10, bf16[768,512]{1,0:T(8,128)(2,1)S(1)} %get-tuple-element.31.inc_ref, bf16[128,128]{1,0:T(8,128)(2,1)S(1)} %get-tuple-element.32.near_ref, f32[24,32]{1,0:T(8,128)S(1)} %copy-done.1, f32[272,128]{1,0:T(8,128)S(1)} %collective-permute-done.refs_2_.refs_3_.prev_ref, ...), custom_call_target="tpu_custom_call" | custom-call | flops 1000000000 | bytes 14000000 | tf_op jit(solution)/shard_map/final/pallas_call | solution.py:872
  68.2 8.8 %all-to-all-done = bf16[32,48,512]{2,1,0:T(8,128)(2,1)S(1)} async-done(((bf16[32,48,512]{2,1,0:T(8,128)(2,1)}), bf16[32,48,512]{2,1,0:T(8,128)(2,1)S(1)}, u32[]{:S(2)}, u32[]{:S(2)}) %all-to-all-start) | async-done | bytes 1572896 | tf_op jit(solution)/shard_map/all_to_all | solution.py:829
  77.0 2.4 %arrange.1 = bf16[3072,128]{1,0:T(8,128)(2,1)} custom-call(bf16[1536,512]{1,0:T(8,128)(2,1)S(1)} %bitcast.11), custom_call_target="tpu_custom_call" | custom-call | flops 1000000 | bytes 3000000 | tf_op jit(solution)/shard_map/arrange/pallas_call | solution.py:907
  (41 shorter events, 0.1 us)
Async XLA Ops:
  3.5 19.1 %collective-permute-start = (f32[272,128]{1,0:T(8,128)}, f32[272,128]{1,0:T(8,128)S(1)}, u32[]{:S(2)}, u32[]{:S(2)}) collective-permute-start(f32[272,128]{1,0:T(8,128)} %get-tuple-element.24.refs_2_), channel_id=1, source_target_pairs={{0,8},{8,16},{16,24},{24,0},{1,9},{9,17},{17,25},{25,1},{2,10},{10... | collective-permute-start | bytes 417800 | tf_op jit(solution)/shard_map/ppermute | solution.py:778
  6.5 20.5 %copy-start.7 = (s32[24,32]{1,0:T(8,128)S(1)}, s32[24,32]{1,0:T(8,128)}, u32[]{:S(2)}) copy-start(s32[24,32]{1,0:T(8,128)} %refs_1_.1) | copy-start | bytes 9220
  6.5 16.1 %collective-permute-start.1 = (f32[272,128]{1,0:T(8,128)}, f32[272,128]{1,0:T(8,128)S(1)}, u32[]{:S(2)}, u32[]{:S(2)}) collective-permute-start(f32[272,128]{1,0:T(8,128)} %get-tuple-element.23.refs_1_), channel_id=1, source_target_pairs={{0,24},{8,0},{16,8},{24,16},{1,25},{9,1},{17,9},{25,17},{2,26},{10... | collective-permute-start | bytes 417800 | tf_op jit(solution)/shard_map/ppermute | solution.py:779
  22.6 0.8 %copy-start.4 = (f32[128,128]{1,0:T(8,128)S(1)}, f32[128,128]{1,0:T(8,128)}, u32[]{:S(2)}) copy-start(f32[128,128]{1,0:T(8,128)} %get-tuple-element.25.refs_0_) | copy-start | bytes 196612
  23.5 0.8 %copy-start.5 = (f32[128,128]{1,0:T(8,128)S(1)}, f32[128,128]{1,0:T(8,128)}, u32[]{:S(2)}) copy-start(f32[128,128]{1,0:T(8,128)} %get-tuple-element.26.refs_1_) | copy-start | bytes 196612
  24.3 8.3 %collective-permute-start.2 = (f32[128,128]{1,0:T(8,128)S(1)}, f32[128,128]{1,0:T(8,128)S(1)}, u32[]{:S(2)}, u32[]{:S(2)}) collective-permute-start(f32[128,128]{1,0:T(8,128)S(1)} %get-tuple-element.28.refs_6_), channel_id=1, source_target_pairs={{0,1},{1,2},{2,3},{3,4},{4,5},{5,6},{6,7},{7,0},{8,9},{9,10},{10,1... | collective-permute-start | bytes 196616 | tf_op jit(solution)/shard_map/ppermute | solution.py:788
  24.4 8.3 %collective-permute-start.3 = (f32[128,128]{1,0:T(8,128)S(1)}, f32[128,128]{1,0:T(8,128)S(1)}, u32[]{:S(2)}, u32[]{:S(2)}) collective-permute-start(f32[128,128]{1,0:T(8,128)S(1)} %get-tuple-element.27.refs_5_), channel_id=1, source_target_pairs={{0,7},{1,0},{2,1},{3,2},{4,3},{5,4},{6,5},{7,6},{8,15},{9,8},{10,9... | collective-permute-start | bytes 196616 | tf_op jit(solution)/shard_map/ppermute | solution.py:789
  27.0 2.8 %copy-start = (f32[96,2,64,128]{3,2,1,0:T(8,128)S(1)}, f32[96,2,64,128]{3,2,1,0:T(8,128)}, u32[]{:S(2)}) copy-start(f32[96,2,64,128]{3,2,1,0:T(8,128)} %get-tuple-element.21.refs_0_.adv_ref) | copy-start | bytes 18874372
  29.8 2.8 %copy-start.2 = (f32[272,128]{1,0:T(8,128)S(1)}, f32[272,128]{1,0:T(8,128)}, u32[]{:S(2)}) copy-start(f32[272,128]{1,0:T(8,128)} %get-tuple-element.23.refs_1_) | copy-start | bytes 417796
  29.8 2.9 %copy-start.3 = (f32[272,128]{1,0:T(8,128)S(1)}, f32[272,128]{1,0:T(8,128)}, u32[]{:S(2)}) copy-start(f32[272,128]{1,0:T(8,128)} %get-tuple-element.24.refs_2_) | copy-start | bytes 417796
  35.9 3.4 %copy-start.6 = (s32[24,32]{1,0:T(8,128)S(1)}, s32[24,32]{1,0:T(8,128)}, u32[]{:S(2)}) copy-start(s32[24,32]{1,0:T(8,128)} %lit_ref.3) | copy-start | bytes 9220
  35.9 3.4 %copy-start.8 = (bf16[512,512]{1,0:T(8,128)(2,1)S(1)}, bf16[512,512]{1,0:T(8,128)(2,1)}, u32[]{:S(2)}) copy-start(bf16[512,512]{1,0:T(8,128)(2,1)} %w2.1) | copy-start | bytes 1572868
  35.9 3.4 %copy-start.15 = (f32[512]{0:T(512)S(1)}, f32[512]{0:T(512)}, u32[]{:S(2)}) copy-start(f32[512]{0:T(512)} %param.27) | copy-start | bytes 6148
  35.9 3.4 %copy-start.16 = (f32[512]{0:T(512)S(1)}, f32[512]{0:T(512)}, u32[]{:S(2)}) copy-start(f32[512]{0:T(512)} %param.29) | copy-start | bytes 6148
  35.9 3.4 %copy-start.17 = (f32[512]{0:T(512)S(1)}, f32[512]{0:T(512)}, u32[]{:S(2)}) copy-start(f32[512]{0:T(512)} %param.31) | copy-start | bytes 6148
  35.9 41.1 %all-to-all-start = ((bf16[32,48,512]{2,1,0:T(8,128)(2,1)}), bf16[32,48,512]{2,1,0:T(8,128)(2,1)S(1)}, u32[]{:S(2)}, u32[]{:S(2)}) async-start(bf16[32,48,512]{2,1,0:T(8,128)(2,1)} %bitcast.7), calls=%async_computation | async-start | bytes 3145728 | tf_op jit(solution)/shard_map/all_to_all | solution.py:829
  39.2 22.3 %slice-start = ((s8[6291456]{0:T(1024)(128)(4,1)}), s8[4194304]{0:T(1024)(128)(4,1)S(1)}, s32[]{:S(2)}) async-start(s8[6291456]{0:T(1024)(128)(4,1)} %bitcast.9), calls=%async_computation.1 | async-start | bytes 8388608
  39.3 1.2 %copy-start.9 = (bf16[512,512]{1,0:T(8,128)(2,1)S(1)}, bf16[512,512]{1,0:T(8,128)(2,1)}, u32[]{:S(2)}) copy-start(bf16[512,512]{1,0:T(8,128)(2,1)} %w3.1) | copy-start | bytes 1572868
  40.5 1.2 %copy-start.10 = (bf16[512,512]{1,0:T(8,128)(2,1)S(1)}, bf16[512,512]{1,0:T(8,128)(2,1)}, u32[]{:S(2)}) copy-start(bf16[512,512]{1,0:T(8,128)(2,1)} %s2_.1) | copy-start | bytes 1572868
  41.7 0.9 %copy-start.11 = (bf16[128,512]{1,0:T(8,128)(2,1)S(1)}, bf16[128,512]{1,0:T(8,128)(2,1)}, u32[]{:S(2)}) copy-start(bf16[128,512]{1,0:T(8,128)(2,1)} %w1.1) | copy-start | bytes 393220
  42.6 0.9 %copy-start.12 = (bf16[512,128]{1,0:T(8,128)(2,1)S(1)}, bf16[512,128]{1,0:T(8,128)(2,1)}, u32[]{:S(2)}) copy-start(bf16[512,128]{1,0:T(8,128)(2,1)} %w4.1) | copy-start | bytes 393220
  43.5 0.9 %copy-start.13 = (bf16[128,512]{1,0:T(8,128)(2,1)S(1)}, bf16[128,512]{1,0:T(8,128)(2,1)}, u32[]{:S(2)}) copy-start(bf16[128,512]{1,0:T(8,128)(2,1)} %s1_.1) | copy-start | bytes 393220
  44.4 0.9 %copy-start.14 = (bf16[512,128]{1,0:T(8,128)(2,1)S(1)}, bf16[512,128]{1,0:T(8,128)(2,1)}, u32[]{:S(2)}) copy-start(bf16[512,128]{1,0:T(8,128)(2,1)} %s3.1) | copy-start | bytes 393220
  45.3 0.7 copy-start.18
  46.0 0.7 copy-start.19
  46.7 0.7 copy-start.20
  47.3 0.7 copy-start.21
  48.0 7.7 %copy-start.1 = (f32[24,32]{1,0:T(8,128)S(1)}, f32[24,32]{1,0:T(8,128)}, u32[]{:S(2)}) copy-start(f32[24,32]{1,0:T(8,128)} %jac_ref.7) | copy-start | bytes 9220
  48.0 13.5 %slice-start.1 = ((s8[6291456]{0:T(1024)(128)(4,1)}), s8[2097152]{0:T(1024)(128)(4,1)S(1)}, s32[]{:S(2)}) async-start(s8[6291456]{0:T(1024)(128)(4,1)} %bitcast.9), calls=%async_computation.2 | async-start | bytes 4194304
  55.8 5.7 %collective-permute-start.4 = (f32[128,128]{1,0:T(8,128)S(1)}, f32[128,128]{1,0:T(8,128)S(1)}, u32[]{:S(2)}, u32[]{:S(2)}) collective-permute-start(f32[128,128]{1,0:T(8,128)S(1)} %get-tuple-element.34.yhi_ref), channel_id=1, source_target_pairs={{0,1},{1,2},{2,3},{3,4},{4,5},{5,6},{6,7},{7,0},{8,9},{9,10},{10,1... | collective-permute-start | bytes 196616 | tf_op jit(solution)/shard_map/ppermute | solution.py:869
  56.1 5.4 %collective-permute-start.5 = (f32[128,128]{1,0:T(8,128)S(1)}, f32[128,128]{1,0:T(8,128)S(1)}, u32[]{:S(2)}, u32[]{:S(2)}) collective-permute-start(f32[128,128]{1,0:T(8,128)S(1)} %get-tuple-element.33.ylo_ref), channel_id=1, source_target_pairs={{0,7},{1,0},{2,1},{3,2},{4,3},{5,4},{6,5},{7,6},{8,15},{9,8},{10,9... | collective-permute-start | bytes 196616 | tf_op jit(solution)/shard_map/ppermute | solution.py:870

commit v2 on v1

--- a/solution.py
+++ b/solution.py
@@ -143,120 +143,137 @@
 
 
 def dynamics_kernel(
-    prog_ref, vel_ref, jac_ref, dcat_ref, adv_ref, ylo_ref, yhi_ref,
-    sy3_ref, vf3_ref, pf3_ref, scale_ref, inside_ref, shared_ref, zlo_ref, zhi_ref,
+    prog_hbm, vel_hbm, jac_ref, dcat_ref, adv_ref, ylo_ref, yhi_ref, prog_ref, vel_ref,
+    sy3_ref, vf3_ref, pf3_ref, scale_ref, inside_ref, shared_ref, zlo_ref, zhi_ref, sems,
 ):
-    step = pl.program_id(0)
-    _, tile, width_x, width = prog_ref.shape
+    _, levels, width_x, width = prog_ref.shape
+    tile = sy3_ref.shape[0] // 2
+    steps = levels // tile
     elements_x, elements_y = jac_ref.shape
     features = zlo_ref.shape[0]
-    levels = features // 2
     planes = 2 * tile
     pitch = sy3_ref.shape[1]
     sy_ref = sy3_ref.reshape(planes * pitch, width)
     vf_ref = vf3_ref.reshape(planes * pitch, width)
     pf_ref = pf3_ref.reshape(planes * pitch, width)
 
-    @pl.when(step == 0)
-    def _():
-        mass = along_lanes(jac_ref[...], width)
-        scale_ref[...] = -TIME_STEP * jnp.sqrt(mass)
-        inside, shared = inner_reciprocals(mass + copies_along_y(mass))
-        inside_ref[...] = inside
-        shared_ref[...] = shared
-
-    vf3_ref[:, 0:width_x, :] = vel_ref[...].astype(F32).reshape(planes, width_x, width)
-    piece = planes // 4
-    for at in range(4):
-        first = at * piece
-        values = prog_ref[first // tile, first % tile : first % tile + piece]
-        pf3_ref[first : first + piece, 0:width_x, :] = values
-        high, low = split(values.reshape(piece * width_x, width))
-        sy3_ref[first : first + piece, 0:width_x, :] = jnp.dot(
-            jnp.concatenate([high, low, high], axis=1), dcat_ref[...], preferred_element_type=F32
-        ).reshape(piece, width_x, width)
-
-    lane = iota((tile, width), 1)
-
-    def rims(lines):
-        first, second, third = lines
-        a = pltpu.roll(first, 1, 1)
-        b = pltpu.roll(second, 2, 1)
-        c = pltpu.roll(third, 3, 1)
-
-        def pick(base):
-            return jnp.where(
-                lane == base, first,
-                jnp.where(
-                    lane == (base + 1) % width, a,
+    def copies(step):
+        at = pl.ds(step * tile, tile)
+        return (
+            pltpu.make_async_copy(prog_hbm.at[:, at], prog_ref.at[:, at], sems.at[0, step]),
+            pltpu.make_async_copy(vel_hbm.at[:, at], vel_ref.at[:, at], sems.at[1, step]),
+        )
+
+    for step in range(steps):
+        for copy in copies(step):
+            copy.start()
+
+    mass = along_lanes(jac_ref[...], width)
+    scale_ref[...] = -TIME_STEP * jnp.sqrt(mass)
+    inside, shared = inner_reciprocals(mass + copies_along_y(mass))
+    inside_ref[...] = inside
+    shared_ref[...] = shared
+
+    def one_tile(step):
+        level = pl.ds(pl.multiple_of(step * tile, tile), tile)
+        vf3_ref[:, 0:width_x, :] = vel_ref[:, pl.ds(step * tile, tile)].astype(F32).reshape(
+            planes, width_x, width
+        )
+        piece = planes // 4
+        for at in range(4):
+            first = at * piece
+            values = prog_ref[first // tile, pl.ds(step * tile + first % tile, piece)]
+            pf3_ref[first : first + piece, 0:width_x, :] = values
+            high, low = split(values.reshape(piece * width_x, width))
+            sy3_ref[first : first + piece, 0:width_x, :] = jnp.dot(
+                jnp.concatenate([high, low, high], axis=1), dcat_ref[...], preferred_element_type=F32
+            ).reshape(piece, width_x, width)
+
+        lane = iota((tile, width), 1)
+
+        def rims(lines):
+            first, second, third = lines
+            a = pltpu.roll(first, 1, 1)
+            b = pltpu.roll(second, 2, 1)
+            c = pltpu.roll(third, 3, 1)
+
+            def pick(base):
+                return jnp.where(
+                    lane == base, first,
                     jnp.where(
-                        lane == (base + 2) % width, b, jnp.where(lane == (base + 3) % width, c, 0.0)
+                        lane == (base + 1) % width, a,
+                        jnp.where(
+                            lane == (base + 2) % width, b, jnp.where(lane == (base + 3) % width, c, 0.0)
+                        ),
                     ),
-                ),
+                )
+
+            return pick(0), pick(width - 1)
+
+        def element(p, carry):
+            scale = scale_ref[p : p + 1, :]
+            inside = inside_ref[p : p + 1, :]
+            shared = shared_ref[p : p + 1, :]
+            shift = (4 * p + width - 1) % width
+            vx = [vf_ref[pl.ds(4 * p + k, tile, stride=pitch), :] for k in range(4)]
+            vy = [
+                vf_ref[pl.ds(tile * pitch + 4 * p + k, tile, stride=pitch), :] for k in range(4)
+            ]
+            out = []
+            for v in range(2):
+                last_e, last_f, z_low, z_high = carry[4 * v : 4 * v + 4]
+                base = v * tile * pitch + 4 * p
+                f = [pf_ref[pl.ds(base + k, tile, stride=pitch), :] for k in range(4)]
+                sy = [sy_ref[pl.ds(base + k, tile, stride=pitch), :] for k in range(4)]
+                sx = element_slopes(f)
+                e = []
+                for k in range(4):
+                    moved = (vx[k] * sx[k] + vy[k] * sy[k]) * scale
+                    e.append(moved + copies_along_y(moved))
+                joined = last_e + e[0]
+                gain = joined * shared
+                adv_ref[4 * p, v, level, :] = f[0] + gain
+                adv_ref[4 * p + 1, v, level, :] = f[1] + e[1] * inside
+                adv_ref[4 * p + 2, v, level, :] = f[2] + e[2] * inside
+
+                if p > 0:
+                    adv_ref[4 * p - 1, v, level, :] = last_f + gain
+
+                low, high = rims((joined, e[1], e[2]))
+                out += [
+                    e[3], f[3],
+                    z_low + pltpu.roll(low, shift, 1), z_high + pltpu.roll(high, shift, 1),
+                ]
+            return tuple(out)
+
+        zero = jnp.zeros((tile, width), F32)
+        final = (zero,) * 8
+        for p in range(elements_x):
+            final = element(p, final)
+        for v in range(2):
+            last_e, last_f, z_low, z_high = final[4 * v : 4 * v + 4]
+            at = pl.ds(pl.multiple_of(v * levels + tile * step, tile), tile)
+            adv_ref[width_x - 1, v, level, :] = last_f
+            zlo_ref[at, :] = jnp.where(
+                lane == width_x - 1, pltpu.roll(last_e, width_x - 1, 1), z_low
             )
-
-        return pick(0), pick(width - 1)
-
-    def element(p, carry):
-        scale = scale_ref[p : p + 1, :]
-        inside = inside_ref[p : p + 1, :]
-        shared = shared_ref[p : p + 1, :]
-        shift = (4 * p + width - 1) % width
-        vx = [vf_ref[pl.ds(4 * p + k, tile, stride=pitch), :] for k in range(4)]
-        vy = [
-            vf_ref[pl.ds(tile * pitch + 4 * p + k, tile, stride=pitch), :] for k in range(4)
-        ]
-        out = []
-        for v in range(2):
-            last_e, last_f, z_low, z_high = carry[4 * v : 4 * v + 4]
-            base = v * tile * pitch + 4 * p
-            f = [pf_ref[pl.ds(base + k, tile, stride=pitch), :] for k in range(4)]
-            sy = [sy_ref[pl.ds(base + k, tile, stride=pitch), :] for k in range(4)]
-            sx = element_slopes(f)
-            e = []
-            for k in range(4):
-                moved = (vx[k] * sx[k] + vy[k] * sy[k]) * scale
-                e.append(moved + copies_along_y(moved))
-            joined = last_e + e[0]
-            gain = joined * shared
-            adv_ref[4 * p, v] = f[0] + gain
-            adv_ref[4 * p + 1, v] = f[1] + e[1] * inside
-            adv_ref[4 * p + 2, v] = f[2] + e[2] * inside
-
-            if p > 0:
-                adv_ref[4 * p - 1, v] = last_f + gain
-
-            low, high = rims((joined, e[1], e[2]))
-            out += [
-                e[3], f[3],
-                z_low + pltpu.roll(low, shift, 1), z_high + pltpu.roll(high, shift, 1),
-            ]
-        return tuple(out)
-
-    zero = jnp.zeros((tile, width), F32)
-    final = (zero,) * 8
-    for p in range(elements_x):
-        final = element(p, final)
-    for v in range(2):
-        last_e, last_f, z_low, z_high = final[4 * v : 4 * v + 4]
-        at = pl.ds(pl.multiple_of(v * levels + tile * step, tile), tile)
-        adv_ref[width_x - 1, v] = last_f
-        zlo_ref[at, :] = jnp.where(
-            lane == width_x - 1, pltpu.roll(last_e, width_x - 1, 1), z_low
-        )
-        zhi_ref[at, :] = pltpu.roll(
-            jnp.where(lane == width_x - 2, pltpu.roll(last_e, width_x - 1, 1), z_high), 1, 1
-        )
-
-    @pl.when(step == pl.num_programs(0) - 1)
-    def _():
-        jac = jac_ref[...]
-        ylo_ref[...] = zlo_ref[...].T
-        yhi_ref[...] = zhi_ref[...].T
-        for ref, q in ((ylo_ref, 0), (yhi_ref, elements_y - 1)):
-            ref[width_x : width_x + elements_x, :] = jnp.broadcast_to(
-                jac[:, q : q + 1], (elements_x, features)
+            zhi_ref[at, :] = pltpu.roll(
+                jnp.where(lane == width_x - 2, pltpu.roll(last_e, width_x - 1, 1), z_high), 1, 1
             )
+
+    @pl.loop(0, steps)
+    def _(step):
+        for copy in copies(step):
+            copy.wait()
+        one_tile(step)
+
+    jac = jac_ref[...]
+    ylo_ref[...] = zlo_ref[...].T
+    yhi_ref[...] = zhi_ref[...].T
+    for ref, q in ((ylo_ref, 0), (yhi_ref, elements_y - 1)):
+        ref[width_x : width_x + elements_x, :] = jnp.broadcast_to(
+            jac[:, q : q + 1], (elements_x, features)
+        )
 
 
 def cells_kernel(capacity, devices, adv_ref, span_ref, col_ref, slot_ref):
@@ -697,26 +714,20 @@
     features = fields * levels
     tile = 8
     dcat = jnp.asarray(y_derivative_operand(width))
+    hbm = pl.BlockSpec(memory_space=pltpu.HBM)
+    vmem = pl.BlockSpec(memory_space=pltpu.VMEM)
     return pl.pallas_call(
         dynamics_kernel,
-        grid=(levels // tile,),
-        in_specs=[
-            pl.BlockSpec((2, tile, width_x, width), lambda t: (0, t, 0, 0)),
-            pl.BlockSpec((2, tile, width_x, width), lambda t: (0, t, 0, 0)),
-            whole((elements_x, elements_y)),
-            whole((3 * width, width)),
-        ],
-        out_specs=[
-            pl.BlockSpec((width_x, 2, tile, width), lambda t: (0, 0, t, 0)),
-            whole((width, features)),
-            whole((width, features)),
-        ],
+        in_specs=[hbm, hbm, vmem, vmem],
+        out_specs=[vmem] * 3,
         out_shape=[
             shape_of((width_x, fields, levels, width)),
             shape_of((width, features)),
             shape_of((width, features)),
         ],
         scratch_shapes=[
+            pltpu.VMEM(prognostic.shape, F32),
+            pltpu.VMEM(velocity.shape, BF16),
             pltpu.VMEM((2 * tile, width_x + 8, width), F32),
             pltpu.VMEM((2 * tile, width_x + 8, width), F32),
             pltpu.VMEM((2 * tile, width_x + 8, width), F32),
@@ -725,8 +736,9 @@
             pltpu.VMEM((elements_x, width), F32),
             pltpu.VMEM((features, width), F32),
             pltpu.VMEM((features, width), F32),
-        ],
-        compiler_params=params(58),
+            pltpu.SemaphoreType.DMA((2, levels // tile)),
+        ],
+        compiler_params=params(42),
         cost_estimate=cost(2_000_000_000, 16_000_000),
         name="dynamics",
     )(prognostic, velocity, jacobian, dcat)

time: 80.1 us -> 74 us (0.924)
  waiting for transfers between devices: 11.9 us -> 5.69 us
  Pallas kernels: 39.6 us -> 42.2 us
  local copies, waits for them, and re-layouts: 13.2 us -> 10.8 us
    all_to_all x1, waiting for transfers between devices: 8.83 us -> 3.73 us  [on_device(): lax.all_to_all(outgoing.reshape(devices, capacity, 4 * features), ('face'...]
    pallas_call x1, Pallas kernels: 7.67 us -> 11.8 us  [on_device(): pl.pallas_call(network_kernel, grid=(3,), in_specs=[smem, pl.BlockSpec((c...]
    unnamed x48, local copies, waits for them, and re-layouts: 13.2 us -> 10.8 us
    pallas_call x1, Pallas kernels: 14 us -> 12.3 us  [dynamics_call(): pl.pallas_call(dynamics_kernel, in_specs=[hbm, hbm, vmem, vmem], out_spec...]
    ppermute x1, waiting for transfers between devices: 3.02 us -> 1.94 us  [on_device(): yprev2 = lax.ppermute(yhi2, 'dom', shifted('dom', 1))]
  transfers between devices with their start and end apart: 7 -> 7, of which waited for: 2 -> 2; matrix products, arithmetic and copies ran while one was open for 0% -> 0% of each run, Pallas kernels for 39% -> 46%
where the time goes in v2:
time: 74 us; the launch traced here: 73.6 us
  Pallas kernels  42.2 us (57%)
  starting transfers between devices  14 us (19%)
  local copies, waits for them, and re-layouts  10.8 us (15%)
  waiting for transfers between devices  5.69 us (8%)
  between operations  0.85 us (1%)
    pallas_call x1, Pallas kernels, dynamics_call(): pl.pallas_call(dynamics_kernel, in_specs=[hbm, hbm, vmem, vmem], out_spec...  12.3 us
    pallas_call x1, Pallas kernels, on_device(): pl.pallas_call(network_kernel, grid=(3,), in_specs=[smem, pl.BlockSpec((c...  11.8 us
    unnamed x48, local copies, waits for them, and re-layouts  10.8 us
    pallas_call x1, Pallas kernels, on_device(): pl.pallas_call(final_kernel, grid=(elements_x // group,), in_specs=[pl.Bl...  6.64 us
    all_to_all x1, waiting for transfers between devices, on_device(): lax.all_to_all(outgoing.reshape(devices, capacity, 4 * features), ('face'...  3.73 us
    all_to_all x1, starting transfers between devices, on_device(): lax.all_to_all(outgoing.reshape(devices, capacity, 4 * features), ('face'...  3.54 us
    pallas_call x1, Pallas kernels, edges_call(): pl.pallas_call(edges_kernel, grid=(1,), in_specs=[pl.BlockSpec(memory_spa...  3.03 us
    ppermute x1, starting transfers between devices, on_device(): prev = lax.ppermute(xhi, 'face', shifted('face', 1))  3.02 us
  transfers between devices with their start and end apart: 7, of which 2 were waited for; matrix products, arithmetic and copies ran while one was open for 0% of the time, Pallas kernels for 46%

profile of v2, /device:TPU:0, one launch (start us, length us, event | category | flops | bytes accessed | tf_op | source)
XLA Modules:
  0.0 73.6 jit_solution(15265657573652635643)
XLA Ops:
  0.6 0.0 copy-start.2
  0.7 3.0 %edges.1 = (f32[272,128]{1,0:T(8,128)}, f32[272,128]{1,0:T(8,128)}) custom-call(s32[24,32]{1,0:T(8,128)} %lit_ref.3, f32[2,64,96,128]{3,2,1,0:T(8,128)} %proghi_ref.1, f32[2,64,96,128]{3,2,1,0:T(8,128)} %proghi_ref.1, bf16[2,64,96,128]{3,2,1,0:T(8,128)(2,1)} %velhi_ref.1, bf16[2,64,96,128]{3,2,1,0:T(8,128)(2,1)} %velhi_ref.1, f32[24,32]{1,0:T(8,128)} %jac_ref.7, ...), custom_call_target="tpu_custom_call" | custom-call | flops 50000000 | bytes 2000000 | tf_op jit(solution)/shard_map/edges/pallas_call | solution.py:690
  3.7 3.0 %collective-permute-start = (f32[272,128]{1,0:T(8,128)}, f32[272,128]{1,0:T(8,128)S(1)}, u32[]{:S(2)}, u32[]{:S(2)}) collective-permute-start(f32[272,128]{1,0:T(8,128)} %get-tuple-element.24.refs_2_), channel_id=1, source_target_pairs={{0,8},{8,16},{16,24},{24,0},{1,9},{9,17},{17,25},{25,1},{2,10},{10... | collective-permute-start | bytes 417800 | tf_op jit(solution)/shard_map/ppermute | solution.py:790
  6.7 2.1 %collective-permute-start.1 = (f32[272,128]{1,0:T(8,128)}, f32[272,128]{1,0:T(8,128)S(1)}, u32[]{:S(2)}, u32[]{:S(2)}) collective-permute-start(f32[272,128]{1,0:T(8,128)} %get-tuple-element.23.refs_1_), channel_id=1, source_target_pairs={{0,24},{8,0},{16,8},{24,16},{1,25},{9,1},{17,9},{25,17},{2,26},{10... | collective-permute-start | bytes 417800 | tf_op jit(solution)/shard_map/ppermute | solution.py:791
  8.8 12.3 %dynamics.1 = (f32[96,2,64,128]{3,2,1,0:T(8,128)S(1)}, f32[128,128]{1,0:T(8,128)S(1)}, f32[128,128]{1,0:T(8,128)S(1)}) custom-call(f32[2,64,96,128]{3,2,1,0:T(8,128)} %proghi_ref.1, bf16[2,64,96,128]{3,2,1,0:T(8,128)(2,1)S(1)} %copy-done, f32[24,32]{1,0:T(8,128)S(1)} %copy-done.3, bf16[384,128]{1,0:T(8,128)(2,1)S(1)} %copy-done.2), custom_call_target="tpu_custom_call" | custom-call | flops 2000000000 | bytes 16000000 | tf_op jit(solution)/shard_map/dynamics/pallas_call | solution.py:719
  21.2 0.1 collective-permute-start.2
  21.2 2.6 %collective-permute-start.3 = (f32[128,128]{1,0:T(8,128)S(1)}, f32[128,128]{1,0:T(8,128)S(1)}, u32[]{:S(2)}, u32[]{:S(2)}) collective-permute-start(f32[128,128]{1,0:T(8,128)S(1)} %get-tuple-element.27.refs_5_), channel_id=1, source_target_pairs={{0,7},{1,0},{2,1},{3,2},{4,3},{5,4},{6,5},{7,6},{8,15},{9,8},{10,9... | collective-permute-start | bytes 196616 | tf_op jit(solution)/shard_map/ppermute | solution.py:801
  23.9 2.8 %cells.1 = (f32[4,768,128]{2,1,0:T(8,128)S(1)}, s32[1,768]{1,0:T(1,128)S(1)}) custom-call(f32[96,2,64,128]{3,2,1,0:T(8,128)S(1)} %get-tuple-element.21.refs_0_.adv_ref, s32[24,32]{1,0:T(8,128)S(1)} %copy-done.7), custom_call_target="tpu_custom_call" | custom-call | flops 1000000000 | bytes 8000000 | tf_op jit(solution)/shard_map/cells/pallas_call | solution.py:770
  26.7 0.5 complete.1
  27.3 2.7 %send.1 = bf16[1536,512]{1,0:T(8,128)(2,1)} custom-call(bf16[768,512]{1,0:T(8,128)(2,1)S(1)} %get-tuple-element.29.col_ref.colbf_ref, s32[1,768]{1,0:T(1,128)S(1)} %get-tuple-element.39.slot_ref), custom_call_target="tpu_custom_call" | custom-call | flops 2000000000 | bytes 3000000 | tf_op jit(solution)/shard_map/send/pallas_call | solution.py:831
  30.0 3.5 %all-to-all-start = ((bf16[32,48,512]{2,1,0:T(8,128)(2,1)}), bf16[32,48,512]{2,1,0:T(8,128)(2,1)S(1)}, u32[]{:S(2)}, u32[]{:S(2)}) async-start(bf16[32,48,512]{2,1,0:T(8,128)(2,1)} %bitcast.7), calls=%async_computation | async-start | bytes 3145728 | tf_op jit(solution)/shard_map/all_to_all | solution.py:841
  33.5 1.2 %copy-done.9 = bf16[512,512]{1,0:T(8,128)(2,1)S(1)} copy-done((bf16[512,512]{1,0:T(8,128)(2,1)S(1)}, bf16[512,512]{1,0:T(8,128)(2,1)}, u32[]{:S(2)}) %copy-start.9) | copy-done | bytes 524312
  34.7 1.2 %copy-done.10 = bf16[512,512]{1,0:T(8,128)(2,1)S(1)} copy-done((bf16[512,512]{1,0:T(8,128)(2,1)S(1)}, bf16[512,512]{1,0:T(8,128)(2,1)}, u32[]{:S(2)}) %copy-start.10) | copy-done | bytes 524312
  36.0 0.9 %copy-done.11 = bf16[128,512]{1,0:T(8,128)(2,1)S(1)} copy-done((bf16[128,512]{1,0:T(8,128)(2,1)S(1)}, bf16[128,512]{1,0:T(8,128)(2,1)}, u32[]{:S(2)}) %copy-start.11) | copy-done | bytes 131096
  36.9 0.9 %copy-done.12 = bf16[512,128]{1,0:T(8,128)(2,1)S(1)} copy-done((bf16[512,128]{1,0:T(8,128)(2,1)S(1)}, bf16[512,128]{1,0:T(8,128)(2,1)}, u32[]{:S(2)}) %copy-start.12) | copy-done | bytes 131096
  37.8 0.9 %copy-done.13 = bf16[128,512]{1,0:T(8,128)(2,1)S(1)} copy-done((bf16[128,512]{1,0:T(8,128)(2,1)S(1)}, bf16[128,512]{1,0:T(8,128)(2,1)}, u32[]{:S(2)}) %copy-start.13) | copy-done | bytes 131096
  38.7 0.9 %copy-done.14 = bf16[512,128]{1,0:T(8,128)(2,1)S(1)} copy-done((bf16[512,128]{1,0:T(8,128)(2,1)S(1)}, bf16[512,128]{1,0:T(8,128)(2,1)}, u32[]{:S(2)}) %copy-start.14) | copy-done | bytes 131096
  39.6 0.7 copy-done.15
  40.3 0.7 copy-done.16
  41.0 0.7 copy-done.17
  41.6 0.7 copy-done.18
  42.3 0.7 copy-done.19
  43.0 0.7 copy-done.20
  43.7 0.7 copy-done.21
  44.3 11.8 %network.1 = (bf16[768,512]{1,0:T(8,128)(2,1)S(1)}, bf16[128,128]{1,0:T(8,128)(2,1)S(1)}) custom-call(s32[24,32]{1,0:T(8,128)S(1)} %copy-done.6, bf16[768,512]{1,0:T(8,128)(2,1)S(1)} %get-tuple-element.29.col_ref.colbf_ref, bf16[128,128]{1,0:T(8,128)(2,1)S(1)} %get-tuple-element.30.ghost_ref, f32[272,128]{1,0:T(8,128)S(1)} %collective-permute-done.refs_2_.refs_3_.prev_ref, ...), custom_call_target="tpu_custom_call" | custom-call | flops 6442450944 | bytes 4000000 | tf_op jit(solution)/shard_map/network/pallas_call | solution.py:846
  56.1 0.1 rims.1
  56.2 0.3 collective-permute-start.4
  56.5 2.4 %collective-permute-start.5 = (f32[128,128]{1,0:T(8,128)S(1)}, f32[128,128]{1,0:T(8,128)S(1)}, u32[]{:S(2)}, u32[]{:S(2)}) collective-permute-start(f32[128,128]{1,0:T(8,128)S(1)} %get-tuple-element.33.ylo_ref), channel_id=1, source_target_pairs={{0,7},{1,0},{2,1},{3,2},{4,3},{5,4},{6,5},{7,6},{8,15},{9,8},{10,9... | collective-permute-start | bytes 196616 | tf_op jit(solution)/shard_map/ppermute | solution.py:882
  58.9 1.9 %collective-permute-done.4.yprev_ref = f32[128,128]{1,0:T(8,128)S(1)} collective-permute-done((f32[128,128]{1,0:T(8,128)S(1)}, f32[128,128]{1,0:T(8,128)S(1)}, u32[]{:S(2)}, u32[]{:S(2)}) %collective-permute-start.4) | collective-permute-done | bytes 65568 | tf_op jit(solution)/shard_map/ppermute | solution.py:881
  60.9 6.6 %final.1 = f32[2,64,96,128]{3,2,1,0:T(8,128)} custom-call(f32[96,2,64,128]{3,2,1,0:T(8,128)S(1)} %bitcast.10, bf16[768,512]{1,0:T(8,128)(2,1)S(1)} %get-tuple-element.31.inc_ref, bf16[128,128]{1,0:T(8,128)(2,1)S(1)} %get-tuple-element.32.near_ref, f32[24,32]{1,0:T(8,128)S(1)} %copy-done.3, f32[272,128]{1,0:T(8,128)S(1)} %collective-permute-done.refs_2_.refs_3_.prev_ref, ...), custom_call_target="tpu_custom_call" | custom-call | flops 1000000000 | bytes 14000000 | tf_op jit(solution)/shard_map/final/pallas_call | solution.py:884
  67.5 3.7 %all-to-all-done = bf16[32,48,512]{2,1,0:T(8,128)(2,1)S(1)} async-done(((bf16[32,48,512]{2,1,0:T(8,128)(2,1)}), bf16[32,48,512]{2,1,0:T(8,128)(2,1)S(1)}, u32[]{:S(2)}, u32[]{:S(2)}) %all-to-all-start) | async-done | bytes 1572896 | tf_op jit(solution)/shard_map/all_to_all | solution.py:841
  71.2 2.4 %arrange.1 = bf16[3072,128]{1,0:T(8,128)(2,1)} custom-call(bf16[1536,512]{1,0:T(8,128)(2,1)S(1)} %bitcast.11), custom_call_target="tpu_custom_call" | custom-call | flops 1000000 | bytes 3000000 | tf_op jit(solution)/shard_map/arrange/pallas_call | solution.py:919
  (41 shorter events, 0.1 us)
Async XLA Ops:
  0.6 8.2 %copy-start.2 = (bf16[384,128]{1,0:T(8,128)(2,1)S(1)}, bf16[384,128]{1,0:T(8,128)(2,1)}, u32[]{:S(2)}) copy-start(bf16[384,128]{1,0:T(8,128)(2,1)} %constant.2.clone.dcat_ref) | copy-start | bytes 294916
  0.6 8.2 %copy-start = (bf16[2,64,96,128]{3,2,1,0:T(8,128)(2,1)S(1)}, bf16[2,64,96,128]{3,2,1,0:T(8,128)(2,1)}, u32[]{:S(2)}) copy-start(bf16[2,64,96,128]{3,2,1,0:T(8,128)(2,1)} %velhi_ref.1) | copy-start | bytes 9437188
  0.7 8.2 %copy-start.3 = (f32[24,32]{1,0:T(8,128)S(1)}, f32[24,32]{1,0:T(8,128)}, u32[]{:S(2)}) copy-start(f32[24,32]{1,0:T(8,128)} %jac_ref.7) | copy-start | bytes 9220
  3.7 17.4 %collective-permute-start = (f32[272,128]{1,0:T(8,128)}, f32[272,128]{1,0:T(8,128)S(1)}, u32[]{:S(2)}, u32[]{:S(2)}) collective-permute-start(f32[272,128]{1,0:T(8,128)} %get-tuple-element.24.refs_2_), channel_id=1, source_target_pairs={{0,8},{8,16},{16,24},{24,0},{1,9},{9,17},{17,25},{25,1},{2,10},{10... | collective-permute-start | bytes 417800 | tf_op jit(solution)/shard_map/ppermute | solution.py:790
  6.7 17.1 %copy-start.7 = (s32[24,32]{1,0:T(8,128)S(1)}, s32[24,32]{1,0:T(8,128)}, u32[]{:S(2)}) copy-start(s32[24,32]{1,0:T(8,128)} %refs_1_.1) | copy-start | bytes 9220
  6.7 14.4 %collective-permute-start.1 = (f32[272,128]{1,0:T(8,128)}, f32[272,128]{1,0:T(8,128)S(1)}, u32[]{:S(2)}, u32[]{:S(2)}) collective-permute-start(f32[272,128]{1,0:T(8,128)} %get-tuple-element.23.refs_1_), channel_id=1, source_target_pairs={{0,24},{8,0},{16,8},{24,16},{1,25},{9,1},{17,9},{25,17},{2,26},{10... | collective-permute-start | bytes 417800 | tf_op jit(solution)/shard_map/ppermute | solution.py:791
  21.1 5.6 %copy-start.1 = (f32[96,2,64,128]{3,2,1,0:T(8,128)}, f32[96,2,64,128]{3,2,1,0:T(8,128)S(1)}, u32[]{:S(2)}) copy-start(f32[96,2,64,128]{3,2,1,0:T(8,128)S(1)} %get-tuple-element.21.refs_0_.adv_ref) | copy-start | bytes 18874372
  21.2 5.5 %collective-permute-start.2 = (f32[128,128]{1,0:T(8,128)S(1)}, f32[128,128]{1,0:T(8,128)S(1)}, u32[]{:S(2)}, u32[]{:S(2)}) collective-permute-start(f32[128,128]{1,0:T(8,128)S(1)} %get-tuple-element.28.refs_6_), channel_id=1, source_target_pairs={{0,1},{1,2},{2,3},{3,4},{4,5},{5,6},{6,7},{7,0},{8,9},{9,10},{10,1... | collective-permute-start | bytes 196616 | tf_op jit(solution)/shard_map/ppermute | solution.py:800
  21.2 5.5 %collective-permute-start.3 = (f32[128,128]{1,0:T(8,128)S(1)}, f32[128,128]{1,0:T(8,128)S(1)}, u32[]{:S(2)}, u32[]{:S(2)}) collective-permute-start(f32[128,128]{1,0:T(8,128)S(1)} %get-tuple-element.27.refs_5_), channel_id=1, source_target_pairs={{0,7},{1,0},{2,1},{3,2},{4,3},{5,4},{6,5},{7,6},{8,15},{9,8},{10,9... | collective-permute-start | bytes 196616 | tf_op jit(solution)/shard_map/ppermute | solution.py:801
  23.9 2.9 %copy-start.4 = (f32[272,128]{1,0:T(8,128)S(1)}, f32[272,128]{1,0:T(8,128)}, u32[]{:S(2)}) copy-start(f32[272,128]{1,0:T(8,128)} %get-tuple-element.23.refs_1_) | copy-start | bytes 417796
  23.9 2.9 %copy-start.5 = (f32[272,128]{1,0:T(8,128)S(1)}, f32[272,128]{1,0:T(8,128)}, u32[]{:S(2)}) copy-start(f32[272,128]{1,0:T(8,128)} %get-tuple-element.24.refs_2_) | copy-start | bytes 417796
  30.0 3.6 %copy-start.6 = (s32[24,32]{1,0:T(8,128)S(1)}, s32[24,32]{1,0:T(8,128)}, u32[]{:S(2)}) copy-start(s32[24,32]{1,0:T(8,128)} %lit_ref.3) | copy-start | bytes 9220
  30.0 3.6 %copy-start.8 = (bf16[512,512]{1,0:T(8,128)(2,1)S(1)}, bf16[512,512]{1,0:T(8,128)(2,1)}, u32[]{:S(2)}) copy-start(bf16[512,512]{1,0:T(8,128)(2,1)} %w2.1) | copy-start | bytes 1572868
  30.0 41.3 %all-to-all-start = ((bf16[32,48,512]{2,1,0:T(8,128)(2,1)}), bf16[32,48,512]{2,1,0:T(8,128)(2,1)S(1)}, u32[]{:S(2)}, u32[]{:S(2)}) async-start(bf16[32,48,512]{2,1,0:T(8,128)(2,1)} %bitcast.7), calls=%async_computation | async-start | bytes 3145728 | tf_op jit(solution)/shard_map/all_to_all | solution.py:841
  33.5 27.4 %slice-start = ((s8[6291456]{0:T(1024)(128)(4,1)}), s8[4194304]{0:T(1024)(128)(4,1)S(1)}, s32[]{:S(2)}) async-start(s8[6291456]{0:T(1024)(128)(4,1)} %bitcast.9), calls=%async_computation.1 | async-start | bytes 8388608
  33.5 1.2 %copy-start.9 = (bf16[512,512]{1,0:T(8,128)(2,1)S(1)}, bf16[512,512]{1,0:T(8,128)(2,1)}, u32[]{:S(2)}) copy-start(bf16[512,512]{1,0:T(8,128)(2,1)} %w3.1) | copy-start | bytes 1572868
  34.7 1.2 %copy-start.10 = (bf16[512,512]{1,0:T(8,128)(2,1)S(1)}, bf16[512,512]{1,0:T(8,128)(2,1)}, u32[]{:S(2)}) copy-start(bf16[512,512]{1,0:T(8,128)(2,1)} %s2_.1) | copy-start | bytes 1572868
  36.0 0.9 %copy-start.11 = (bf16[128,512]{1,0:T(8,128)(2,1)S(1)}, bf16[128,512]{1,0:T(8,128)(2,1)}, u32[]{:S(2)}) copy-start(bf16[128,512]{1,0:T(8,128)(2,1)} %w1.1) | copy-start | bytes 393220
  36.9 0.9 %copy-start.12 = (bf16[512,128]{1,0:T(8,128)(2,1)S(1)}, bf16[512,128]{1,0:T(8,128)(2,1)}, u32[]{:S(2)}) copy-start(bf16[512,128]{1,0:T(8,128)(2,1)} %w4.1) | copy-start | bytes 393220
  37.8 0.9 %copy-start.13 = (bf16[128,512]{1,0:T(8,128)(2,1)S(1)}, bf16[128,512]{1,0:T(8,128)(2,1)}, u32[]{:S(2)}) copy-start(bf16[128,512]{1,0:T(8,128)(2,1)} %s1_.1) | copy-start | bytes 393220
  38.7 0.9 %copy-start.14 = (bf16[512,128]{1,0:T(8,128)(2,1)S(1)}, bf16[512,128]{1,0:T(8,128)(2,1)}, u32[]{:S(2)}) copy-start(bf16[512,128]{1,0:T(8,128)(2,1)} %s3.1) | copy-start | bytes 393220
  39.6 0.7 copy-start.15
  40.3 0.7 copy-start.16
  41.0 0.7 copy-start.17
  41.6 0.7 copy-start.18
  42.3 0.7 copy-start.19
  43.0 0.7 copy-start.20
  43.7 0.7 copy-start.21
  44.3 16.6 %slice-start.1 = ((s8[6291456]{0:T(1024)(128)(4,1)}), s8[2097152]{0:T(1024)(128)(4,1)S(1)}, s32[]{:S(2)}) async-start(s8[6291456]{0:T(1024)(128)(4,1)} %bitcast.9), calls=%async_computation.2 | async-start | bytes 4194304
  56.2 4.6 %collective-permute-start.4 = (f32[128,128]{1,0:T(8,128)S(1)}, f32[128,128]{1,0:T(8,128)S(1)}, u32[]{:S(2)}, u32[]{:S(2)}) collective-permute-start(f32[128,128]{1,0:T(8,128)S(1)} %get-tuple-element.34.yhi_ref), channel_id=1, source_target_pairs={{0,1},{1,2},{2,3},{3,4},{4,5},{5,6},{6,7},{7,0},{8,9},{9,10},{10,1... | collective-permute-start | bytes 196616 | tf_op jit(solution)/shard_map/ppermute | solution.py:881
  56.5 4.3 %collective-permute-start.5 = (f32[128,128]{1,0:T(8,128)S(1)}, f32[128,128]{1,0:T(8,128)S(1)}, u32[]{:S(2)}, u32[]{:S(2)}) collective-permute-start(f32[128,128]{1,0:T(8,128)S(1)} %get-tuple-element.33.ylo_ref), channel_id=1, source_target_pairs={{0,7},{1,0},{2,1},{3,2},{4,3},{5,4},{6,5},{7,6},{8,15},{9,8},{10,9... | collective-permute-start | bytes 196616 | tf_op jit(solution)/shard_map/ppermute | solution.py:882

commit v3 on v2

--- a/solution.py
+++ b/solution.py
@@ -415,16 +415,23 @@
         colbf_ref[:, k * features : (k + 1) * features] = work_ref[k].astype(BF16)
 
 
-def send_kernel(colbf_ref, slot_ref, out_ref):
+def send_kernel(colbf_ref, slot_ref, out_hbm, out_ref, sems):
     elements = colbf_ref.shape[0]
     slots = out_ref.shape[0]
-    piece = slots // 4
-    for part in range(4):
+    pieces = sems.shape[0]
+    piece = slots // pieces
+    copies = []
+    for part in range(pieces):
+        at = pl.ds(part * piece, piece)
         chosen = (iota((piece, elements), 0) + part * piece) == slot_ref[...]
         chosen = jnp.where(chosen, 1.0, 0.0)
         filled = jnp.max(chosen, axis=1, keepdims=True)
         moved = jnp.dot(chosen.astype(BF16), colbf_ref[...], preferred_element_type=F32)
-        out_ref[pl.ds(part * piece, piece), :] = jnp.where(filled > 0.0, moved, EMPTY).astype(BF16)
+        out_ref[at, :] = jnp.where(filled > 0.0, moved, EMPTY).astype(BF16)
+        copies.append(pltpu.make_async_copy(out_ref.at[at], out_hbm.at[at], sems.at[part]))
+        copies[-1].start()
+    for copy in copies:
+        copy.wait()
 
 
 def dense(inputs, weight_ref, bias_ref):
@@ -632,7 +639,9 @@
         out[at, :] = out[at, :] + edge_ref[1]
 
 
-def arrange_kernel(capacity, data_ref, out_ref, wide_ref, rows_ref, vector_ref, start_ref, sem):
+def arrange_kernel(
+    capacity, data_ref, out_hbm, wide_ref, rows_ref, out_ref, vector_ref, start_ref, sem, sems
+):
     devices = vector_ref.shape[0]
     slots = data_ref.shape[0]
     features = data_ref.shape[1] // 4
@@ -657,8 +666,17 @@
             ]
         return carry
 
-    lax.fori_loop(0, devices, one, 0)
-    out_ref[...] = rows_ref[0 : out_ref.shape[0], :].astype(BF16)
+    lax.fori_loop(0, devices, one, 0, unroll=4)
+    pieces = sems.shape[0]
+    piece = 4 * elements // pieces
+    copies = []
+    for part in range(pieces):
+        at = pl.ds(part * piece, piece)
+        out_ref[at, :] = rows_ref[at, :].astype(BF16)
+        copies.append(pltpu.make_async_copy(out_ref.at[at], out_hbm.at[at], sems.at[part]))
+        copies[-1].start()
+    for copy in copies:
+        copy.wait()
 
 
 def params(mib):
@@ -761,6 +779,7 @@
     slots = devices * capacity
     packet = 2 * features + 16
     vmem = pl.BlockSpec(memory_space=pltpu.VMEM)
+    hbm = pl.BlockSpec(memory_space=pltpu.HBM)
     smem = pl.BlockSpec(memory_space=pltpu.SMEM)
 
     xlo, xhi = edges_call(sunlit, prognostic, velocity, jacobian)
@@ -831,8 +850,12 @@
     outgoing = pl.pallas_call(
         send_kernel,
         in_specs=[vmem] * 2,
-        out_specs=vmem,
+        out_specs=hbm,
         out_shape=shape_of((slots, 4 * features), BF16),
+        scratch_shapes=[
+            pltpu.VMEM((slots, 4 * features), BF16),
+            pltpu.SemaphoreType.DMA((4,)),
+        ],
         compiler_params=params(16),
         cost_estimate=cost(2_000_000_000, 3_000_000),
         name="send",
@@ -919,14 +942,16 @@
     span_state = pl.pallas_call(
         lambda *refs: arrange_kernel(capacity, *refs),
         in_specs=[vmem],
-        out_specs=vmem,
+        out_specs=hbm,
         out_shape=shape_of((4 * elements, features), BF16),
         scratch_shapes=[
             pltpu.VMEM((4, slots, features), F32),
             pltpu.VMEM((4 * (elements + capacity), features), F32),
+            pltpu.VMEM((4 * elements, features), BF16),
             pltpu.VMEM((devices, features), jnp.int32),
             pltpu.SMEM((devices, features), jnp.int32),
             pltpu.SemaphoreType.DMA,
+            pltpu.SemaphoreType.DMA((4,)),
         ],
         compiler_params=params(24),
         cost_estimate=cost(1_000_000, 3_000_000),

time: 74 us -> 73.5 us (level)
  Pallas kernels: 42.2 us -> 37.5 us
  starting transfers between devices: 14 us -> 18.1 us
    pallas_call x1, Pallas kernels: 11.8 us -> 7.64 us  [on_device(): pl.pallas_call(network_kernel, grid=(3,), in_specs=[smem, pl.BlockSpec((c...]
    ppermute x1, starting transfers between devices: 0.3 us -> 4.47 us  [on_device(): yprev2 = lax.ppermute(yhi2, 'dom', shifted('dom', 1))]
  transfers between devices with their start and end apart: 7 -> 7, of which waited for: 2 -> 2; matrix products, arithmetic and copies ran while one was open for 0% -> 0% of each run, Pallas kernels for 46% -> 40%
where the time goes in v3:
time: 73.5 us; the launch traced here: 73.1 us
  Pallas kernels  37.5 us (51%)
  starting transfers between devices  18.1 us (25%)
  local copies, waits for them, and re-layouts  10.8 us (15%)
  waiting for transfers between devices  5.86 us (8%)
  between operations  0.86 us (1%)
    pallas_call x1, Pallas kernels, dynamics_call(): pl.pallas_call(dynamics_kernel, in_specs=[hbm, hbm, vmem, vmem], out_spec...  12.3 us
    unnamed x48, local copies, waits for them, and re-layouts  10.8 us
    pallas_call x1, Pallas kernels, on_device(): pl.pallas_call(network_kernel, grid=(3,), in_specs=[smem, pl.BlockSpec((c...  7.64 us
    pallas_call x1, Pallas kernels, on_device(): pl.pallas_call(final_kernel, grid=(elements_x // group,), in_specs=[pl.Bl...  6.63 us
    ppermute x1, starting transfers between devices, on_device(): yprev2 = lax.ppermute(yhi2, 'dom', shifted('dom', 1))  4.47 us
    all_to_all x1, waiting for transfers between devices, on_device(): lax.all_to_all(outgoing.reshape(devices, capacity, 4 * features), ('face'...  3.94 us
    all_to_all x1, starting transfers between devices, on_device(): lax.all_to_all(outgoing.reshape(devices, capacity, 4 * features), ('face'...  3.55 us
    pallas_call x1, Pallas kernels, edges_call(): pl.pallas_call(edges_kernel, grid=(1,), in_specs=[pl.BlockSpec(memory_spa...  3.03 us
  transfers between devices with their start and end apart: 7, of which 2 were waited for; matrix products, arithmetic and copies ran while one was open for 0% of the time, Pallas kernels for 40%

profile of v3, /device:TPU:0, one launch (start us, length us, event | category | flops | bytes accessed | tf_op | source)
XLA Modules:
  0.0 73.1 jit_solution(12548064359665426425)
XLA Ops:
  0.7 3.0 %edges.1 = (f32[272,128]{1,0:T(8,128)}, f32[272,128]{1,0:T(8,128)}) custom-call(s32[24,32]{1,0:T(8,128)} %lit_ref.3, f32[2,64,96,128]{3,2,1,0:T(8,128)} %proghi_ref.1, f32[2,64,96,128]{3,2,1,0:T(8,128)} %proghi_ref.1, bf16[2,64,96,128]{3,2,1,0:T(8,128)(2,1)} %velhi_ref.1, bf16[2,64,96,128]{3,2,1,0:T(8,128)(2,1)} %velhi_ref.1, f32[24,32]{1,0:T(8,128)} %jac_ref.7, ...), custom_call_target="tpu_custom_call" | custom-call | flops 50000000 | bytes 2000000 | tf_op jit(solution)/shard_map/edges/pallas_call | solution.py:708
  3.7 3.0 %collective-permute-start = (f32[272,128]{1,0:T(8,128)}, f32[272,128]{1,0:T(8,128)S(1)}, u32[]{:S(2)}, u32[]{:S(2)}) collective-permute-start(f32[272,128]{1,0:T(8,128)} %get-tuple-element.24.refs_2_), channel_id=1, source_target_pairs={{0,8},{8,16},{16,24},{24,0},{1,9},{9,17},{17,25},{25,1},{2,10},{10... | collective-permute-start | bytes 417800 | tf_op jit(solution)/shard_map/ppermute | solution.py:809
  6.7 2.1 %collective-permute-start.1 = (f32[272,128]{1,0:T(8,128)}, f32[272,128]{1,0:T(8,128)S(1)}, u32[]{:S(2)}, u32[]{:S(2)}) collective-permute-start(f32[272,128]{1,0:T(8,128)} %get-tuple-element.23.refs_1_), channel_id=1, source_target_pairs={{0,24},{8,0},{16,8},{24,16},{1,25},{9,1},{17,9},{25,17},{2,26},{10... | collective-permute-start | bytes 417800 | tf_op jit(solution)/shard_map/ppermute | solution.py:810
  8.8 12.3 %dynamics.1 = (f32[96,2,64,128]{3,2,1,0:T(8,128)S(1)}, f32[128,128]{1,0:T(8,128)S(1)}, f32[128,128]{1,0:T(8,128)S(1)}) custom-call(f32[2,64,96,128]{3,2,1,0:T(8,128)} %proghi_ref.1, bf16[2,64,96,128]{3,2,1,0:T(8,128)(2,1)S(1)} %copy-done, f32[24,32]{1,0:T(8,128)S(1)} %copy-done.3, bf16[384,128]{1,0:T(8,128)(2,1)S(1)} %copy-done.2), custom_call_target="tpu_custom_call" | custom-call | flops 2000000000 | bytes 16000000 | tf_op jit(solution)/shard_map/dynamics/pallas_call | solution.py:737
  21.2 0.1 collective-permute-start.2
  21.2 2.6 %collective-permute-start.3 = (f32[128,128]{1,0:T(8,128)S(1)}, f32[128,128]{1,0:T(8,128)S(1)}, u32[]{:S(2)}, u32[]{:S(2)}) collective-permute-start(f32[128,128]{1,0:T(8,128)S(1)} %get-tuple-element.27.refs_5_), channel_id=1, source_target_pairs={{0,7},{1,0},{2,1},{3,2},{4,3},{5,4},{6,5},{7,6},{8,15},{9,8},{10,9... | collective-permute-start | bytes 196616 | tf_op jit(solution)/shard_map/ppermute | solution.py:820
  23.9 2.8 %cells.1 = (f32[4,768,128]{2,1,0:T(8,128)S(1)}, s32[1,768]{1,0:T(1,128)S(1)}) custom-call(f32[96,2,64,128]{3,2,1,0:T(8,128)S(1)} %get-tuple-element.21.refs_0_.adv_ref, s32[24,32]{1,0:T(8,128)S(1)} %copy-done.7), custom_call_target="tpu_custom_call" | custom-call | flops 1000000000 | bytes 8000000 | tf_op jit(solution)/shard_map/cells/pallas_call | solution.py:789
  26.7 0.5 complete.1
  27.3 2.3 %send.1 = bf16[1536,512]{1,0:T(8,128)(2,1)} custom-call(bf16[768,512]{1,0:T(8,128)(2,1)S(1)} %get-tuple-element.29.col_ref.colbf_ref, s32[1,768]{1,0:T(1,128)S(1)} %get-tuple-element.39.slot_ref), custom_call_target="tpu_custom_call" | custom-call | flops 2000000000 | bytes 3000000 | tf_op jit(solution)/shard_map/send/pallas_call | solution.py:850
  29.6 3.5 %all-to-all-start = ((bf16[32,48,512]{2,1,0:T(8,128)(2,1)}), bf16[32,48,512]{2,1,0:T(8,128)(2,1)S(1)}, u32[]{:S(2)}, u32[]{:S(2)}) async-start(bf16[32,48,512]{2,1,0:T(8,128)(2,1)} %bitcast.7), calls=%async_computation | async-start | bytes 3145728 | tf_op jit(solution)/shard_map/all_to_all | solution.py:864
  33.2 1.2 %copy-done.9 = bf16[512,512]{1,0:T(8,128)(2,1)S(1)} copy-done((bf16[512,512]{1,0:T(8,128)(2,1)S(1)}, bf16[512,512]{1,0:T(8,128)(2,1)}, u32[]{:S(2)}) %copy-start.9) | copy-done | bytes 524312
  34.4 1.2 %copy-done.10 = bf16[512,512]{1,0:T(8,128)(2,1)S(1)} copy-done((bf16[512,512]{1,0:T(8,128)(2,1)S(1)}, bf16[512,512]{1,0:T(8,128)(2,1)}, u32[]{:S(2)}) %copy-start.10) | copy-done | bytes 524312
  35.6 0.9 %copy-done.11 = bf16[128,512]{1,0:T(8,128)(2,1)S(1)} copy-done((bf16[128,512]{1,0:T(8,128)(2,1)S(1)}, bf16[128,512]{1,0:T(8,128)(2,1)}, u32[]{:S(2)}) %copy-start.11) | copy-done | bytes 131096
  36.5 0.9 %copy-done.12 = bf16[512,128]{1,0:T(8,128)(2,1)S(1)} copy-done((bf16[512,128]{1,0:T(8,128)(2,1)S(1)}, bf16[512,128]{1,0:T(8,128)(2,1)}, u32[]{:S(2)}) %copy-start.12) | copy-done | bytes 131096
  37.4 0.9 %copy-done.13 = bf16[128,512]{1,0:T(8,128)(2,1)S(1)} copy-done((bf16[128,512]{1,0:T(8,128)(2,1)S(1)}, bf16[128,512]{1,0:T(8,128)(2,1)}, u32[]{:S(2)}) %copy-start.13) | copy-done | bytes 131096
  38.3 0.9 %copy-done.14 = bf16[512,128]{1,0:T(8,128)(2,1)S(1)} copy-done((bf16[512,128]{1,0:T(8,128)(2,1)S(1)}, bf16[512,128]{1,0:T(8,128)(2,1)}, u32[]{:S(2)}) %copy-start.14) | copy-done | bytes 131096
  39.2 0.7 copy-done.15
  39.9 0.7 copy-done.16
  40.6 0.7 copy-done.17
  41.3 0.7 copy-done.18
  41.9 0.7 copy-done.19
  42.6 0.7 copy-done.20
  43.3 0.7 copy-done.21
  43.9 7.6 %network.1 = (bf16[768,512]{1,0:T(8,128)(2,1)S(1)}, bf16[128,128]{1,0:T(8,128)(2,1)S(1)}) custom-call(s32[24,32]{1,0:T(8,128)S(1)} %copy-done.6, bf16[768,512]{1,0:T(8,128)(2,1)S(1)} %get-tuple-element.29.col_ref.colbf_ref, bf16[128,128]{1,0:T(8,128)(2,1)S(1)} %get-tuple-element.30.ghost_ref, f32[272,128]{1,0:T(8,128)S(1)} %collective-permute-done.refs_2_.refs_3_.prev_ref, ...), custom_call_target="tpu_custom_call" | custom-call | flops 6442450944 | bytes 4000000 | tf_op jit(solution)/shard_map/network/pallas_call | solution.py:869
  51.6 0.1 rims.1
  51.7 4.5 %collective-permute-start.4 = (f32[128,128]{1,0:T(8,128)S(1)}, f32[128,128]{1,0:T(8,128)S(1)}, u32[]{:S(2)}, u32[]{:S(2)}) collective-permute-start(f32[128,128]{1,0:T(8,128)S(1)} %get-tuple-element.34.yhi_ref), channel_id=1, source_target_pairs={{0,1},{1,2},{2,3},{3,4},{4,5},{5,6},{6,7},{7,0},{8,9},{9,10},{10,1... | collective-permute-start | bytes 196616 | tf_op jit(solution)/shard_map/ppermute | solution.py:904
  56.1 2.2 %collective-permute-start.5 = (f32[128,128]{1,0:T(8,128)S(1)}, f32[128,128]{1,0:T(8,128)S(1)}, u32[]{:S(2)}, u32[]{:S(2)}) collective-permute-start(f32[128,128]{1,0:T(8,128)S(1)} %get-tuple-element.33.ylo_ref), channel_id=1, source_target_pairs={{0,7},{1,0},{2,1},{3,2},{4,3},{5,4},{6,5},{7,6},{8,15},{9,8},{10,9... | collective-permute-start | bytes 196616 | tf_op jit(solution)/shard_map/ppermute | solution.py:905
  58.4 1.9 %collective-permute-done.4.yprev_ref = f32[128,128]{1,0:T(8,128)S(1)} collective-permute-done((f32[128,128]{1,0:T(8,128)S(1)}, f32[128,128]{1,0:T(8,128)S(1)}, u32[]{:S(2)}, u32[]{:S(2)}) %collective-permute-start.4) | collective-permute-done | bytes 65568 | tf_op jit(solution)/shard_map/ppermute | solution.py:904
  60.3 0.0 collective-permute-done.5.ynext_ref
  60.3 6.6 %final.1 = f32[2,64,96,128]{3,2,1,0:T(8,128)} custom-call(f32[96,2,64,128]{3,2,1,0:T(8,128)S(1)} %bitcast.10, bf16[768,512]{1,0:T(8,128)(2,1)S(1)} %get-tuple-element.31.inc_ref, bf16[128,128]{1,0:T(8,128)(2,1)S(1)} %get-tuple-element.32.near_ref, f32[24,32]{1,0:T(8,128)S(1)} %copy-done.3, f32[272,128]{1,0:T(8,128)S(1)} %collective-permute-done.refs_2_.refs_3_.prev_ref, ...), custom_call_target="tpu_custom_call" | custom-call | flops 1000000000 | bytes 14000000 | tf_op jit(solution)/shard_map/final/pallas_call | solution.py:907
  66.9 3.9 %all-to-all-done = bf16[32,48,512]{2,1,0:T(8,128)(2,1)S(1)} async-done(((bf16[32,48,512]{2,1,0:T(8,128)(2,1)}), bf16[32,48,512]{2,1,0:T(8,128)(2,1)S(1)}, u32[]{:S(2)}, u32[]{:S(2)}) %all-to-all-start) | async-done | bytes 1572896 | tf_op jit(solution)/shard_map/all_to_all | solution.py:864
  70.9 2.2 %arrange.1 = bf16[3072,128]{1,0:T(8,128)(2,1)} custom-call(bf16[1536,512]{1,0:T(8,128)(2,1)S(1)} %bitcast.11), custom_call_target="tpu_custom_call" | custom-call | flops 1000000 | bytes 3000000 | tf_op jit(solution)/shard_map/arrange/pallas_call | solution.py:942
  (41 shorter events, 0.1 us)
Async XLA Ops:
  0.6 8.2 %copy-start.2 = (bf16[384,128]{1,0:T(8,128)(2,1)S(1)}, bf16[384,128]{1,0:T(8,128)(2,1)}, u32[]{:S(2)}) copy-start(bf16[384,128]{1,0:T(8,128)(2,1)} %constant.2.clone.dcat_ref) | copy-start | bytes 294916
  0.6 8.2 %copy-start = (bf16[2,64,96,128]{3,2,1,0:T(8,128)(2,1)S(1)}, bf16[2,64,96,128]{3,2,1,0:T(8,128)(2,1)}, u32[]{:S(2)}) copy-start(bf16[2,64,96,128]{3,2,1,0:T(8,128)(2,1)} %velhi_ref.1) | copy-start | bytes 9437188
  0.7 8.2 %copy-start.3 = (f32[24,32]{1,0:T(8,128)S(1)}, f32[24,32]{1,0:T(8,128)}, u32[]{:S(2)}) copy-start(f32[24,32]{1,0:T(8,128)} %jac_ref.7) | copy-start | bytes 9220
  3.7 17.4 %collective-permute-start = (f32[272,128]{1,0:T(8,128)}, f32[272,128]{1,0:T(8,128)S(1)}, u32[]{:S(2)}, u32[]{:S(2)}) collective-permute-start(f32[272,128]{1,0:T(8,128)} %get-tuple-element.24.refs_2_), channel_id=1, source_target_pairs={{0,8},{8,16},{16,24},{24,0},{1,9},{9,17},{17,25},{25,1},{2,10},{10... | collective-permute-start | bytes 417800 | tf_op jit(solution)/shard_map/ppermute | solution.py:809
  6.7 17.1 %copy-start.7 = (s32[24,32]{1,0:T(8,128)S(1)}, s32[24,32]{1,0:T(8,128)}, u32[]{:S(2)}) copy-start(s32[24,32]{1,0:T(8,128)} %refs_1_.1) | copy-start | bytes 9220
  6.7 14.4 %collective-permute-start.1 = (f32[272,128]{1,0:T(8,128)}, f32[272,128]{1,0:T(8,128)S(1)}, u32[]{:S(2)}, u32[]{:S(2)}) collective-permute-start(f32[272,128]{1,0:T(8,128)} %get-tuple-element.23.refs_1_), channel_id=1, source_target_pairs={{0,24},{8,0},{16,8},{24,16},{1,25},{9,1},{17,9},{25,17},{2,26},{10... | collective-permute-start | bytes 417800 | tf_op jit(solution)/shard_map/ppermute | solution.py:810
  21.1 5.6 %copy-start.1 = (f32[96,2,64,128]{3,2,1,0:T(8,128)}, f32[96,2,64,128]{3,2,1,0:T(8,128)S(1)}, u32[]{:S(2)}) copy-start(f32[96,2,64,128]{3,2,1,0:T(8,128)S(1)} %get-tuple-element.21.refs_0_.adv_ref) | copy-start | bytes 18874372
  21.2 5.5 %collective-permute-start.2 = (f32[128,128]{1,0:T(8,128)S(1)}, f32[128,128]{1,0:T(8,128)S(1)}, u32[]{:S(2)}, u32[]{:S(2)}) collective-permute-start(f32[128,128]{1,0:T(8,128)S(1)} %get-tuple-element.28.refs_6_), channel_id=1, source_target_pairs={{0,1},{1,2},{2,3},{3,4},{4,5},{5,6},{6,7},{7,0},{8,9},{9,10},{10,1... | collective-permute-start | bytes 196616 | tf_op jit(solution)/shard_map/ppermute | solution.py:819
  21.2 5.5 %collective-permute-start.3 = (f32[128,128]{1,0:T(8,128)S(1)}, f32[128,128]{1,0:T(8,128)S(1)}, u32[]{:S(2)}, u32[]{:S(2)}) collective-permute-start(f32[128,128]{1,0:T(8,128)S(1)} %get-tuple-element.27.refs_5_), channel_id=1, source_target_pairs={{0,7},{1,0},{2,1},{3,2},{4,3},{5,4},{6,5},{7,6},{8,15},{9,8},{10,9... | collective-permute-start | bytes 196616 | tf_op jit(solution)/shard_map/ppermute | solution.py:820
  23.9 2.9 %copy-start.4 = (f32[272,128]{1,0:T(8,128)S(1)}, f32[272,128]{1,0:T(8,128)}, u32[]{:S(2)}) copy-start(f32[272,128]{1,0:T(8,128)} %get-tuple-element.23.refs_1_) | copy-start | bytes 417796
  23.9 2.9 %copy-start.5 = (f32[272,128]{1,0:T(8,128)S(1)}, f32[272,128]{1,0:T(8,128)}, u32[]{:S(2)}) copy-start(f32[272,128]{1,0:T(8,128)} %get-tuple-element.24.refs_2_) | copy-start | bytes 417796
  29.6 3.6 %copy-start.6 = (s32[24,32]{1,0:T(8,128)S(1)}, s32[24,32]{1,0:T(8,128)}, u32[]{:S(2)}) copy-start(s32[24,32]{1,0:T(8,128)} %lit_ref.3) | copy-start | bytes 9220
  29.6 3.6 %copy-start.8 = (bf16[512,512]{1,0:T(8,128)(2,1)S(1)}, bf16[512,512]{1,0:T(8,128)(2,1)}, u32[]{:S(2)}) copy-start(bf16[512,512]{1,0:T(8,128)(2,1)} %w2.1) | copy-start | bytes 1572868
  29.6 41.3 %all-to-all-start = ((bf16[32,48,512]{2,1,0:T(8,128)(2,1)}), bf16[32,48,512]{2,1,0:T(8,128)(2,1)S(1)}, u32[]{:S(2)}, u32[]{:S(2)}) async-start(bf16[32,48,512]{2,1,0:T(8,128)(2,1)} %bitcast.7), calls=%async_computation | async-start | bytes 3145728 | tf_op jit(solution)/shard_map/all_to_all | solution.py:864
  33.1 27.2 %slice-start = ((s8[6291456]{0:T(1024)(128)(4,1)}), s8[4194304]{0:T(1024)(128)(4,1)S(1)}, s32[]{:S(2)}) async-start(s8[6291456]{0:T(1024)(128)(4,1)} %bitcast.9), calls=%async_computation.1 | async-start | bytes 8388608
  33.2 1.2 %copy-start.9 = (bf16[512,512]{1,0:T(8,128)(2,1)S(1)}, bf16[512,512]{1,0:T(8,128)(2,1)}, u32[]{:S(2)}) copy-start(bf16[512,512]{1,0:T(8,128)(2,1)} %w3.1) | copy-start | bytes 1572868
  34.4 1.2 %copy-start.10 = (bf16[512,512]{1,0:T(8,128)(2,1)S(1)}, bf16[512,512]{1,0:T(8,128)(2,1)}, u32[]{:S(2)}) copy-start(bf16[512,512]{1,0:T(8,128)(2,1)} %s2_.1) | copy-start | bytes 1572868
  35.6 0.9 %copy-start.11 = (bf16[128,512]{1,0:T(8,128)(2,1)S(1)}, bf16[128,512]{1,0:T(8,128)(2,1)}, u32[]{:S(2)}) copy-start(bf16[128,512]{1,0:T(8,128)(2,1)} %w1.1) | copy-start | bytes 393220
  36.5 0.9 %copy-start.12 = (bf16[512,128]{1,0:T(8,128)(2,1)S(1)}, bf16[512,128]{1,0:T(8,128)(2,1)}, u32[]{:S(2)}) copy-start(bf16[512,128]{1,0:T(8,128)(2,1)} %w4.1) | copy-start | bytes 393220
  37.4 0.9 %copy-start.13 = (bf16[128,512]{1,0:T(8,128)(2,1)S(1)}, bf16[128,512]{1,0:T(8,128)(2,1)}, u32[]{:S(2)}) copy-start(bf16[128,512]{1,0:T(8,128)(2,1)} %s1_.1) | copy-start | bytes 393220
  38.3 0.9 %copy-start.14 = (bf16[512,128]{1,0:T(8,128)(2,1)S(1)}, bf16[512,128]{1,0:T(8,128)(2,1)}, u32[]{:S(2)}) copy-start(bf16[512,128]{1,0:T(8,128)(2,1)} %s3.1) | copy-start | bytes 393220
  39.2 0.7 copy-start.15
  39.9 0.7 copy-start.16
  40.6 0.7 copy-start.17
  41.3 0.7 copy-start.18
  41.9 0.7 copy-start.19
  42.6 0.7 copy-start.20
  43.3 0.7 copy-start.21
  43.9 16.4 %slice-start.1 = ((s8[6291456]{0:T(1024)(128)(4,1)}), s8[2097152]{0:T(1024)(128)(4,1)S(1)}, s32[]{:S(2)}) async-start(s8[6291456]{0:T(1024)(128)(4,1)} %bitcast.9), calls=%async_computation.2 | async-start | bytes 4194304
  51.7 8.6 %collective-permute-start.4 = (f32[128,128]{1,0:T(8,128)S(1)}, f32[128,128]{1,0:T(8,128)S(1)}, u32[]{:S(2)}, u32[]{:S(2)}) collective-permute-start(f32[128,128]{1,0:T(8,128)S(1)} %get-tuple-element.34.yhi_ref), channel_id=1, source_target_pairs={{0,1},{1,2},{2,3},{3,4},{4,5},{5,6},{6,7},{7,0},{8,9},{9,10},{10,1... | collective-permute-start | bytes 196616 | tf_op jit(solution)/shard_map/ppermute | solution.py:904
  56.1 4.1 %collective-permute-start.5 = (f32[128,128]{1,0:T(8,128)S(1)}, f32[128,128]{1,0:T(8,128)S(1)}, u32[]{:S(2)}, u32[]{:S(2)}) collective-permute-start(f32[128,128]{1,0:T(8,128)S(1)} %get-tuple-element.33.ylo_ref), channel_id=1, source_target_pairs={{0,7},{1,0},{2,1},{3,2},{4,3},{5,4},{6,5},{7,6},{8,15},{9,8},{10,9... | collective-permute-start | bytes 196616 | tf_op jit(solution)/shard_map/ppermute | solution.py:905

commit v4 on v3

--- a/solution.py
+++ b/solution.py
@@ -143,7 +143,7 @@
 
 
 def dynamics_kernel(
-    prog_hbm, vel_hbm, jac_ref, dcat_ref, adv_ref, ylo_ref, yhi_ref, prog_ref, vel_ref,
+    prog_hbm, vel_ref, jac_ref, dcat_ref, adv_ref, ylo_ref, yhi_ref, prog_ref,
     sy3_ref, vf3_ref, pf3_ref, scale_ref, inside_ref, shared_ref, zlo_ref, zhi_ref, sems,
 ):
     _, levels, width_x, width = prog_ref.shape
@@ -157,16 +157,12 @@
     vf_ref = vf3_ref.reshape(planes * pitch, width)
     pf_ref = pf3_ref.reshape(planes * pitch, width)
 
-    def copies(step):
+    def arrival(step):
         at = pl.ds(step * tile, tile)
-        return (
-            pltpu.make_async_copy(prog_hbm.at[:, at], prog_ref.at[:, at], sems.at[0, step]),
-            pltpu.make_async_copy(vel_hbm.at[:, at], vel_ref.at[:, at], sems.at[1, step]),
-        )
+        return pltpu.make_async_copy(prog_hbm.at[:, at], prog_ref.at[:, at], sems.at[step])
 
     for step in range(steps):
-        for copy in copies(step):
-            copy.start()
+        arrival(step).start()
 
     mass = along_lanes(jac_ref[...], width)
     scale_ref[...] = -TIME_STEP * jnp.sqrt(mass)
@@ -263,8 +259,7 @@
 
     @pl.loop(0, steps)
     def _(step):
-        for copy in copies(step):
-            copy.wait()
+        arrival(step).wait()
         one_tile(step)
 
     jac = jac_ref[...]
@@ -736,7 +731,7 @@
     vmem = pl.BlockSpec(memory_space=pltpu.VMEM)
     return pl.pallas_call(
         dynamics_kernel,
-        in_specs=[hbm, hbm, vmem, vmem],
+        in_specs=[hbm, vmem, vmem, vmem],
         out_specs=[vmem] * 3,
         out_shape=[
             shape_of((width_x, fields, levels, width)),
@@ -745,7 +740,6 @@
         ],
         scratch_shapes=[
             pltpu.VMEM(prognostic.shape, F32),
-            pltpu.VMEM(velocity.shape, BF16),
             pltpu.VMEM((2 * tile, width_x + 8, width), F32),
             pltpu.VMEM((2 * tile, width_x + 8, width), F32),
             pltpu.VMEM((2 * tile, width_x + 8, width), F32),
@@ -754,7 +748,7 @@
             pltpu.VMEM((elements_x, width), F32),
             pltpu.VMEM((features, width), F32),
             pltpu.VMEM((features, width), F32),
-            pltpu.SemaphoreType.DMA((2, levels // tile)),
+            pltpu.SemaphoreType.DMA((levels // tile,)),
         ],
         compiler_params=params(42),
         cost_estimate=cost(2_000_000_000, 16_000_000),
@@ -946,7 +940,7 @@
         out_shape=shape_of((4 * elements, features), BF16),
         scratch_shapes=[
             pltpu.VMEM((4, slots, features), F32),
-            pltpu.VMEM((4 * (elements + capacity), features), F32),
+            pltpu.VMEM((4 * (elements + capacity) + 8, features), F32),
             pltpu.VMEM((4 * elements, features), BF16),
             pltpu.VMEM((devices, features), jnp.int32),
             pltpu.SMEM((devices, features), jnp.int32),

time: 73.5 us -> 73.4 us (level)
  Pallas kernels: 37.5 us -> 41.6 us
  starting transfers between devices: 18.1 us -> 14 us
    ppermute x1, starting transfers between devices: 4.47 us -> 0.3 us  [on_device(): yprev2 = lax.ppermute(yhi2, 'dom', shifted('dom', 1))]
    pallas_call x1, Pallas kernels: 7.64 us -> 11.8 us  [on_device(): pl.pallas_call(network_kernel, grid=(3,), in_specs=[smem, pl.BlockSpec((c...]
  transfers between devices with their start and end apart: 7 -> 7, of which waited for: 2 -> 2; matrix products, arithmetic and copies ran while one was open for 0% -> 0% of each run, Pallas kernels for 40% -> 46%
where the time goes in v4:
time: 73.4 us; the launch traced here: 73 us
  Pallas kernels  41.6 us (57%)
  starting transfers between devices  14 us (19%)
  local copies, waits for them, and re-layouts  10.8 us (15%)
  waiting for transfers between devices  5.69 us (8%)
  between operations  0.87 us (1%)
    pallas_call x1, Pallas kernels, dynamics_call(): pl.pallas_call(dynamics_kernel, in_specs=[hbm, vmem, vmem, vmem], out_spe...  12.2 us
    pallas_call x1, Pallas kernels, on_device(): pl.pallas_call(network_kernel, grid=(3,), in_specs=[smem, pl.BlockSpec((c...  11.8 us
    unnamed x48, local copies, waits for them, and re-layouts  10.8 us
    pallas_call x1, Pallas kernels, on_device(): pl.pallas_call(final_kernel, grid=(elements_x // group,), in_specs=[pl.Bl...  6.64 us
    all_to_all x1, waiting for transfers between devices, on_device(): lax.all_to_all(outgoing.reshape(devices, capacity, 4 * features), ('face'...  3.73 us
    all_to_all x1, starting transfers between devices, on_device(): lax.all_to_all(outgoing.reshape(devices, capacity, 4 * features), ('face'...  3.54 us
    pallas_call x1, Pallas kernels, edges_call(): pl.pallas_call(edges_kernel, grid=(1,), in_specs=[pl.BlockSpec(memory_spa...  3.03 us
    ppermute x1, starting transfers between devices, on_device(): prev = lax.ppermute(xhi, 'face', shifted('face', 1))  3.02 us
  transfers between devices with their start and end apart: 7, of which 2 were waited for; matrix products, arithmetic and copies ran while one was open for 0% of the time, Pallas kernels for 46%

profile of v4, /device:TPU:0, one launch (start us, length us, event | category | flops | bytes accessed | tf_op | source)
XLA Modules:
  0.0 73.0 jit_solution(2149442704547129402)
XLA Ops:
  0.6 0.0 copy-start.2
  0.7 3.0 %edges.1 = (f32[272,128]{1,0:T(8,128)}, f32[272,128]{1,0:T(8,128)}) custom-call(s32[24,32]{1,0:T(8,128)} %lit_ref.3, f32[2,64,96,128]{3,2,1,0:T(8,128)} %proghi_ref.1, f32[2,64,96,128]{3,2,1,0:T(8,128)} %proghi_ref.1, bf16[2,64,96,128]{3,2,1,0:T(8,128)(2,1)} %velhi_ref.1, bf16[2,64,96,128]{3,2,1,0:T(8,128)(2,1)} %velhi_ref.1, f32[24,32]{1,0:T(8,128)} %jac_ref.7, ...), custom_call_target="tpu_custom_call" | custom-call | flops 50000000 | bytes 2000000 | tf_op jit(solution)/shard_map/edges/pallas_call | solution.py:703
  3.7 3.0 %collective-permute-start = (f32[272,128]{1,0:T(8,128)}, f32[272,128]{1,0:T(8,128)S(1)}, u32[]{:S(2)}, u32[]{:S(2)}) collective-permute-start(f32[272,128]{1,0:T(8,128)} %get-tuple-element.24.refs_2_), channel_id=1, source_target_pairs={{0,8},{8,16},{16,24},{24,0},{1,9},{9,17},{17,25},{25,1},{2,10},{10... | collective-permute-start | bytes 417800 | tf_op jit(solution)/shard_map/ppermute | solution.py:803
  6.7 2.1 %collective-permute-start.1 = (f32[272,128]{1,0:T(8,128)}, f32[272,128]{1,0:T(8,128)S(1)}, u32[]{:S(2)}, u32[]{:S(2)}) collective-permute-start(f32[272,128]{1,0:T(8,128)} %get-tuple-element.23.refs_1_), channel_id=1, source_target_pairs={{0,24},{8,0},{16,8},{24,16},{1,25},{9,1},{17,9},{25,17},{2,26},{10... | collective-permute-start | bytes 417800 | tf_op jit(solution)/shard_map/ppermute | solution.py:804
  8.8 12.2 %dynamics.1 = (f32[96,2,64,128]{3,2,1,0:T(8,128)S(1)}, f32[128,128]{1,0:T(8,128)S(1)}, f32[128,128]{1,0:T(8,128)S(1)}) custom-call(f32[2,64,96,128]{3,2,1,0:T(8,128)} %proghi_ref.1, bf16[2,64,96,128]{3,2,1,0:T(8,128)(2,1)S(1)} %copy-done, f32[24,32]{1,0:T(8,128)S(1)} %copy-done.3, bf16[384,128]{1,0:T(8,128)(2,1)S(1)} %copy-done.2), custom_call_target="tpu_custom_call" | custom-call | flops 2000000000 | bytes 16000000 | tf_op jit(solution)/shard_map/dynamics/pallas_call | solution.py:732
  21.1 0.1 collective-permute-start.2
  21.2 2.6 %collective-permute-start.3 = (f32[128,128]{1,0:T(8,128)S(1)}, f32[128,128]{1,0:T(8,128)S(1)}, u32[]{:S(2)}, u32[]{:S(2)}) collective-permute-start(f32[128,128]{1,0:T(8,128)S(1)} %get-tuple-element.27.refs_5_), channel_id=1, source_target_pairs={{0,7},{1,0},{2,1},{3,2},{4,3},{5,4},{6,5},{7,6},{8,15},{9,8},{10,9... | collective-permute-start | bytes 196616 | tf_op jit(solution)/shard_map/ppermute | solution.py:814
  23.8 2.8 %cells.1 = (f32[4,768,128]{2,1,0:T(8,128)S(1)}, s32[1,768]{1,0:T(1,128)S(1)}) custom-call(f32[96,2,64,128]{3,2,1,0:T(8,128)S(1)} %get-tuple-element.21.refs_0_.adv_ref, s32[24,32]{1,0:T(8,128)S(1)} %copy-done.7), custom_call_target="tpu_custom_call" | custom-call | flops 1000000000 | bytes 8000000 | tf_op jit(solution)/shard_map/cells/pallas_call | solution.py:783
  26.7 0.5 complete.1
  27.2 2.3 %send.1 = bf16[1536,512]{1,0:T(8,128)(2,1)} custom-call(bf16[768,512]{1,0:T(8,128)(2,1)S(1)} %get-tuple-element.29.col_ref.colbf_ref, s32[1,768]{1,0:T(1,128)S(1)} %get-tuple-element.39.slot_ref), custom_call_target="tpu_custom_call" | custom-call | flops 2000000000 | bytes 3000000 | tf_op jit(solution)/shard_map/send/pallas_call | solution.py:844
  29.5 3.5 %all-to-all-start = ((bf16[32,48,512]{2,1,0:T(8,128)(2,1)}), bf16[32,48,512]{2,1,0:T(8,128)(2,1)S(1)}, u32[]{:S(2)}, u32[]{:S(2)}) async-start(bf16[32,48,512]{2,1,0:T(8,128)(2,1)} %bitcast.7), calls=%async_computation | async-start | bytes 3145728 | tf_op jit(solution)/shard_map/all_to_all | solution.py:858
  33.1 1.2 %copy-done.9 = bf16[512,512]{1,0:T(8,128)(2,1)S(1)} copy-done((bf16[512,512]{1,0:T(8,128)(2,1)S(1)}, bf16[512,512]{1,0:T(8,128)(2,1)}, u32[]{:S(2)}) %copy-start.9) | copy-done | bytes 524312
  34.3 1.2 %copy-done.10 = bf16[512,512]{1,0:T(8,128)(2,1)S(1)} copy-done((bf16[512,512]{1,0:T(8,128)(2,1)S(1)}, bf16[512,512]{1,0:T(8,128)(2,1)}, u32[]{:S(2)}) %copy-start.10) | copy-done | bytes 524312
  35.5 0.9 %copy-done.11 = bf16[128,512]{1,0:T(8,128)(2,1)S(1)} copy-done((bf16[128,512]{1,0:T(8,128)(2,1)S(1)}, bf16[128,512]{1,0:T(8,128)(2,1)}, u32[]{:S(2)}) %copy-start.11) | copy-done | bytes 131096
  36.4 0.9 %copy-done.12 = bf16[512,128]{1,0:T(8,128)(2,1)S(1)} copy-done((bf16[512,128]{1,0:T(8,128)(2,1)S(1)}, bf16[512,128]{1,0:T(8,128)(2,1)}, u32[]{:S(2)}) %copy-start.12) | copy-done | bytes 131096
  37.3 0.9 %copy-done.13 = bf16[128,512]{1,0:T(8,128)(2,1)S(1)} copy-done((bf16[128,512]{1,0:T(8,128)(2,1)S(1)}, bf16[128,512]{1,0:T(8,128)(2,1)}, u32[]{:S(2)}) %copy-start.13) | copy-done | bytes 131096
  38.2 0.9 %copy-done.14 = bf16[512,128]{1,0:T(8,128)(2,1)S(1)} copy-done((bf16[512,128]{1,0:T(8,128)(2,1)S(1)}, bf16[512,128]{1,0:T(8,128)(2,1)}, u32[]{:S(2)}) %copy-start.14) | copy-done | bytes 131096
  39.1 0.7 copy-done.15
  39.8 0.7 copy-done.16
  40.5 0.7 copy-done.17
  41.2 0.7 copy-done.18
  41.9 0.7 copy-done.19
  42.6 0.7 copy-done.20
  43.2 0.7 copy-done.21
  43.9 11.8 %network.1 = (bf16[768,512]{1,0:T(8,128)(2,1)S(1)}, bf16[128,128]{1,0:T(8,128)(2,1)S(1)}) custom-call(s32[24,32]{1,0:T(8,128)S(1)} %copy-done.6, bf16[768,512]{1,0:T(8,128)(2,1)S(1)} %get-tuple-element.29.col_ref.colbf_ref, bf16[128,128]{1,0:T(8,128)(2,1)S(1)} %get-tuple-element.30.ghost_ref, f32[272,128]{1,0:T(8,128)S(1)} %collective-permute-done.refs_2_.refs_3_.prev_ref, ...), custom_call_target="tpu_custom_call" | custom-call | flops 6442450944 | bytes 4000000 | tf_op jit(solution)/shard_map/network/pallas_call | solution.py:863
  55.7 0.1 rims.1
  55.8 0.3 collective-permute-start.4
  56.1 2.4 %collective-permute-start.5 = (f32[128,128]{1,0:T(8,128)S(1)}, f32[128,128]{1,0:T(8,128)S(1)}, u32[]{:S(2)}, u32[]{:S(2)}) collective-permute-start(f32[128,128]{1,0:T(8,128)S(1)} %get-tuple-element.33.ylo_ref), channel_id=1, source_target_pairs={{0,7},{1,0},{2,1},{3,2},{4,3},{5,4},{6,5},{7,6},{8,15},{9,8},{10,9... | collective-permute-start | bytes 196616 | tf_op jit(solution)/shard_map/ppermute | solution.py:899
  58.5 1.9 %collective-permute-done.4.yprev_ref = f32[128,128]{1,0:T(8,128)S(1)} collective-permute-done((f32[128,128]{1,0:T(8,128)S(1)}, f32[128,128]{1,0:T(8,128)S(1)}, u32[]{:S(2)}, u32[]{:S(2)}) %collective-permute-start.4) | collective-permute-done | bytes 65568 | tf_op jit(solution)/shard_map/ppermute | solution.py:898
  60.4 6.6 %final.1 = f32[2,64,96,128]{3,2,1,0:T(8,128)} custom-call(f32[96,2,64,128]{3,2,1,0:T(8,128)S(1)} %bitcast.10, bf16[768,512]{1,0:T(8,128)(2,1)S(1)} %get-tuple-element.31.inc_ref, bf16[128,128]{1,0:T(8,128)(2,1)S(1)} %get-tuple-element.32.near_ref, f32[24,32]{1,0:T(8,128)S(1)} %copy-done.3, f32[272,128]{1,0:T(8,128)S(1)} %collective-permute-done.refs_2_.refs_3_.prev_ref, ...), custom_call_target="tpu_custom_call" | custom-call | flops 1000000000 | bytes 14000000 | tf_op jit(solution)/shard_map/final/pallas_call | solution.py:901
  67.1 3.7 %all-to-all-done = bf16[32,48,512]{2,1,0:T(8,128)(2,1)S(1)} async-done(((bf16[32,48,512]{2,1,0:T(8,128)(2,1)}), bf16[32,48,512]{2,1,0:T(8,128)(2,1)S(1)}, u32[]{:S(2)}, u32[]{:S(2)}) %all-to-all-start) | async-done | bytes 1572896 | tf_op jit(solution)/shard_map/all_to_all | solution.py:858
  70.8 2.2 %arrange.1 = bf16[3072,128]{1,0:T(8,128)(2,1)} custom-call(bf16[1536,512]{1,0:T(8,128)(2,1)S(1)} %bitcast.11), custom_call_target="tpu_custom_call" | custom-call | flops 1000000 | bytes 3000000 | tf_op jit(solution)/shard_map/arrange/pallas_call | solution.py:936
  (41 shorter events, 0.1 us)
Async XLA Ops:
  0.6 8.2 %copy-start.2 = (bf16[384,128]{1,0:T(8,128)(2,1)S(1)}, bf16[384,128]{1,0:T(8,128)(2,1)}, u32[]{:S(2)}) copy-start(bf16[384,128]{1,0:T(8,128)(2,1)} %constant.2.clone.dcat_ref) | copy-start | bytes 294916
  0.6 8.2 %copy-start = (bf16[2,64,96,128]{3,2,1,0:T(8,128)(2,1)S(1)}, bf16[2,64,96,128]{3,2,1,0:T(8,128)(2,1)}, u32[]{:S(2)}) copy-start(bf16[2,64,96,128]{3,2,1,0:T(8,128)(2,1)} %velhi_ref.1) | copy-start | bytes 9437188
  0.7 8.2 %copy-start.3 = (f32[24,32]{1,0:T(8,128)S(1)}, f32[24,32]{1,0:T(8,128)}, u32[]{:S(2)}) copy-start(f32[24,32]{1,0:T(8,128)} %jac_ref.7) | copy-start | bytes 9220
  3.7 17.4 %collective-permute-start = (f32[272,128]{1,0:T(8,128)}, f32[272,128]{1,0:T(8,128)S(1)}, u32[]{:S(2)}, u32[]{:S(2)}) collective-permute-start(f32[272,128]{1,0:T(8,128)} %get-tuple-element.24.refs_2_), channel_id=1, source_target_pairs={{0,8},{8,16},{16,24},{24,0},{1,9},{9,17},{17,25},{25,1},{2,10},{10... | collective-permute-start | bytes 417800 | tf_op jit(solution)/shard_map/ppermute | solution.py:803
  6.7 17.1 %copy-start.7 = (s32[24,32]{1,0:T(8,128)S(1)}, s32[24,32]{1,0:T(8,128)}, u32[]{:S(2)}) copy-start(s32[24,32]{1,0:T(8,128)} %refs_1_.1) | copy-start | bytes 9220
  6.7 14.3 %collective-permute-start.1 = (f32[272,128]{1,0:T(8,128)}, f32[272,128]{1,0:T(8,128)S(1)}, u32[]{:S(2)}, u32[]{:S(2)}) collective-permute-start(f32[272,128]{1,0:T(8,128)} %get-tuple-element.23.refs_1_), channel_id=1, source_target_pairs={{0,24},{8,0},{16,8},{24,16},{1,25},{9,1},{17,9},{25,17},{2,26},{10... | collective-permute-start | bytes 417800 | tf_op jit(solution)/shard_map/ppermute | solution.py:804
  21.0 5.6 %copy-start.1 = (f32[96,2,64,128]{3,2,1,0:T(8,128)}, f32[96,2,64,128]{3,2,1,0:T(8,128)S(1)}, u32[]{:S(2)}) copy-start(f32[96,2,64,128]{3,2,1,0:T(8,128)S(1)} %get-tuple-element.21.refs_0_.adv_ref) | copy-start | bytes 18874372
  21.1 5.5 %collective-permute-start.2 = (f32[128,128]{1,0:T(8,128)S(1)}, f32[128,128]{1,0:T(8,128)S(1)}, u32[]{:S(2)}, u32[]{:S(2)}) collective-permute-start(f32[128,128]{1,0:T(8,128)S(1)} %get-tuple-element.28.refs_6_), channel_id=1, source_target_pairs={{0,1},{1,2},{2,3},{3,4},{4,5},{5,6},{6,7},{7,0},{8,9},{9,10},{10,1... | collective-permute-start | bytes 196616 | tf_op jit(solution)/shard_map/ppermute | solution.py:813
  21.2 5.5 %collective-permute-start.3 = (f32[128,128]{1,0:T(8,128)S(1)}, f32[128,128]{1,0:T(8,128)S(1)}, u32[]{:S(2)}, u32[]{:S(2)}) collective-permute-start(f32[128,128]{1,0:T(8,128)S(1)} %get-tuple-element.27.refs_5_), channel_id=1, source_target_pairs={{0,7},{1,0},{2,1},{3,2},{4,3},{5,4},{6,5},{7,6},{8,15},{9,8},{10,9... | collective-permute-start | bytes 196616 | tf_op jit(solution)/shard_map/ppermute | solution.py:814
  23.8 2.9 %copy-start.4 = (f32[272,128]{1,0:T(8,128)S(1)}, f32[272,128]{1,0:T(8,128)}, u32[]{:S(2)}) copy-start(f32[272,128]{1,0:T(8,128)} %get-tuple-element.23.refs_1_) | copy-start | bytes 417796
  23.8 2.9 %copy-start.5 = (f32[272,128]{1,0:T(8,128)S(1)}, f32[272,128]{1,0:T(8,128)}, u32[]{:S(2)}) copy-start(f32[272,128]{1,0:T(8,128)} %get-tuple-element.24.refs_2_) | copy-start | bytes 417796
  29.5 3.6 %copy-start.6 = (s32[24,32]{1,0:T(8,128)S(1)}, s32[24,32]{1,0:T(8,128)}, u32[]{:S(2)}) copy-start(s32[24,32]{1,0:T(8,128)} %lit_ref.3) | copy-start | bytes 9220
  29.5 3.6 %copy-start.8 = (bf16[512,512]{1,0:T(8,128)(2,1)S(1)}, bf16[512,512]{1,0:T(8,128)(2,1)}, u32[]{:S(2)}) copy-start(bf16[512,512]{1,0:T(8,128)(2,1)} %w2.1) | copy-start | bytes 1572868
  29.5 41.3 %all-to-all-start = ((bf16[32,48,512]{2,1,0:T(8,128)(2,1)}), bf16[32,48,512]{2,1,0:T(8,128)(2,1)S(1)}, u32[]{:S(2)}, u32[]{:S(2)}) async-start(bf16[32,48,512]{2,1,0:T(8,128)(2,1)} %bitcast.7), calls=%async_computation | async-start | bytes 3145728 | tf_op jit(solution)/shard_map/all_to_all | solution.py:858
  33.1 27.4 %slice-start = ((s8[6291456]{0:T(1024)(128)(4,1)}), s8[4194304]{0:T(1024)(128)(4,1)S(1)}, s32[]{:S(2)}) async-start(s8[6291456]{0:T(1024)(128)(4,1)} %bitcast.9), calls=%async_computation.1 | async-start | bytes 8388608
  33.1 1.2 %copy-start.9 = (bf16[512,512]{1,0:T(8,128)(2,1)S(1)}, bf16[512,512]{1,0:T(8,128)(2,1)}, u32[]{:S(2)}) copy-start(bf16[512,512]{1,0:T(8,128)(2,1)} %w3.1) | copy-start | bytes 1572868
  34.3 1.2 %copy-start.10 = (bf16[512,512]{1,0:T(8,128)(2,1)S(1)}, bf16[512,512]{1,0:T(8,128)(2,1)}, u32[]{:S(2)}) copy-start(bf16[512,512]{1,0:T(8,128)(2,1)} %s2_.1) | copy-start | bytes 1572868
  35.5 0.9 %copy-start.11 = (bf16[128,512]{1,0:T(8,128)(2,1)S(1)}, bf16[128,512]{1,0:T(8,128)(2,1)}, u32[]{:S(2)}) copy-start(bf16[128,512]{1,0:T(8,128)(2,1)} %w1.1) | copy-start | bytes 393220
  36.4 0.9 %copy-start.12 = (bf16[512,128]{1,0:T(8,128)(2,1)S(1)}, bf16[512,128]{1,0:T(8,128)(2,1)}, u32[]{:S(2)}) copy-start(bf16[512,128]{1,0:T(8,128)(2,1)} %w4.1) | copy-start | bytes 393220
  37.3 0.9 %copy-start.13 = (bf16[128,512]{1,0:T(8,128)(2,1)S(1)}, bf16[128,512]{1,0:T(8,128)(2,1)}, u32[]{:S(2)}) copy-start(bf16[128,512]{1,0:T(8,128)(2,1)} %s1_.1) | copy-start | bytes 393220
  38.2 0.9 %copy-start.14 = (bf16[512,128]{1,0:T(8,128)(2,1)S(1)}, bf16[512,128]{1,0:T(8,128)(2,1)}, u32[]{:S(2)}) copy-start(bf16[512,128]{1,0:T(8,128)(2,1)} %s3.1) | copy-start | bytes 393220
  39.1 0.7 copy-start.15
  39.8 0.7 copy-start.16
  40.5 0.7 copy-start.17
  41.2 0.7 copy-start.18
  41.9 0.7 copy-start.19
  42.5 0.7 copy-start.20
  43.2 0.7 copy-start.21
  43.9 16.5 %slice-start.1 = ((s8[6291456]{0:T(1024)(128)(4,1)}), s8[2097152]{0:T(1024)(128)(4,1)S(1)}, s32[]{:S(2)}) async-start(s8[6291456]{0:T(1024)(128)(4,1)} %bitcast.9), calls=%async_computation.2 | async-start | bytes 4194304
  55.8 4.6 %collective-permute-start.4 = (f32[128,128]{1,0:T(8,128)S(1)}, f32[128,128]{1,0:T(8,128)S(1)}, u32[]{:S(2)}, u32[]{:S(2)}) collective-permute-start(f32[128,128]{1,0:T(8,128)S(1)} %get-tuple-element.34.yhi_ref), channel_id=1, source_target_pairs={{0,1},{1,2},{2,3},{3,4},{4,5},{5,6},{6,7},{7,0},{8,9},{9,10},{10,1... | collective-permute-start | bytes 196616 | tf_op jit(solution)/shard_map/ppermute | solution.py:898
  56.1 4.3 %collective-permute-start.5 = (f32[128,128]{1,0:T(8,128)S(1)}, f32[128,128]{1,0:T(8,128)S(1)}, u32[]{:S(2)}, u32[]{:S(2)}) collective-permute-start(f32[128,128]{1,0:T(8,128)S(1)} %get-tuple-element.33.ylo_ref), channel_id=1, source_target_pairs={{0,7},{1,0},{2,1},{3,2},{4,3},{5,4},{6,5},{7,6},{8,15},{9,8},{10,9... | collective-permute-start | bytes 196616 | tf_op jit(solution)/shard_map/ppermute | solution.py:899
